TPU v7x, 256 devices: a whole 4x4x8 slice. The times are simulated.
256 devices in a mesh: box: 128 (over z, y, x), slab: 2 (over core).
Axes of the slice: x: 4, y: 4, z: 8, core: 2. Of those that a mesh axis runs over, the one named last changes fastest.
Arguments:
- pressure_guess: float32 [16, 4096, 256], P('slab', 'box'), may hold values from -3 to 3
- right_side: float32 [16, 4096, 256], P('slab', 'box'), may hold values from -4 to 4
- coefficient: float32 [16, 4096, 256], P('slab', 'box'), may hold values from 0.2 to 5
Outputs:
- solution: float32 [16, 4096, 256], P('slab', 'box')
- residual: float32 [16, 4096, 256], P('slab', 'box')
All inputs are finite; a program needn't handle non-finite values.
Results may differ from a plain program's by a relative error of at most 0.0003.
Values sent between devices are 32-bit elements; how exact they have to be, the bound alone decides.
No kernel may reach another device: no remote copies, remote signals or barrier semaphores. Data moves between devices by JAX's collectives and lax.ppermute only.
A program may use at most 192 MiB of HBM per device.

v0:
```python
import jax
import jax.numpy as jnp
from jax import lax
from jax.sharding import PartitionSpec as P

LEVELS = 4
NU = 2
COARSE_ITERS = 8


def extended(shard, sides, width):
    for axis, dim in sides:
        size, length = (lax.axis_size(axis), shard.shape[dim])
        up = [(i, (i + 1) % size) for i in range(size - 1)]
        down = [(j, i) for i, j in up]
        last = lax.slice_in_dim(shard, length - width, length, axis=dim)
        first = lax.slice_in_dim(shard, 0, width, axis=dim)
        before = lax.ppermute(last, axis, up)
        after = lax.ppermute(first, axis, down)
        shard = jnp.concatenate([before, shard, after], axis=dim)
    return shard


def face_terms(coefficient_padded, factor):
    along_first = (
        0.5 * (coefficient_padded[1:, 1:-1, 1:-1] + coefficient_padded[:-1, 1:-1, 1:-1]) * factor
    )
    along_second = (
        0.5 * (coefficient_padded[1:-1, 1:, 1:-1] + coefficient_padded[1:-1, :-1, 1:-1]) * factor
    )
    along_third = (
        0.5 * (coefficient_padded[1:-1, 1:-1, 1:] + coefficient_padded[1:-1, 1:-1, :-1]) * factor
    )
    center = (
        along_first[1:]
        + along_first[:-1]
        + (along_second[:, 1:] + along_second[:, :-1])
        + (along_third[:, :, 1:] + along_third[:, :, :-1])
    )
    return (along_first, along_second, along_third, center)


def neighbour_sum(padded, face_set):
    along_first, along_second, along_third, center = face_set
    summed = along_first[1:] * padded[2:, 1:-1, 1:-1] + along_first[:-1] * padded[:-2, 1:-1, 1:-1]
    summed = summed + (
        along_second[:, 1:] * padded[1:-1, 2:, 1:-1]
        + along_second[:, :-1] * padded[1:-1, :-2, 1:-1]
    )
    summed = summed + (
        along_third[:, :, 1:] * padded[1:-1, 1:-1, 2:]
        + along_third[:, :, :-1] * padded[1:-1, 1:-1, :-2]
    )
    return summed


def colour_cells(extent, parity):
    summed = (
        lax.broadcasted_iota(jnp.int32, extent, 0)
        + lax.broadcasted_iota(jnp.int32, extent, 1)
        + lax.broadcasted_iota(jnp.int32, extent, 2)
    )
    return summed % 2 == parity


def zero_pad(values):
    return jnp.pad(values, 1)


def halo_cells(values):
    padded = extended(values, (("box", 1), ("slab", 0)), 1)
    return jnp.pad(padded, ((0, 0), (0, 0), (1, 1)))


def halo_coefficient(values):
    padded = extended(values, (("box", 1), ("slab", 0)), 1)
    return jnp.pad(padded, ((0, 0), (0, 0), (1, 1)))


def smooth_half(solution, source, face_set, cells, pad_cells):
    updated = (source + neighbour_sum(pad_cells(solution), face_set)) / face_set[3]
    return jnp.where(cells, updated, solution)


def first_half(source, face_set, cells):
    return jnp.where(cells, source / face_set[3], jnp.zeros_like(source))


def residual_of(solution, source, face_set, pad_cells):
    return source - (face_set[3] * solution - neighbour_sum(pad_cells(solution), face_set))


def coarse_solve(source, face_set):
    solution = jnp.zeros_like(source)
    remainder = source
    direction = source
    norm_now = jnp.sum(remainder * remainder)
    for repeat_index in range(COARSE_ITERS):
        image = face_set[3] * direction - neighbour_sum(zero_pad(direction), face_set)
        alpha = norm_now / jnp.sum(direction * image)
        solution = solution + alpha * direction
        remainder = remainder - alpha * image
        norm_next = jnp.sum(remainder * remainder)
        direction = remainder + norm_next / norm_now * direction
        norm_now = norm_next
    return solution


def coarsen(values):
    grouped = values.reshape(
        values.shape[0] // 2, 2, values.shape[1] // 2, 2, values.shape[2] // 2, 2
    )
    return jnp.sum(grouped, axis=(1, 3, 5)) * 0.125


def refine(values):
    return jnp.repeat(jnp.repeat(jnp.repeat(values, 2, axis=0), 2, axis=1), 2, axis=2)


def consolidate(source, coefficient):
    depth_first = source.shape[0]
    width_second = source.shape[1]
    boxes = lax.axis_size("box")
    slabs = lax.axis_size("slab")
    gathered = (
        lax.all_gather(source, ("box", "slab"), axis=1, tiled=True),
        lax.all_gather(coefficient, ("box", "slab"), axis=1, tiled=True),
    )

    def arrange(values):
        split_up = values.reshape(depth_first, boxes, slabs, width_second, values.shape[2])
        moved = jnp.transpose(split_up, (2, 0, 1, 3, 4))
        return moved.reshape(slabs * depth_first, boxes * width_second, values.shape[2])

    return (arrange(gathered[0]), arrange(gathered[1]))


def cycle(level_index, initial, source, coefficient, replicated, bottom):
    if replicated:
        pad_cells = zero_pad
        face_set = face_terms(zero_pad(coefficient), 0.25**level_index)
    else:
        pad_cells = halo_cells
        face_set = face_terms(halo_coefficient(coefficient), 0.25**level_index)
    if level_index == LEVELS - 1:
        return (coarse_solve(source, face_set), face_set)
    red_cells = colour_cells(source.shape, 0)
    black_cells = colour_cells(source.shape, 1)
    if level_index == 0:
        solution = smooth_half(initial, source, face_set, red_cells, pad_cells)
    else:
        solution = first_half(source, face_set, red_cells)
    solution = smooth_half(solution, source, face_set, black_cells, pad_cells)
    solution = smooth_half(solution, source, face_set, red_cells, pad_cells)
    solution = smooth_half(solution, source, face_set, black_cells, pad_cells)
    residual = residual_of(solution, source, face_set, pad_cells)
    coarse_source = coarsen(residual)
    coarse_coefficient = coarsen(coefficient)
    if replicated or level_index + 1 < bottom:
        correction, unused = cycle(
            level_index + 1, None, coarse_source, coarse_coefficient, replicated, bottom
        )
    else:
        whole_source, whole_coefficient = consolidate(coarse_source, coarse_coefficient)
        whole_correction, unused = cycle(
            level_index + 1, None, whole_source, whole_coefficient, True, bottom
        )
        offset_first = lax.axis_index("slab") * coarse_source.shape[0]
        offset_second = lax.axis_index("box") * coarse_source.shape[1]
        correction = lax.dynamic_slice(
            whole_correction, (offset_first, offset_second, 0), coarse_source.shape
        )
    solution = solution + refine(correction)
    for repeat_index in range(NU):
        solution = smooth_half(solution, source, face_set, red_cells, pad_cells)
        solution = smooth_half(solution, source, face_set, black_cells, pad_cells)
    return (solution, face_set)


def body(pressure_guess, right_side, coefficient):
    bottom = LEVELS - 1
    solution, face_set = cycle(0, pressure_guess, right_side, coefficient, False, bottom)
    return (solution, residual_of(solution, right_side, face_set, halo_cells))


def solution(mesh):
    placed = (P("slab", "box", None), P("slab", "box", None), P("slab", "box", None))
    return jax.shard_map(
        body,
        mesh=mesh,
        in_specs=placed,
        out_specs=(P("slab", "box", None), P("slab", "box", None)),
        check_vma=False,
    )
```

profile of v0, /device:TPU:127, one launch (start us, length us, event | category | flops | bytes accessed | tf_op | source)
XLA Modules:
  0.0 764.1 jit_solution(7026840649521089913)
XLA Ops:
  8.7 8.8 %collective-permute-start.4 = (f32[8,1,256]{2,0,1:T(8,128)S(1)}, f32[8,1,256]{2,0,1:T(8,128)S(1)}, u32[]{:S(2)}, u32[]{:S(2)}) collective-permute-start(f32[8,1,256]{2,0,1:T(8,128)S(1)} %copy.684), channel_id=1, source_target_pairs={{0,2},{2,4},{4,6},{6,8},{8,10},{10,12},{12,14},{14,16},{16,18},{18... | collective-permute-start | bytes 24584 | tf_op jit(solution)/shard_map/ppermute | solution.py:18
  39.9 6.4 collective-permute-start.8
  48.4 18.9 %reshape.81 = f32[4,2,16,2,128,2]{5,4,3,2,1,0:T(8,128)} reshape(f32[8,32,256]{2,1,0:T(8,128)} %param.5) | data formatting | bytes 524288 | tf_op jit(solution)/shard_map/reshape | solution.py:110
  67.2 7.0 reduce_sum.213
  81.5 9.1 %collective-permute-start.12 = (f32[8,1,256]{2,0,1:T(8,128)S(1)}, f32[8,1,256]{2,0,1:T(8,128)S(1)}, u32[]{:S(2)}, u32[]{:S(2)}) collective-permute-start(f32[8,1,256]{2,0,1:T(8,128)S(1)} %copy.617), channel_id=1, source_target_pairs={{0,2},{2,4},{4,6},{6,8},{8,10},{10,12},{12,14},{14,16},{16,18},{18... | collective-permute-start | bytes 24584 | tf_op jit(solution)/shard_map/ppermute | solution.py:18
  92.6 8.8 %collective-permute-start.24 = (f32[4,1,128]{2,1,0:T(1,128)S(1)}, f32[4,1,128]{2,1,0:T(1,128)S(1)}, u32[]{:S(2)}, u32[]{:S(2)}) collective-permute-start(f32[4,1,128]{2,1,0:T(1,128)S(1)} %get-tuple-element.115), channel_id=1, source_target_pairs={{0,2},{2,4},{4,6},{6,8},{8,10},{10,12},{12,14},{14,16},{16,18},{18... | collective-permute-start | bytes 6152 | tf_op jit(solution)/shard_map/ppermute | solution.py:18
  119.8 7.6 collective-permute-start.16
  129.4 7.8 %collective-permute-done.17 = f32[8,1,256]{2,0,1:T(8,128)S(1)} collective-permute-done((f32[8,1,256]{2,0,1:T(8,128)S(1)}, f32[8,1,256]{2,0,1:T(8,128)S(1)}, u32[]{:S(2)}, u32[]{:S(2)}) %collective-permute-start.17) | collective-permute-done | bytes 8224 | tf_op jit(solution)/shard_map/ppermute | solution.py:19
  151.1 6.3 collective-permute-done.21
  164.5 18.1 %reshape.80 = f32[4,2,16,2,128,2]{5,4,3,2,1,0:T(8,128)} reshape(f32[8,32,256]{2,1,0:T(8,128)S(1)} %fusion.69) | data formatting | bytes 524288 | tf_op jit(solution)/shard_map/reshape | solution.py:110
  182.6 7.0 reduce_sum.212
  195.0 6.4 collective-permute-done.29
  211.7 7.3 collective-permute-start.32
  221.0 7.8 %collective-permute-done.33 = f32[4,1,128]{2,1,0:T(1,128)S(1)} collective-permute-done((f32[4,1,128]{2,1,0:T(1,128)S(1)}, f32[4,1,128]{2,1,0:T(1,128)S(1)}, u32[]{:S(2)}, u32[]{:S(2)}) %collective-permute-start.33) | collective-permute-done | bytes 2080 | tf_op jit(solution)/shard_map/ppermute | solution.py:19
  287.5 6.4 collective-permute-done.49
  325.3 66.4 %all-gather.3 = f32[256,4,32]{2,1,0:T(4,128)S(1)} all-gather(f32[1,4,32]{2,1,0:T(4,128)S(1)} %multiply_bitcast_fusion), channel_id=3, replica_groups=mesh['box'=128,'slab'=2] {'box','slab'}, dimensions={0}, use_global_device_ids=true | all-gather | bytes 131584 | tf_op jit(solution)/shard_map/all_gather | solution.py:127
  398.1 6.9 collective-permute-start.60
  407.0 7.7 %collective-permute-done.61 = f32[2,1,64]{2,1,0:T(1,128)S(1)} collective-permute-done((f32[2,1,64]{2,1,0:T(1,128)S(1)}, f32[2,1,64]{2,1,0:T(1,128)S(1)}, u32[]{:S(2)}, u32[]{:S(2)}) %collective-permute-start.61) | collective-permute-done | bytes 544 | tf_op jit(solution)/shard_map/ppermute | solution.py:19
  422.5 65.9 %all-gather.2 = f32[256,4,32]{2,1,0:T(4,128)S(1)} all-gather(f32[1,4,32]{2,1,0:T(4,128)S(1)} %multiply_bitcast_fusion.1), channel_id=2, replica_groups=mesh['box'=128,'slab'=2] {'box','slab'}, dimensions={0}, use_global_device_ids=true | all-gather | bytes 131584 | tf_op jit(solution)/shard_map/all_gather | solution.py:126
  525.7 7.8 %collective-permute-done.65 = f32[2,1,64]{2,1,0:T(1,128)S(1)} collective-permute-done((f32[2,1,64]{2,1,0:T(1,128)S(1)}, f32[2,1,64]{2,1,0:T(1,128)S(1)}, u32[]{:S(2)}, u32[]{:S(2)}) %collective-permute-start.65) | collective-permute-done | bytes 544 | tf_op jit(solution)/shard_map/ppermute | solution.py:19
  545.6 6.4 collective-permute-done.69
  563.7 6.4 collective-permute-done.73
  581.9 6.4 collective-permute-done.77
  600.4 6.4 collective-permute-done.81
  618.7 6.4 collective-permute-done.85
  636.9 6.4 collective-permute-done.89
  655.2 6.4 collective-permute-done.93
  674.3 6.4 collective-permute-done.97
  693.2 6.4 collective-permute-done.101
  712.1 6.4 collective-permute-done.105
  731.0 6.4 collective-permute-done.109
  749.9 6.4 collective-permute-done.113
  (469 shorter events, 377.3 us)
Async XLA Ops:
  1.5 17.9 %collective-permute-start = (f32[8,1,256]{2,0,1:T(8,128)S(1)}, f32[8,1,256]{2,0,1:T(8,128)S(1)}, u32[]{:S(2)}, u32[]{:S(2)}) collective-permute-start(f32[8,1,256]{2,0,1:T(8,128)S(1)} %copy.682), channel_id=1, source_target_pairs={{0,2},{2,4},{4,6},{6,8},{8,10},{10,12},{12,14},{14,16},{16,18},{18... | collective-permute-start | bytes 24584 | tf_op jit(solution)/shard_map/ppermute | solution.py:18
  5.9 13.6 %collective-permute-start.1 = (f32[8,1,256]{2,0,1:T(8,128)S(1)}, f32[8,1,256]{2,0,1:T(8,128)S(1)}, u32[]{:S(2)}, u32[]{:S(2)}) collective-permute-start(f32[8,1,256]{2,0,1:T(8,128)S(1)} %copy.683), channel_id=1, source_target_pairs={{2,0},{4,2},{6,4},{8,6},{10,8},{12,10},{14,12},{16,14},{18,16},{20... | collective-permute-start | bytes 24584 | tf_op jit(solution)/shard_map/ppermute | solution.py:19
  8.7 17.4 %collective-permute-start.4 = (f32[8,1,256]{2,0,1:T(8,128)S(1)}, f32[8,1,256]{2,0,1:T(8,128)S(1)}, u32[]{:S(2)}, u32[]{:S(2)}) collective-permute-start(f32[8,1,256]{2,0,1:T(8,128)S(1)} %copy.684), channel_id=1, source_target_pairs={{0,2},{2,4},{4,6},{6,8},{8,10},{10,12},{12,14},{14,16},{16,18},{18... | collective-permute-start | bytes 24584 | tf_op jit(solution)/shard_map/ppermute | solution.py:18
  17.5 9.8 %collective-permute-start.5 = (f32[8,1,256]{2,0,1:T(8,128)S(1)}, f32[8,1,256]{2,0,1:T(8,128)S(1)}, u32[]{:S(2)}, u32[]{:S(2)}) collective-permute-start(f32[8,1,256]{2,0,1:T(8,128)S(1)} %copy.685), channel_id=1, source_target_pairs={{2,0},{4,2},{6,4},{8,6},{10,8},{12,10},{14,12},{16,14},{18,16},{20... | collective-permute-start | bytes 24584 | tf_op jit(solution)/shard_map/ppermute | solution.py:19
  21.4 12.6 %collective-permute-start.2 = (f32[1,34,256]{2,1,0:T(8,128)S(1)}, f32[1,34,256]{2,1,0:T(8,128)S(1)}, u32[]{:S(2)}, u32[]{:S(2)}) collective-permute-start(f32[1,34,256]{2,1,0:T(8,128)S(1)} %get-tuple-element.53), channel_id=1, source_target_pairs={{1,0},{3,2},{5,4},{7,6},{9,8},{11,10},{13,12},{15,14},{17,16},{19,... | collective-permute-start | bytes 104456 | tf_op jit(solution)/shard_map/ppermute | solution.py:19
  39.9 34.3 %collective-permute-start.8 = (f32[8,1,256]{2,0,1:T(8,128)S(1)}, f32[8,1,256]{2,0,1:T(8,128)S(1)}, u32[]{:S(2)}, u32[]{:S(2)}) collective-permute-start(f32[8,1,256]{2,0,1:T(8,128)S(1)} %copy.611), channel_id=1, source_target_pairs={{0,2},{2,4},{4,6},{6,8},{8,10},{10,12},{12,14},{14,16},{16,18},{18... | collective-permute-start | bytes 24584 | tf_op jit(solution)/shard_map/ppermute | solution.py:18
  46.3 28.0 %collective-permute-start.9 = (f32[8,1,256]{2,0,1:T(8,128)S(1)}, f32[8,1,256]{2,0,1:T(8,128)S(1)}, u32[]{:S(2)}, u32[]{:S(2)}) collective-permute-start(f32[8,1,256]{2,0,1:T(8,128)S(1)} %copy.612), channel_id=1, source_target_pairs={{2,0},{4,2},{6,4},{8,6},{10,8},{12,10},{14,12},{16,14},{18,16},{20... | collective-permute-start | bytes 24584 | tf_op jit(solution)/shard_map/ppermute | solution.py:19
  81.5 24.1 %collective-permute-start.12 = (f32[8,1,256]{2,0,1:T(8,128)S(1)}, f32[8,1,256]{2,0,1:T(8,128)S(1)}, u32[]{:S(2)}, u32[]{:S(2)}) collective-permute-start(f32[8,1,256]{2,0,1:T(8,128)S(1)} %copy.617), channel_id=1, source_target_pairs={{0,2},{2,4},{4,6},{6,8},{8,10},{10,12},{12,14},{14,16},{16,18},{18... | collective-permute-start | bytes 24584 | tf_op jit(solution)/shard_map/ppermute | solution.py:18
  90.6 15.0 %collective-permute-start.13 = (f32[8,1,256]{2,0,1:T(8,128)S(1)}, f32[8,1,256]{2,0,1:T(8,128)S(1)}, u32[]{:S(2)}, u32[]{:S(2)}) collective-permute-start(f32[8,1,256]{2,0,1:T(8,128)S(1)} %copy.618), channel_id=1, source_target_pairs={{2,0},{4,2},{6,4},{8,6},{10,8},{12,10},{14,12},{16,14},{18,16},{20... | collective-permute-start | bytes 24584 | tf_op jit(solution)/shard_map/ppermute | solution.py:19
  92.6 18.1 %collective-permute-start.24 = (f32[4,1,128]{2,1,0:T(1,128)S(1)}, f32[4,1,128]{2,1,0:T(1,128)S(1)}, u32[]{:S(2)}, u32[]{:S(2)}) collective-permute-start(f32[4,1,128]{2,1,0:T(1,128)S(1)} %get-tuple-element.115), channel_id=1, source_target_pairs={{0,2},{2,4},{4,6},{6,8},{8,10},{10,12},{12,14},{14,16},{16,18},{18... | collective-permute-start | bytes 6152 | tf_op jit(solution)/shard_map/ppermute | solution.py:18
  106.5 10.0 %collective-permute-start.14 = (f32[1,34,256]{2,1,0:T(8,128)S(1)}, f32[1,34,256]{2,1,0:T(8,128)S(1)}, u32[]{:S(2)}, u32[]{:S(2)}) collective-permute-start(f32[1,34,256]{2,1,0:T(8,128)S(1)} %get-tuple-element.49), channel_id=1, source_target_pairs={{1,0},{3,2},{5,4},{7,6},{9,8},{11,10},{13,12},{15,14},{17,16},{19,... | collective-permute-start | bytes 104456 | tf_op jit(solution)/shard_map/ppermute | solution.py:19
  111.2 31.9 %collective-permute-start.26 = (f32[1,18,128]{2,1,0:T(8,128)S(1)}, f32[1,18,128]{2,1,0:T(8,128)S(1)}, u32[]{:S(2)}, u32[]{:S(2)}) collective-permute-start(f32[1,18,128]{2,1,0:T(8,128)S(1)} %get-tuple-element.98), channel_id=1, source_target_pairs={{1,0},{3,2},{5,4},{7,6},{9,8},{11,10},{13,12},{15,14},{17,16},{19,... | collective-permute-start | bytes 27656 | tf_op jit(solution)/shard_map/ppermute | solution.py:19
  115.2 27.8 %collective-permute-start.27 = (f32[1,18,128]{2,1,0:T(8,128)S(1)}, f32[1,18,128]{2,1,0:T(8,128)S(1)}, u32[]{:S(2)}, u32[]{:S(2)}) collective-permute-start(f32[1,18,128]{2,1,0:T(8,128)S(1)} %get-tuple-element.97), channel_id=1, source_target_pairs={{0,1},{2,3},{4,5},{6,7},{8,9},{10,11},{12,13},{14,15},{16,17},{18,... | collective-permute-start | bytes 27656 | tf_op jit(solution)/shard_map/ppermute | solution.py:18
  127.4 9.8 %collective-permute-start.17 = (f32[8,1,256]{2,0,1:T(8,128)S(1)}, f32[8,1,256]{2,0,1:T(8,128)S(1)}, u32[]{:S(2)}, u32[]{:S(2)}) collective-permute-start(f32[8,1,256]{2,0,1:T(8,128)S(1)} %copy.624), channel_id=1, source_target_pairs={{2,0},{4,2},{6,4},{8,6},{10,8},{12,10},{14,12},{16,14},{18,16},{20... | collective-permute-start | bytes 24584 | tf_op jit(solution)/shard_map/ppermute | solution.py:19
  147.6 9.8 %collective-permute-start.21 = (f32[8,1,256]{2,0,1:T(8,128)S(1)}, f32[8,1,256]{2,0,1:T(8,128)S(1)}, u32[]{:S(2)}, u32[]{:S(2)}) collective-permute-start(f32[8,1,256]{2,0,1:T(8,128)S(1)} %copy.630), channel_id=1, source_target_pairs={{2,0},{4,2},{6,4},{8,6},{10,8},{12,10},{14,12},{16,14},{18,16},{20... | collective-permute-start | bytes 24584 | tf_op jit(solution)/shard_map/ppermute | solution.py:19
  191.6 9.8 %collective-permute-start.29 = (f32[4,1,128]{2,1,0:T(1,128)S(1)}, f32[4,1,128]{2,1,0:T(1,128)S(1)}, u32[]{:S(2)}, u32[]{:S(2)}) collective-permute-start(f32[4,1,128]{2,1,0:T(1,128)S(1)} %get-tuple-element.114), channel_id=1, source_target_pairs={{2,0},{4,2},{6,4},{8,6},{10,8},{12,10},{14,12},{16,14},{18,16},{20... | collective-permute-start | bytes 6152 | tf_op jit(solution)/shard_map/ppermute | solution.py:19
  201.4 10.0 %collective-permute-start.30 = (f32[1,18,128]{2,1,0:T(8,128)S(1)}, f32[1,18,128]{2,1,0:T(8,128)S(1)}, u32[]{:S(2)}, u32[]{:S(2)}) collective-permute-start(f32[1,18,128]{2,1,0:T(8,128)S(1)} %get-tuple-element.96), channel_id=1, source_target_pairs={{1,0},{3,2},{5,4},{7,6},{9,8},{11,10},{13,12},{15,14},{17,16},{19,... | collective-permute-start | bytes 27656 | tf_op jit(solution)/shard_map/ppermute | solution.py:19
  206.1 14.9 %collective-permute-start.44 = (f32[2,1,64]{2,1,0:T(1,128)S(1)}, f32[2,1,64]{2,1,0:T(1,128)S(1)}, u32[]{:S(2)}, u32[]{:S(2)}) collective-permute-start(f32[2,1,64]{2,1,0:T(1,128)S(1)} %get-tuple-element.153), channel_id=1, source_target_pairs={{0,2},{2,4},{4,6},{6,8},{8,10},{10,12},{12,14},{14,16},{16,18},{18... | collective-permute-start | bytes 1544 | tf_op jit(solution)/shard_map/ppermute | solution.py:18
  208.1 12.9 %collective-permute-start.45 = (f32[2,1,64]{2,1,0:T(1,128)S(1)}, f32[2,1,64]{2,1,0:T(1,128)S(1)}, u32[]{:S(2)}, u32[]{:S(2)}) collective-permute-start(f32[2,1,64]{2,1,0:T(1,128)S(1)} %get-tuple-element.154), channel_id=1, source_target_pairs={{2,0},{4,2},{6,4},{8,6},{10,8},{12,10},{14,12},{16,14},{18,16},{20... | collective-permute-start | bytes 1544 | tf_op jit(solution)/shard_map/ppermute | solution.py:19
  219.1 9.8 %collective-permute-start.33 = (f32[4,1,128]{2,1,0:T(1,128)S(1)}, f32[4,1,128]{2,1,0:T(1,128)S(1)}, u32[]{:S(2)}, u32[]{:S(2)}) collective-permute-start(f32[4,1,128]{2,1,0:T(1,128)S(1)} %get-tuple-element.112), channel_id=1, source_target_pairs={{2,0},{4,2},{6,4},{8,6},{10,8},{12,10},{14,12},{16,14},{18,16},{20... | collective-permute-start | bytes 6152 | tf_op jit(solution)/shard_map/ppermute | solution.py:19
  228.8 10.4 %collective-permute-start.34 = (f32[1,18,128]{2,1,0:T(8,128)S(1)}, f32[1,18,128]{2,1,0:T(8,128)S(1)}, u32[]{:S(2)}, u32[]{:S(2)}) collective-permute-start(f32[1,18,128]{2,1,0:T(8,128)S(1)} %get-tuple-element.94), channel_id=1, source_target_pairs={{1,0},{3,2},{5,4},{7,6},{9,8},{11,10},{13,12},{15,14},{17,16},{19,... | collective-permute-start | bytes 27656 | tf_op jit(solution)/shard_map/ppermute | solution.py:19
  234.9 21.8 %collective-permute-start.46 = (f32[1,10,64]{2,1,0:T(8,128)S(1)}, f32[1,10,64]{2,1,0:T(8,128)S(1)}, u32[]{:S(2)}, u32[]{:S(2)}) collective-permute-start(f32[1,10,64]{2,1,0:T(8,128)S(1)} %get-tuple-element.134), channel_id=1, source_target_pairs={{1,0},{3,2},{5,4},{7,6},{9,8},{11,10},{13,12},{15,14},{17,16},{19,... | collective-permute-start | bytes 7688 | tf_op jit(solution)/shard_map/ppermute | solution.py:19
  237.9 18.8 %collective-permute-start.47 = (f32[1,10,64]{2,1,0:T(8,128)S(1)}, f32[1,10,64]{2,1,0:T(8,128)S(1)}, u32[]{:S(2)}, u32[]{:S(2)}) collective-permute-start(f32[1,10,64]{2,1,0:T(8,128)S(1)} %get-tuple-element.133), channel_id=1, source_target_pairs={{0,1},{2,3},{4,5},{6,7},{8,9},{10,11},{12,13},{14,15},{16,17},{18,... | collective-permute-start | bytes 7688 | tf_op jit(solution)/shard_map/ppermute | solution.py:18
  260.6 9.8 %collective-permute-start.41 = (f32[4,1,128]{2,1,0:T(1,128)S(1)}, f32[4,1,128]{2,1,0:T(1,128)S(1)}, u32[]{:S(2)}, u32[]{:S(2)}) collective-permute-start(f32[4,1,128]{2,1,0:T(1,128)S(1)} %get-tuple-element.108), channel_id=1, source_target_pairs={{2,0},{4,2},{6,4},{8,6},{10,8},{12,10},{14,12},{16,14},{18,16},{20... | collective-permute-start | bytes 6152 | tf_op jit(solution)/shard_map/ppermute | solution.py:19
  320.0 71.9 %collective-permute-start.56 = (f32[2,1,64]{2,1,0:T(1,128)S(1)}, f32[2,1,64]{2,1,0:T(1,128)S(1)}, u32[]{:S(2)}, u32[]{:S(2)}) collective-permute-start(f32[2,1,64]{2,1,0:T(1,128)S(1)} %get-tuple-element.147), channel_id=1, source_target_pairs={{0,2},{2,4},{4,6},{6,8},{8,10},{10,12},{12,14},{14,16},{16,18},{18... | collective-permute-start | bytes 1544 | tf_op jit(solution)/shard_map/ppermute | solution.py:18
  322.0 70.0 %collective-permute-start.57 = (f32[2,1,64]{2,1,0:T(1,128)S(1)}, f32[2,1,64]{2,1,0:T(1,128)S(1)}, u32[]{:S(2)}, u32[]{:S(2)}) collective-permute-start(f32[2,1,64]{2,1,0:T(1,128)S(1)} %get-tuple-element.148), channel_id=1, source_target_pairs={{2,0},{4,2},{6,4},{8,6},{10,8},{12,10},{14,12},{16,14},{18,16},{20... | collective-permute-start | bytes 1544 | tf_op jit(solution)/shard_map/ppermute | solution.py:19
  615.3 9.8 %collective-permute-start.85 = (f32[4,1,128]{2,1,0:T(1,128)S(1)}, f32[4,1,128]{2,1,0:T(1,128)S(1)}, u32[]{:S(2)}, u32[]{:S(2)}) collective-permute-start(f32[4,1,128]{2,1,0:T(1,128)S(1)} %get-tuple-element.104), channel_id=1, source_target_pairs={{2,0},{4,2},{6,4},{8,6},{10,8},{12,10},{14,12},{16,14},{18,16},{20... | collective-permute-start | bytes 6152 | tf_op jit(solution)/shard_map/ppermute | solution.py:19
  670.9 9.8 %collective-permute-start.97 = (f32[8,1,256]{2,0,1:T(8,128)S(1)}, f32[8,1,256]{2,0,1:T(8,128)S(1)}, u32[]{:S(2)}, u32[]{:S(2)}) collective-permute-start(f32[8,1,256]{2,0,1:T(8,128)S(1)} %copy.653), channel_id=1, source_target_pairs={{2,0},{4,2},{6,4},{8,6},{10,8},{12,10},{14,12},{16,14},{18,16},{20... | collective-permute-start | bytes 24584 | tf_op jit(solution)/shard_map/ppermute | solution.py:19
  689.8 9.8 %collective-permute-start.101 = (f32[8,1,256]{2,0,1:T(8,128)S(1)}, f32[8,1,256]{2,0,1:T(8,128)S(1)}, u32[]{:S(2)}, u32[]{:S(2)}) collective-permute-start(f32[8,1,256]{2,0,1:T(8,128)S(1)} %copy.659), channel_id=1, source_target_pairs={{2,0},{4,2},{6,4},{8,6},{10,8},{12,10},{14,12},{16,14},{18,16},{20... | collective-permute-start | bytes 24584 | tf_op jit(solution)/shard_map/ppermute | solution.py:19
  708.7 9.8 %collective-permute-start.105 = (f32[8,1,256]{2,0,1:T(8,128)S(1)}, f32[8,1,256]{2,0,1:T(8,128)S(1)}, u32[]{:S(2)}, u32[]{:S(2)}) collective-permute-start(f32[8,1,256]{2,0,1:T(8,128)S(1)} %copy.665), channel_id=1, source_target_pairs={{2,0},{4,2},{6,4},{8,6},{10,8},{12,10},{14,12},{16,14},{18,16},{20... | collective-permute-start | bytes 24584 | tf_op jit(solution)/shard_map/ppermute | solution.py:19
  727.6 9.8 %collective-permute-start.109 = (f32[8,1,256]{2,0,1:T(8,128)S(1)}, f32[8,1,256]{2,0,1:T(8,128)S(1)}, u32[]{:S(2)}, u32[]{:S(2)}) collective-permute-start(f32[8,1,256]{2,0,1:T(8,128)S(1)} %copy.671), channel_id=1, source_target_pairs={{2,0},{4,2},{6,4},{8,6},{10,8},{12,10},{14,12},{16,14},{18,16},{20... | collective-permute-start | bytes 24584 | tf_op jit(solution)/shard_map/ppermute | solution.py:19
  746.5 9.8 %collective-permute-start.113 = (f32[8,1,256]{2,0,1:T(8,128)S(1)}, f32[8,1,256]{2,0,1:T(8,128)S(1)}, u32[]{:S(2)}, u32[]{:S(2)}) collective-permute-start(f32[8,1,256]{2,0,1:T(8,128)S(1)} %copy.677), channel_id=1, source_target_pairs={{2,0},{4,2},{6,4},{8,6},{10,8},{12,10},{14,12},{16,14},{18,16},{20... | collective-permute-start | bytes 24584 | tf_op jit(solution)/shard_map/ppermute | solution.py:19
  (96 other events, 2276.9 us)
where the time goes:
time: 768 us; the launch traced here: 764 us
  starting transfers between devices  323 us (42%)
  waiting for transfers between devices  185 us (24%)
  blocking collectives  132 us (17%)
  other arithmetic  56.6 us (7%)
  local copies, waits for them, and re-layouts  46.3 us (6%)
  between operations  21.8 us (3%)
    ppermute x58, starting transfers between devices, extended(): after = lax.ppermute(first, axis, down)  183 us
    ppermute x58, waiting for transfers between devices, extended(): after = lax.ppermute(first, axis, down)  147 us
    ppermute x58, starting transfers between devices, extended(): before = lax.ppermute(last, axis, up)  139 us
    all_gather x1, blocking collectives, consolidate(): lax.all_gather(coefficient, ('box', 'slab'), axis=1, tiled=True)  66.4 us
    all_gather x1, blocking collectives, consolidate(): lax.all_gather(source, ('box', 'slab'), axis=1, tiled=True)  65.9 us
    reshape x3, local copies, waits for them, and re-layouts, coarsen(): values.reshape(values.shape[0] // 2, 2, values.shape[1] // 2, 2, values.s...  39.8 us
    ppermute x58, waiting for transfers between devices, extended(): before = lax.ppermute(last, axis, up)  37.7 us
    reduce_sum x8, other arithmetic, coarsen(): return jnp.sum(grouped, axis=(1, 3, 5)) * 0.125  16.1 us
  transfers between devices with their start and end apart: 116, of which 46 were waited for; matrix products, arithmetic and copies ran while one was open for 5% of the time, Pallas kernels for 0%

commit v1 on v0

v1 whole, which is shorter than its diff:
```python
import functools

import jax
import jax.numpy as jnp
from jax import lax
from jax.experimental import pallas as pl
from jax.experimental.pallas import tpu as pltpu
from jax.sharding import PartitionSpec as P

ITERS = 8
F32 = jnp.float32
BF16 = jnp.bfloat16

H0 = 9
H1 = 12
N0 = 32 + 2 * H0
N1 = 16 + 2 * (H1 + 1)
N2 = 24
ROWS = 20
EDGE = 184
SEND1 = H1 + (H1 + 1) + 8


def matmul(x, m):
    high = x.astype(BF16)
    rest = x - high.astype(F32)
    mid = rest.astype(BF16)
    low = (rest - mid.astype(F32)).astype(BF16)
    dot = functools.partial(jnp.dot, preferred_element_type=F32)
    return dot(high, m) + (dot(mid, m) + dot(low, m))


def one_hot(shape, rule):
    i = lax.broadcasted_iota(jnp.int32, shape, 0)
    j = lax.broadcasted_iota(jnp.int32, shape, 1)
    return rule(i, j).astype(F32).astype(BF16)


def iota(shape, axis):
    return lax.broadcasted_iota(jnp.int32, shape, axis)


def up(v, axis):
    return pltpu.roll(v, v.shape[axis] - 1, axis)


def down(v, axis):
    return pltpu.roll(v, 1, axis)


def slab_rows(x, half, odd):
    return pl.ds((x // 8) * 16 + half * 8 + x % 8 + 64 * odd, 4, stride=128)


def pack_kernel(g, r, c, low, high):
    even_y = (iota((4, 128), 1) & 1) == 0
    odd_y = jnp.logical_not(even_y)
    for x in range(32):
        out, base = (low, x * ROWS) if x < 16 else (high, (x - 16) * ROWS)
        p0 = even_y if x % 2 == 0 else odd_y
        for half in range(2):
            lanes = slice(128 * half, 128 * half + 128)
            even, odd = slab_rows(x, half, 0), slab_rows(x, half, 1)
            out[base : base + 4, lanes] = c[even, :]
            out[base + 4 : base + 8, lanes] = c[odd, :]
            fe, fo = r[even, :], r[odd, :]
            out[base + 8 : base + 12, lanes] = jnp.where(p0, fe, fo)
            out[base + 12 : base + 16, lanes] = jnp.where(p0, fo, fe)
            out[base + 16 : base + 20, lanes] = jnp.where(p0, g[odd, :], g[even, :])


def parity(i, shape, shift):
    return ((iota(shape, 1) + i + shift) & 1) == 0


def nsum_packed(lv, v, xa, xb, ya, yb, i, p):
    here = v[i]
    t = xa[i] * v[i + 1] + xb[i - 1] * v[i - 1]
    t = t + (ya[i] * up(here, 1) + down(yb[i] * here, 1))
    cross = lv["c"][i]
    z = jnp.where(p, down(cross * here, 0), cross * up(here, 0))
    return t + (lv["s"][i] * here + z)


def sweep_packed(lv, red, first, last):
    def body(i, carry):
        p = parity(i, (8, 256), 1)
        if red:
            n = nsum_packed(lv, lv["vB"], lv["xR"], lv["xB"], lv["yR"], lv["yB"], i, p)
            lv["vR"][i] = (lv["fR"][i] + n) * lv["iR"][i]
        else:
            p = jnp.logical_not(p)
            n = nsum_packed(lv, lv["vR"], lv["xB"], lv["xR"], lv["yB"], lv["yR"], i, p)
            lv["vB"][i] = (lv["fB"][i] + n) * lv["iB"][i]
        return carry

    lax.fori_loop(first, last, body, 0, unroll=6)


def residual_packed(lv, i):
    p = parity(i, (8, 256), 1)
    n = nsum_packed(lv, lv["vB"], lv["xR"], lv["xB"], lv["yR"], lv["yB"], i, p)
    r_red = lv["fR"][i] - (lv["cR"][i] * lv["vR"][i] - n)
    q = jnp.logical_not(p)
    n = nsum_packed(lv, lv["vR"], lv["xB"], lv["xR"], lv["yB"], lv["yR"], i, q)
    r_black = lv["fB"][i] - (lv["cB"][i] * lv["vB"][i] - n)
    return r_red, r_black, p


PACKED = ("vB", "fR", "fB", "xR", "xB", "yR", "yB", "s", "c", "iR", "iB", "cR", "cB")


def fine_kernel(place, lo, hi, halo, *refs):
    outs = dict(zip(PACKED, refs))
    own, send, bottom = refs[len(PACKED) : len(PACKED) + 3]
    vR, bE, bO, pair_r, pair_b, tmp = refs[len(PACKED) + 3 :]
    lv = dict(outs, vR=vR)
    slab, box, boxes = place[0], place[1], place[2]

    def source(t, i):
        if i < H0:
            return halo.at[t, 0], i * ROWS + (EDGE - H0 * ROWS)
        if i >= H0 + 32:
            return halo.at[t, 1], (i - H0 - 32) * ROWS
        x = i - H0
        return (lo.at[t], x * ROWS) if x < 16 else (hi.at[t], (x - 16) * ROWS)

    for i in range(N0):
        for t in range(2):
            ref, base = source(t, i)
            for k, out in enumerate((bE, bO, lv["fR"], lv["fB"], lv["vB"])):
                out[i, 4 * t : 4 * t + 4, :] = ref[base + 4 * k : base + 4 * k + 4, :]

    row, lane = iota((8, 256), 0), iota((8, 256), 1)
    top, bot = row == 7, row == 0
    end, begin = lane == 255, lane == 0

    def faces(i, carry):
        p = parity(i, (8, 256), 1)
        e, o = bE[i], bO[i]
        fxe, fxo = 0.5 * (e + bE[i + 1]), 0.5 * (o + bO[i + 1])
        lv["xR"][i] = jnp.where(p, fxe, fxo)
        lv["xB"][i] = jnp.where(p, fxo, fxe)
        fye = 0.5 * (e + jnp.where(end, 0.0, up(e, 1)))
        fyo = 0.5 * (o + jnp.where(end, 0.0, up(o, 1)))
        gye = 0.5 * (e + jnp.where(begin, 0.0, down(e, 1)))
        gyo = 0.5 * (o + jnp.where(begin, 0.0, down(o, 1)))
        yr, yb = jnp.where(p, fye, fyo), jnp.where(p, fyo, fye)
        lv["yR"][i] = jnp.where(end, 0.0, yr)
        lv["yB"][i] = jnp.where(end, 0.0, yb)
        s = 0.5 * (e + o)
        above = 0.5 * (o + jnp.where(top, 0.0, up(e, 0)))
        below = 0.5 * (e + jnp.where(bot, 0.0, down(o, 0)))
        lv["s"][i] = s
        lv["c"][i] = jnp.where(top, 0.0, above)
        ze, zo = fye + gye + (s + below), fyo + gyo + (s + above)
        lv["cR"][i] = jnp.where(p, ze, zo)
        lv["cB"][i] = jnp.where(p, zo, ze)
        return carry

    lax.fori_loop(0, N0 - 1, faces, 0, unroll=7)

    def inverses(i, carry):
        x = box * 32 - H0 + i
        inside = jnp.logical_and(x >= 0, x < boxes * 32)
        cr = lv["cR"][i] + (lv["xR"][i] + lv["xB"][i - 1])
        cb = lv["cB"][i] + (lv["xB"][i] + lv["xR"][i - 1])
        lv["cR"][i] = cr
        lv["cB"][i] = cb
        lv["iR"][i] = jnp.where(inside, 1.0 / cr, 0.0)
        lv["iB"][i] = jnp.where(inside, 1.0 / cb, 0.0)
        return carry

    lax.fori_loop(1, N0 - 1, inverses, 0, unroll=6)

    for k in range(2):
        sweep_packed(lv, True, 1 + 2 * k, N0 - 1 - 2 * k)
        sweep_packed(lv, False, 2 + 2 * k, N0 - 2 - 2 * k)

    def restrict(j, carry):
        a, b, _ = residual_packed(lv, H0 + 2 * j)
        c, d, _ = residual_packed(lv, H0 + 1 + 2 * j)
        i = H0 + 2 * j
        pair_r[j] = (a + b) + (c + d)
        pair_b[j] = (bE[i] + bO[i]) + (bE[i + 1] + bO[i + 1])
        return carry

    lax.fori_loop(0, 16, restrict, 0, unroll=4)

    halve = one_hot((256, 128), lambda i, j: (i >> 1) == j)
    f1 = 0.125 * matmul(pair_r[...].reshape(128, 256), halve)
    b1 = 0.125 * matmul(pair_b[...].reshape(128, 256), halve)
    own[0:16] = f1.reshape(16, 8, 128)
    own[16:32] = b1.reshape(16, 8, 128)

    for k in range(8):
        tmp[8 * k : 8 * k + 8, :] = own[16 + 2 * k] + own[17 + 2 * k]
    summed = tmp[pl.ds(0, 32, stride=2), :] + tmp[pl.ds(1, 32, stride=2), :]
    halve = one_hot((128, 128), lambda i, j: (i >> 1) == j)
    b2 = 0.125 * matmul(summed, halve)
    own[32:40] = jnp.zeros((8, 8, 128), F32)
    for k in range(8):
        own[32 + k, 0:4, :] = b2[4 * k : 4 * k + 4]
    bottom[...] = bottom_row([own[32 + 2 * k] + own[33 + 2 * k] for k in range(4)], slab)

    first = jnp.where(slab == 0, 1, 0)
    send[0:H1] = own[pl.ds(first * (16 - H1), H1)]
    send[H1 : 2 * H1 + 1] = own[pl.ds(16 + first * (15 - H1), H1 + 1)]
    send[2 * H1 + 1 :] = own[32:40]


def bottom_row(pairs, slab):
    total = None
    for k, plane in enumerate(pairs):
        spread = one_hot((128, 128), lambda i, j, k=k: jnp.logical_and((i >> 1) + 32 * k == j, i < 64))
        part = matmul(plane, spread)
        total = part if total is None else total + part
    low, high = total[0:1] + total[1:2], total[2:3] + total[3:4]
    row = 0.125 * jnp.where(slab == 0, low, high)
    return jnp.broadcast_to(row, (8, 128))


def level_faces(b, ax, ay, az, inv, n, factor, depth, width, inside):
    row, lane = iota((8, 128), 0), iota((8, 128), 1)
    top, bot = row == depth - 1, row == 0
    end, begin = lane == width - 1, lane == 0
    cell = jnp.logical_and(row < depth, lane < width)
    for i in range(n - 1):
        ax[i] = factor * (b[i] + b[i + 1])
    for i in range(1, n - 1):
        v = b[i]
        fy = factor * (v + jnp.where(end, 0.0, up(v, 1)))
        gy = factor * (v + jnp.where(begin, 0.0, down(v, 1)))
        fz = factor * (v + jnp.where(top, 0.0, up(v, 0)))
        gz = factor * (v + jnp.where(bot, 0.0, down(v, 0)))
        ay[i] = jnp.where(end, 0.0, fy)
        az[i] = jnp.where(top, 0.0, fz)
        center = (fz + gz) + (ax[i] + ax[i - 1]) + (fy + gy)
        inv[i] = jnp.where(jnp.logical_and(cell, inside(i)), 1.0 / center, 0.0)


def nsum_plain(v, ax, ay, az, i):
    here = v[i]
    t = ax[i] * v[i + 1] + ax[i - 1] * v[i - 1]
    t = t + (ay[i] * up(here, 1) + down(ay[i] * here, 1))
    return t + (az[i] * up(here, 0) + down(az[i] * here, 0))


def sweep_plain(v, f, ax, ay, az, inv, odd, shift, first, last):
    row, lane = iota((8, 128), 0), iota((8, 128), 1)
    even = ((row + lane) & 1) == 0
    masks = (even, jnp.logical_not(even))
    for i in range(first, last):
        cells = masks[(i + shift + odd) % 2]
        v[i] = jnp.where(cells, (f[i] + nsum_plain(v, ax, ay, az, i)) * inv[i], v[i])


def first_plain(v, f, inv, shift, first, last):
    row, lane = iota((8, 128), 0), iota((8, 128), 1)
    even = ((row + lane) & 1) == 0
    masks = (even, jnp.logical_not(even))
    for i in range(first, last):
        v[i] = jnp.where(masks[(i + shift) % 2], f[i] * inv[i], 0.0)


def residual_plain(v, f, ax, ay, az, inv, center, i):
    return f[i] - (center * v[i] - nsum_plain(v, ax, ay, az, i))


def center_plain(b, ax, i, factor, depth, width):
    row, lane = iota((8, 128), 0), iota((8, 128), 1)
    v = b[i]
    fy = jnp.where(lane == width - 1, 0.0, up(v, 1)) + jnp.where(lane == 0, 0.0, down(v, 1))
    fz = jnp.where(row == depth - 1, 0.0, up(v, 0)) + jnp.where(row == 0, 0.0, down(v, 0))
    return factor * (4.0 * v + fy + fz) + (ax[i] + ax[i - 1])


def middle_kernel(place, own, halo, bottom, v1, f1, ax1, ay1, az1, inv1, ax2, ay2, az2, inv2, send, message, b1, b2, v2, f2, tmp):
    slab, box, boxes = place[0], place[1], place[2]
    w = H1 + 1
    b1[0:w] = halo[0, H1 : H1 + w]
    b1[w : w + 16] = own[16:32]
    b1[w + 16 :] = halo[1, H1 : H1 + w]
    f1[0:1] = jnp.zeros((1, 8, 128), F32)
    f1[1 : 1 + H1] = halo[0, 0:H1]
    f1[w : w + 16] = own[0:16]
    f1[w + 16 : w + 16 + H1] = halo[1, 0:H1]
    f1[N1 - 1 :] = jnp.zeros((1, 8, 128), F32)
    b2[0:8] = halo[0, H1 + w :]
    b2[8:16] = own[32:40]
    b2[16:24] = halo[1, H1 + w :]
    v1[...] = jnp.zeros(v1.shape, F32)
    v2[...] = jnp.zeros(v2.shape, F32)
    f2[...] = jnp.zeros(f2.shape, F32)

    def within(size, width):
        def inside(i):
            x = box * size - width + i
            return jnp.logical_and(x >= 0, x < boxes * size)

        return inside

    k1, k2 = 0.5 * 0.25, 0.5 * 0.25**2
    level_faces(b1, ax1, ay1, az1, inv1, N1, k1, 8, 128, within(16, w))
    level_faces(b2, ax2, ay2, az2, inv2, N2, k2, 4, 64, within(8, 8))

    one = (f1, ax1, ay1, az1, inv1)
    first_plain(v1, f1, inv1, 1, 1, N1 - 1)
    sweep_plain(v1, *one, 1, 1, 2, N1 - 2)
    sweep_plain(v1, *one, 0, 1, 3, N1 - 3)
    sweep_plain(v1, *one, 1, 1, 4, N1 - 4)
    for j in range(16):
        parts = [
            residual_plain(v1, *one, center_plain(b1, ax1, i, k1, 8, 128), i)
            for i in (5 + 2 * j, 6 + 2 * j)
        ]
        tmp[8 * j : 8 * j + 8, :] = parts[0] + parts[1]
    summed = tmp[pl.ds(0, 64, stride=2), :] + tmp[pl.ds(1, 64, stride=2), :]
    coarse = 0.125 * matmul(summed, one_hot((128, 128), lambda i, j: (i >> 1) == j))
    for j in range(16):
        f2[4 + j, 0:4, :] = coarse[4 * j : 4 * j + 4]

    two = (f2, ax2, ay2, az2, inv2)
    first_plain(v2, f2, inv2, 0, 4, 20)
    sweep_plain(v2, *two, 1, 0, 5, 19)
    sweep_plain(v2, *two, 0, 0, 6, 18)
    sweep_plain(v2, *two, 1, 0, 7, 17)
    pairs = []
    for k in range(4):
        parts = [
            residual_plain(v2, *two, center_plain(b2, ax2, i, k2, 4, 64), i)
            for i in (8 + 2 * k, 9 + 2 * k)
        ]
        pairs.append(parts[0] + parts[1])
    source = bottom_row(pairs, slab)
    send[0:8] = v2[8:16]
    send[8:16] = f2[8:16]
    rows = jnp.where((iota((8, 128), 0) & 1) == 0, source, bottom[...])
    count = message.shape[0] // 8

    def spread(k, carry):
        message[pl.ds(pl.multiple_of(8 * k, 8), 8), :] = rows
        return carry

    lax.fori_loop(0, count, spread, 0, unroll=4)


def coarse_solve(n, source, coefficient, dref, qref, eref):
    row, lane = iota((n, 128), 0), iota((n, 128), 1)
    factor = 0.5 * 0.25**3
    last = jnp.logical_and(row == n - 1, lane >= 96)
    first = jnp.logical_and(row == 0, lane < 32)
    inner_hi, inner_lo = lane < 96, lane >= 32
    end, begin = (lane & 31) == 31, (lane & 31) == 0

    def xp(v):
        a = pltpu.roll(v, 96, 1)
        return jnp.where(inner_hi, a, up(a, 0))

    def xm(v):
        a = pltpu.roll(v, 32, 1)
        return jnp.where(inner_lo, a, down(a, 0))

    ax, ay, center = [], [], []
    az = factor * (coefficient[0] + coefficient[1])
    for b in coefficient:
        fx = factor * (b + jnp.where(last, 0.0, xp(b)))
        gx = factor * (b + jnp.where(first, 0.0, xm(b)))
        fy = factor * (b + jnp.where(end, 0.0, up(b, 1)))
        gy = factor * (b + jnp.where(begin, 0.0, down(b, 1)))
        ax.append(jnp.where(last, 0.0, fx))
        ay.append(jnp.where(end, 0.0, fy))
        center.append((factor * b + az) + (fx + gx) + (fy + gy))

    def total(u, w):
        s = u[0] * w[0] + u[1] * w[1]
        return jnp.sum(jnp.sum(s, axis=0, keepdims=True), axis=1, keepdims=True)

    for t in range(2):
        dref[t] = source[t]
        qref[t] = source[t]
        eref[t, 8 : 8 + n] = jnp.zeros((n, 128), F32)
        eref[t, 0:8] = jnp.zeros((8, 128), F32)
        eref[t, 8 + n :] = jnp.zeros((8, 128), F32)

    def iterate(k, now):
        d = (dref[0], dref[1])
        w = []
        for t in range(2):
            v = d[t]
            s = ax[t] * xp(v) + xm(ax[t] * v)
            s = s + (ay[t] * up(v, 1) + down(ay[t] * v, 1))
            w.append(center[t] * v - (s + az * d[1 - t]))
        alpha = now / total(d, w)
        q = []
        for t in range(2):
            eref[t, 8 : 8 + n] = eref[t, 8 : 8 + n] + alpha * d[t]
            q.append(qref[t] - alpha * w[t])
            qref[t] = q[t]
        later = total(q, q)
        beta = later / now
        for t in range(2):
            dref[t] = q[t] + beta * d[t]
        return later

    lax.fori_loop(0, ITERS, iterate, total(source, source))


def last_kernel(boxes, place, *refs):
    names = ("all", "own2", "v1", "f1", "ax1", "ay1", "az1", "inv1", "ax2", "ay2", "az2", "inv2")
    given = dict(zip(names, refs))
    refs = refs[len(names) :]
    level0 = dict(zip(PACKED, refs))
    refs = refs[len(PACKED) :]
    out_v, out_r, vR, vB, v1, v2, f2, dref, qref, eref, wide, e0 = refs
    slab, box = place[0], place[1]
    gathered = given["all"]

    source = [gathered[t, pl.ds(0, boxes, stride=2), :] for t in range(2)]
    coefficient = [gathered[t, pl.ds(1, boxes, stride=2), :] for t in range(2)]
    coarse_solve(boxes, source, coefficient, dref, qref, eref)

    base = 2 * boxes
    for side, at in ((0, 0), (1, 16)):
        for k in range(8):
            v2[at + k] = gathered[side, base + 8 * k : base + 8 * k + 8, :]
            f2[at + k] = gathered[side, base + 64 + 8 * k : base + 64 + 8 * k + 8, :]
    v2[8:16] = given["own2"][0:8]
    f2[8:16] = given["own2"][8:16]
    near = [eref[t, pl.ds(7 + box, 8), :] for t in range(2)]
    spread = one_hot((128, 512), lambda i, j: jnp.logical_and(((j >> 7) * 32) + ((j & 127) >> 1) == i, (j & 127) < 64))
    fine = [matmul(e, spread) for e in near]
    row = iota((8, 128), 0)
    for i in range(N2):
        cell, k = (i // 2) // 4, (i // 2) % 4
        low, high = (f[cell : cell + 1, 128 * k : 128 * k + 128] for f in fine)
        v2[i] = v2[i] + jnp.where(row < 2, low, jnp.where(row < 4, high, 0.0))
    two = (f2, given["ax2"], given["ay2"], given["az2"], given["inv2"])
    for k in range(2):
        sweep_plain(v2, *two, 0, 0, 1 + 2 * k, N2 - 1 - 2 * k)
        sweep_plain(v2, *two, 1, 0, 2 + 2 * k, N2 - 2 - 2 * k)

    packed = jnp.concatenate([v2[4 + j, 0:4, :] for j in range(16)], axis=0)
    fine = matmul(packed, one_hot((128, 128), lambda i, j: (j >> 1) == i))
    wide[pl.ds(0, 64, stride=2), :] = fine
    wide[pl.ds(1, 64, stride=2), :] = fine
    for i in range(6, N1 - 6):
        j = (i + 3) // 2 - 4
        v1[i] = given["v1"][i] + wide[8 * j : 8 * j + 8, :]
    one = (given["f1"], given["ax1"], given["ay1"], given["az1"], given["inv1"])
    for k in range(2):
        sweep_plain(v1, *one, 0, 1, 7 + 2 * k, N1 - 7 - 2 * k)
        sweep_plain(v1, *one, 1, 1, 8 + 2 * k, N1 - 8 - 2 * k)

    double = one_hot((128, 256), lambda i, j: (j >> 1) == i)
    e0[...] = matmul(v1[10:32].reshape(176, 128), double).reshape(22, 8, 256)
    lv = dict(level0, vR=vR, vB=vB)

    def correct(j, carry):
        e = e0[j]
        vB[3 + 2 * j] = level0["vB"][3 + 2 * j] + e
        vB[4 + 2 * j] = level0["vB"][4 + 2 * j] + e
        return carry

    lax.fori_loop(0, 22, correct, 0, unroll=2)
    for k in range(2):
        sweep_packed(lv, True, 5 + 2 * k, N0 - 5 - 2 * k)
        sweep_packed(lv, False, 6 + 2 * k, N0 - 6 - 2 * k)

    for x in range(32):
        i = H0 + x
        red, black, p = residual_packed(lv, i)
        for out, a, b in ((out_v, vR[i], vB[i]), (out_r, red, black)):
            even, odd = jnp.where(p, a, b), jnp.where(p, b, a)
            even = jnp.where(slab == 0, even[0:4], even[4:8])
            odd = jnp.where(slab == 0, odd[0:4], odd[4:8])
            for half in range(2):
                lanes = slice(128 * half, 128 * half + 128)
                out[slab_rows(x, half, 0), :] = even[:, lanes]
                out[slab_rows(x, half, 1), :] = odd[:, lanes]


def call(kernel, outs, scratch, *args, scalars=0):
    vmem = pl.BlockSpec(memory_space=pltpu.VMEM)
    smem = pl.BlockSpec(memory_space=pltpu.SMEM)
    shapes = [jax.ShapeDtypeStruct(s, F32) for s in outs]
    return pl.pallas_call(
        kernel,
        out_shape=shapes,
        in_specs=[smem] * scalars + [vmem] * (len(args) - scalars),
        out_specs=[vmem] * len(shapes),
        scratch_shapes=[pltpu.VMEM(s, F32) for s in scratch],
        compiler_params=pltpu.CompilerParams(vmem_limit_bytes=40 * 1024 * 1024),
    )(*args)


def by_tiles(a):
    return a.reshape(8, 4, 8, 2, 128).transpose(0, 1, 3, 2, 4).reshape(512, 128)


def from_tiles(a):
    return a.reshape(8, 4, 2, 8, 128).transpose(0, 1, 3, 2, 4).reshape(8, 32, 256)


def body(pressure_guess, right_side, coefficient):
    boxes = lax.axis_size("box")
    slab, box = lax.axis_index("slab"), lax.axis_index("box")
    place = jnp.stack([slab, box, jnp.int32(boxes), jnp.int32(0)]).astype(jnp.int32)
    rightward = [(i, i + 1) for i in range(boxes - 1)]
    leftward = [(i + 1, i) for i in range(boxes - 1)]
    both = [(2 * i, 2 * i + 2) for i in range(boxes - 1)] + [(2 * i + 3, 2 * i + 1) for i in range(boxes - 1)]

    flat = [by_tiles(a) for a in (pressure_guess, right_side, coefficient)]
    low, high = call(pack_kernel, [(16 * ROWS, 256)] * 2, [], *flat)
    from_left = lax.ppermute(high[16 * ROWS - EDGE :], "box", rightward)
    from_right = lax.ppermute(low[:EDGE], "box", leftward)
    low, high = lax.all_gather(low, "slab"), lax.all_gather(high, "slab")
    halo = lax.all_gather(jnp.stack([from_left, from_right]), "slab")

    plane = (N0, 8, 256)
    fine = call(
        fine_kernel,
        [plane] * len(PACKED) + [(40, 8, 128), (SEND1, 8, 128), (8, 128)],
        [plane] * 3 + [(16, 8, 256)] * 2 + [(64, 128)],
        place,
        low,
        high,
        halo,
        scalars=1,
    )
    level0 = fine[: len(PACKED)]
    own, send, bottom = fine[len(PACKED) :]
    halo = lax.all_gather(lax.ppermute(send, ("box", "slab"), both), "slab")

    one, two = (N1, 8, 128), (N2, 8, 128)
    *levels, send, message = call(
        middle_kernel,
        [one] * 6 + [two] * 4 + [(16, 8, 128), (2 * boxes, 128)],
        [one, two, two, two, (128, 128)],
        place,
        own,
        halo,
        bottom,
        scalars=1,
    )
    beside = lax.ppermute(send, ("box", "slab"), both)
    spread = lax.all_to_all(message.reshape(boxes, 2, 128), "box", 0, 0)
    both_parts = jnp.concatenate([spread.reshape(2 * boxes, 128), beside.reshape(128, 128)], axis=0)
    gathered = lax.all_gather(both_parts, "slab")

    flat_out = [(512, 128)] * 2
    pressure, residual = call(
        functools.partial(last_kernel, boxes),
        flat_out,
        [plane, plane, one, two, two, (2, boxes, 128), (2, boxes, 128), (2, boxes + 16, 128), (128, 128), (22, 8, 256)],
        place,
        gathered,
        send,
        *levels,
        *level0,
        scalars=1,
    )
    return from_tiles(pressure), from_tiles(residual)


def solution(mesh):
    split = P("slab", "box", None)
    return jax.shard_map(body, mesh=mesh, in_specs=(split,) * 3, out_specs=(split,) * 2, check_vma=False)
```

time: 768 us -> 108 us (0.14)
  the two profiles are of different devices: /device:TPU:127 before, /device:TPU:1 now
where the time goes in v1:
time: 108 us; the launch traced here: 107 us
  starting transfers between devices  32.8 us (30%)
  local copies, waits for them, and re-layouts  22.7 us (21%)
  Pallas kernels  20.4 us (19%)
  waiting for transfers between devices  14.9 us (14%)
  blocking collectives  14.7 us (14%)
  other arithmetic  1.1 us (1%)
    all_to_all x1, starting transfers between devices, body(): spread = lax.all_to_all(message.reshape(boxes, 2, 128), 'box', 0, 0)  25 us
    unnamed x68, local copies, waits for them, and re-layouts  22.7 us
    pallas_call x4, Pallas kernels, call(): pl.pallas_call(kernel, out_shape=shapes, in_specs=[smem] * scalars + [vme...  20.4 us
    all_to_all x1, waiting for transfers between devices, body(): spread = lax.all_to_all(message.reshape(boxes, 2, 128), 'box', 0, 0)  5.16 us
    all_gather x2, blocking collectives, body(): low, high = (lax.all_gather(low, 'slab'), lax.all_gather(high, 'slab'))  5.12 us
    ppermute x1, waiting for transfers between devices, body(): beside = lax.ppermute(send, ('box', 'slab'), both)  4.58 us
    ppermute x1, waiting for transfers between devices, body(): halo = lax.all_gather(lax.ppermute(send, ('box', 'slab'), both), 'slab')  4.46 us
    ppermute x1, starting transfers between devices, body(): from_left = lax.ppermute(high[16 * ROWS - EDGE:], 'box', rightward)  3.96 us
  transfers between devices with their start and end apart: 5, of which 4 were waited for; matrix products, arithmetic and copies ran while one was open for 0% of the time, Pallas kernels for 0%

profile of v1, /device:TPU:1, one launch (start us, length us, event | category | flops | bytes accessed | tf_op | source)
XLA Modules:
  0.0 107.4 jit_solution(9429266300953680772)
XLA Ops:
  0.6 0.9 copy-done.12
  1.6 0.9 copy-done.13
  2.5 0.9 copy-done.14
  4.0 4.0 %collective-permute-start = (f32[184,256]{1,0:T(8,128)S(1)}, f32[184,256]{1,0:T(8,128)S(1)}, u32[]{:S(2)}, u32[]{:S(2)}) collective-permute-start(f32[184,256]{1,0:T(8,128)S(1)} %slice.6), channel_id=1, source_target_pairs={{0,2},{2,4},{4,6},{6,8},{8,10},{10,12},{12,14},{14,16},{16,18},{18... | collective-permute-start | bytes 565256 | tf_op jit(solution)/shard_map/ppermute | solution.py:515
  8.0 1.3 %collective-permute-start.1 = (f32[184,256]{1,0:T(8,128)S(1)}, f32[184,256]{1,0:T(8,128)S(1)}, u32[]{:S(2)}, u32[]{:S(2)}) collective-permute-start(f32[184,256]{1,0:T(8,128)S(1)} %slice.7), channel_id=1, source_target_pairs={{2,0},{4,2},{6,4},{8,6},{10,8},{12,10},{14,12},{16,14},{18,16},{20... | collective-permute-start | bytes 565256 | tf_op jit(solution)/shard_map/ppermute | solution.py:516
  9.3 2.9 %all-gather.1 = f32[640,256]{1,0:T(8,128)S(1)} all-gather(f32[320,256]{1,0:T(8,128)S(1)} %get-tuple-element.35), channel_id=3, replica_groups=mesh['box'=128,'slab'=2] {'slab'}, dimensions={0}, use_global_device_ids=true | all-gather | bytes 983040 | tf_op jit(solution)/shard_map/all_gather | solution.py:517
  12.2 2.3 %all-gather = f32[640,256]{1,0:T(8,128)S(1)} all-gather(f32[320,256]{1,0:T(8,128)S(1)} %get-tuple-element.34), channel_id=2, replica_groups=mesh['box'=128,'slab'=2] {'slab'}, dimensions={0}, use_global_device_ids=true | all-gather | bytes 983040 | tf_op jit(solution)/shard_map/all_gather | solution.py:517
  15.2 3.8 %all-gather.2 = f32[4,184,256]{2,1,0:T(8,128)S(1)} all-gather(f32[2,184,256]{2,1,0:T(8,128)S(1)} %pad_maximum_fusion), channel_id=4, replica_groups=mesh['box'=128,'slab'=2] {'slab'}, dimensions={0}, use_global_device_ids=true | all-gather | bytes 1130496 | tf_op jit(solution)/shard_map/all_gather | solution.py:518
  19.0 6.8 %shard_map.51 = (f32[50,8,256]{2,1,0:T(8,128)S(1)}, f32[50,8,256]{2,1,0:T(8,128)S(1)}, f32[50,8,256]{2,1,0:T(8,128)S(1)}, f32[50,8,256]{2,1,0:T(8,128)S(1)}, f32...) custom-call(s32[4]{0:T(128)S(1)} %pad_add_fusion.place, ...), custom_call_target="tpu_custom_call" | custom-call | tf_op jit(solution)/shard_map/pallas_call | solution.py:487
  25.8 0.8 copy-done
  28.9 1.3 %collective-permute-start.2 = (f32[33,8,128]{2,1,0:T(8,128)S(1)}, f32[33,8,128]{2,1,0:T(8,128)S(1)}, u32[]{:S(2)}, u32[]{:S(2)}) collective-permute-start(f32[33,8,128]{2,1,0:T(8,128)S(1)} %get-tuple-element.37), channel_id=1, source_target_pairs={{0,2},{2,4},{4,6},{6,8},{8,10},{10,12},{12,14},{14,16},{16,18},{18... | collective-permute-start | bytes 405512 | tf_op jit(solution)/shard_map/ppermute | solution.py:533
  30.2 4.5 %collective-permute-done.2 = f32[33,8,128]{2,1,0:T(8,128)S(1)} collective-permute-done((f32[33,8,128]{2,1,0:T(8,128)S(1)}, f32[33,8,128]{2,1,0:T(8,128)S(1)}, u32[]{:S(2)}, u32[]{:S(2)}) %collective-permute-start.2) | collective-permute-done | bytes 135200 | tf_op jit(solution)/shard_map/ppermute | solution.py:533
  34.6 2.2 %all-gather.3 = f32[66,8,128]{2,1,0:T(8,128)S(1)} all-gather(f32[33,8,128]{2,1,0:T(8,128)S(1)} %collective-permute-done.2), channel_id=5, replica_groups=mesh['box'=128,'slab'=2] {'slab'}, dimensions={0}, use_global_device_ids=true | all-gather | bytes 405504 | tf_op jit(solution)/shard_map/all_gather | solution.py:533
  36.8 2.4 %shard_map.52 = (f32[42,8,128]{2,1,0:T(8,128)S(1)}, f32[42,8,128]{2,1,0:T(8,128)S(1)}, f32[42,8,128]{2,1,0:T(8,128)S(1)}, f32[42,8,128]{2,1,0:T(8,128)S(1)}, f32...) custom-call(s32[4]{0:T(128)S(1)} %pad_add_fusion.place, ...), custom_call_target="tpu_custom_call" | custom-call | tf_op jit(solution)/shard_map/pallas_call | solution.py:487
  45.8 25.0 %all-to-all-start = ((f32[128,2,128]{2,1,0:T(2,128)}), f32[128,2,128]{2,1,0:T(2,128)}, u32[]{:S(2)}, u32[]{:S(2)}) async-start(f32[128,2,128]{2,1,0:T(2,128)} %bitcast.45), calls=%async_computation | async-start | bytes 262144 | tf_op jit(solution)/shard_map/all_to_all | solution.py:547
  70.8 1.3 %collective-permute-start.3 = (f32[16,8,128]{2,1,0:T(8,128)}, f32[16,8,128]{2,1,0:T(8,128)}, u32[]{:S(2)}, u32[]{:S(2)}) collective-permute-start(f32[16,8,128]{2,1,0:T(8,128)} %copy-done.32), channel_id=1, source_target_pairs={{0,2},{2,4},{4,6},{6,8},{8,10},{10,12},{12,14},{14,16},{16,18},{18... | collective-permute-start | bytes 196616 | tf_op jit(solution)/shard_map/ppermute | solution.py:546
  72.1 4.6 %collective-permute-done.3 = f32[16,8,128]{2,1,0:T(8,128)} collective-permute-done((f32[16,8,128]{2,1,0:T(8,128)}, f32[16,8,128]{2,1,0:T(8,128)}, u32[]{:S(2)}, u32[]{:S(2)}) %collective-permute-start.3) | collective-permute-done | bytes 65568 | tf_op jit(solution)/shard_map/ppermute | solution.py:546
  76.7 5.2 %all-to-all-done = f32[128,2,128]{2,1,0:T(2,128)} async-done(((f32[128,2,128]{2,1,0:T(2,128)}), f32[128,2,128]{2,1,0:T(2,128)}, u32[]{:S(2)}, u32[]{:S(2)}) %all-to-all-start) | async-done | bytes 131104 | tf_op jit(solution)/shard_map/all_to_all | solution.py:547
  81.9 1.0 pad_maximum_fusion.1
  82.9 3.6 %all-gather.4 = f32[768,128]{1,0:T(8,128)S(1)} all-gather(f32[384,128]{1,0:T(8,128)S(1)} %pad_maximum_fusion.1), channel_id=6, replica_groups=mesh['box'=128,'slab'=2] {'slab'}, dimensions={0}, use_global_device_ids=true | all-gather | bytes 589824 | tf_op jit(solution)/shard_map/all_gather | solution.py:549
  86.5 1.0 copy-done.7
  87.5 1.0 copy-done.9
  88.5 1.0 copy-done.11
  89.5 0.9 copy-done.16
  90.4 0.9 copy-done.18
  91.3 0.9 copy-done.20
  92.2 0.9 copy-done.22
  93.1 0.9 copy-done.24
  94.1 0.9 copy-done.27
  95.0 0.9 copy-done.29
  95.8 0.9 copy-done.31
  96.7 10.7 %shard_map.53 = (f32[512,128]{1,0:T(8,128)}, f32[512,128]{1,0:T(8,128)}) custom-call(s32[4]{0:T(128)S(1)} %pad_add_fusion.place, f32[2,384,128]{2,1,0:T(8,128)S(1)} %bitcast.40, f32[16,8,128]{2,1,0:T(8,128)S(1)} %copy-done.33, f32[42,8,128]{2,1,0:T(8,128)S(1)} %get-tuple-element.41.refs_2_, f32[42,8,128]{2,1,0:T(8,128)S(1)} %copy-done.16, ...), custom_call_target="tpu_custom_call" | custom-call | tf_op jit(solution)/shard_map/pallas_call | solution.py:487
  (60 shorter events, 10.1 us)
Async XLA Ops:
  0.6 1.0 copy-start.12
  1.6 0.9 copy-start.13
  2.5 0.9 copy-start.14
  4.0 10.5 %collective-permute-start = (f32[184,256]{1,0:T(8,128)S(1)}, f32[184,256]{1,0:T(8,128)S(1)}, u32[]{:S(2)}, u32[]{:S(2)}) collective-permute-start(f32[184,256]{1,0:T(8,128)S(1)} %slice.6), channel_id=1, source_target_pairs={{0,2},{2,4},{4,6},{6,8},{8,10},{10,12},{12,14},{14,16},{16,18},{18... | collective-permute-start | bytes 565256 | tf_op jit(solution)/shard_map/ppermute | solution.py:515
  8.0 7.2 %collective-permute-start.1 = (f32[184,256]{1,0:T(8,128)S(1)}, f32[184,256]{1,0:T(8,128)S(1)}, u32[]{:S(2)}, u32[]{:S(2)}) collective-permute-start(f32[184,256]{1,0:T(8,128)S(1)} %slice.7), channel_id=1, source_target_pairs={{2,0},{4,2},{6,4},{8,6},{10,8},{12,10},{14,12},{16,14},{18,16},{20... | collective-permute-start | bytes 565256 | tf_op jit(solution)/shard_map/ppermute | solution.py:516
  25.8 0.8 copy-start
  26.6 0.7 copy-start.6
  27.4 0.8 copy-start.8
  28.2 0.7 copy-start.10
  28.9 10.3 %copy-start.2 = (f32[50,8,256]{2,1,0:T(8,128)}, f32[50,8,256]{2,1,0:T(8,128)S(1)}, u32[]{:S(2)}) copy-start(f32[50,8,256]{2,1,0:T(8,128)S(1)} %get-tuple-element.59.refs_20_) | copy-start | bytes 1228804
  28.9 10.3 %copy-start.4 = (f32[50,8,256]{2,1,0:T(8,128)}, f32[50,8,256]{2,1,0:T(8,128)S(1)}, u32[]{:S(2)}) copy-start(f32[50,8,256]{2,1,0:T(8,128)S(1)} %get-tuple-element.60.refs_21_) | copy-start | bytes 1228804
  28.9 5.7 %collective-permute-start.2 = (f32[33,8,128]{2,1,0:T(8,128)S(1)}, f32[33,8,128]{2,1,0:T(8,128)S(1)}, u32[]{:S(2)}, u32[]{:S(2)}) collective-permute-start(f32[33,8,128]{2,1,0:T(8,128)S(1)} %get-tuple-element.37), channel_id=1, source_target_pairs={{0,2},{2,4},{4,6},{6,8},{8,10},{10,12},{12,14},{14,16},{16,18},{18... | collective-permute-start | bytes 405512 | tf_op jit(solution)/shard_map/ppermute | solution.py:533
  39.2 0.7 copy-start.15
  39.9 0.7 copy-start.17
  41.2 0.7 copy-start.21
  45.8 40.7 %copy-start.5 = (f32[50,8,256]{2,1,0:T(8,128)S(1)}, f32[50,8,256]{2,1,0:T(8,128)}, u32[]{:S(2)}) copy-start(f32[50,8,256]{2,1,0:T(8,128)} %copy-done.4) | copy-start | bytes 1228804
  45.8 36.1 %all-to-all-start = ((f32[128,2,128]{2,1,0:T(2,128)}), f32[128,2,128]{2,1,0:T(2,128)}, u32[]{:S(2)}, u32[]{:S(2)}) async-start(f32[128,2,128]{2,1,0:T(2,128)} %bitcast.45), calls=%async_computation | async-start | bytes 262144 | tf_op jit(solution)/shard_map/all_to_all | solution.py:547
  70.8 5.9 %collective-permute-start.3 = (f32[16,8,128]{2,1,0:T(8,128)}, f32[16,8,128]{2,1,0:T(8,128)}, u32[]{:S(2)}, u32[]{:S(2)}) collective-permute-start(f32[16,8,128]{2,1,0:T(8,128)} %copy-done.32), channel_id=1, source_target_pairs={{0,2},{2,4},{4,6},{6,8},{8,10},{10,12},{12,14},{14,16},{16,18},{18... | collective-permute-start | bytes 196616 | tf_op jit(solution)/shard_map/ppermute | solution.py:546
  81.9 4.6 %copy-start.3 = (f32[50,8,256]{2,1,0:T(8,128)S(1)}, f32[50,8,256]{2,1,0:T(8,128)}, u32[]{:S(2)}) copy-start(f32[50,8,256]{2,1,0:T(8,128)} %copy-done.2) | copy-start | bytes 1228804
  82.9 3.6 %copy-start.1 = (f32[50,8,256]{2,1,0:T(8,128)S(1)}, f32[50,8,256]{2,1,0:T(8,128)}, u32[]{:S(2)}) copy-start(f32[50,8,256]{2,1,0:T(8,128)} %copy-done) | copy-start | bytes 1228804
  82.9 3.6 %copy-start.33 = (f32[16,8,128]{2,1,0:T(8,128)S(1)}, f32[16,8,128]{2,1,0:T(8,128)}, u32[]{:S(2)}) copy-start(f32[16,8,128]{2,1,0:T(8,128)} %copy-done.32) | copy-start | bytes 196612
  86.5 1.0 copy-start.7
  87.5 1.0 copy-start.9
  88.5 1.0 copy-start.11
  89.5 0.9 copy-start.16
  90.4 0.9 copy-start.18
  91.3 0.9 copy-start.20
  92.2 0.9 copy-start.22
  93.1 0.9 copy-start.24
  94.1 0.9 copy-start.27
  95.0 0.9 copy-start.29
  95.8 0.9 copy-start.31
  (7 other events, 4.5 us)

commit v2 on v1

--- a/solution.py
+++ b/solution.py
@@ -52,7 +52,12 @@
     return pl.ds((x // 8) * 16 + half * 8 + x % 8 + 64 * odd, 4, stride=128)
 
 
-def pack_kernel(g, r, c, low, high):
+def pack_kernel(g_hbm, r_hbm, c_hbm, low, high, g, r, c, sem):
+    copies = [pltpu.make_async_copy(a, b, sem.at[k]) for k, (a, b) in enumerate(((g_hbm, g), (r_hbm, r), (c_hbm, c)))]
+    for copy in copies:
+        copy.start()
+    for copy in copies:
+        copy.wait()
     even_y = (iota((4, 128), 1) & 1) == 0
     odd_y = jnp.logical_not(even_y)
     for x in range(32):
@@ -263,7 +268,7 @@
         v[i] = jnp.where(masks[(i + shift) % 2], f[i] * inv[i], 0.0)
 
 
-def residual_plain(v, f, ax, ay, az, inv, center, i):
+def residual_plain(v, f, ax, ay, az, center, i):
     return f[i] - (center * v[i] - nsum_plain(v, ax, ay, az, i))
 
 
@@ -275,8 +280,8 @@
     return factor * (4.0 * v + fy + fz) + (ax[i] + ax[i - 1])
 
 
-def middle_kernel(place, own, halo, bottom, v1, f1, ax1, ay1, az1, inv1, ax2, ay2, az2, inv2, send, message, b1, b2, v2, f2, tmp):
-    slab, box, boxes = place[0], place[1], place[2]
+def middle_kernel(place, own, halo, v1, f1, ax1, ay1, az1, inv1, ax2, ay2, az2, inv2, send, v2, f2, b2, b1, tmp):
+    box, boxes = place[1], place[2]
     w = H1 + 1
     b1[0:w] = halo[0, H1 : H1 + w]
     b1[w : w + 16] = own[16:32]
@@ -311,7 +316,7 @@
     sweep_plain(v1, *one, 1, 1, 4, N1 - 4)
     for j in range(16):
         parts = [
-            residual_plain(v1, *one, center_plain(b1, ax1, i, k1, 8, 128), i)
+            residual_plain(v1, *one[:4], center_plain(b1, ax1, i, k1, 8, 128), i)
             for i in (5 + 2 * j, 6 + 2 * j)
         ]
         tmp[8 * j : 8 * j + 8, :] = parts[0] + parts[1]
@@ -325,6 +330,12 @@
     sweep_plain(v2, *two, 1, 0, 5, 19)
     sweep_plain(v2, *two, 0, 0, 6, 18)
     sweep_plain(v2, *two, 1, 0, 7, 17)
+    send[0:8] = v2[8:16]
+    send[8:16] = f2[8:16]
+
+
+def source_kernel(place, v2, f2, b2, ax2, ay2, az2, bottom, rows):
+    two, k2 = (f2, ax2, ay2, az2), 0.5 * 0.25**2
     pairs = []
     for k in range(4):
         parts = [
@@ -332,17 +343,15 @@
             for i in (8 + 2 * k, 9 + 2 * k)
         ]
         pairs.append(parts[0] + parts[1])
-    source = bottom_row(pairs, slab)
-    send[0:8] = v2[8:16]
-    send[8:16] = f2[8:16]
-    rows = jnp.where((iota((8, 128), 0) & 1) == 0, source, bottom[...])
-    count = message.shape[0] // 8
-
-    def spread(k, carry):
-        message[pl.ds(pl.multiple_of(8 * k, 8), 8), :] = rows
-        return carry
-
-    lax.fori_loop(0, count, spread, 0, unroll=4)
+    source = bottom_row(pairs, place[0])
+    rows[...] = jnp.where((iota((8, 128), 0) & 1) == 0, source, bottom[...])
+
+
+def spread_kernel(rows, beside, message):
+    del beside
+    value = rows[...]
+    for k in range(message.shape[0] // 8):
+        message[8 * k : 8 * k + 8, :] = value
 
 
 def coarse_solve(n, source, coefficient, dref, qref, eref):
@@ -480,17 +489,27 @@
                 out[slab_rows(x, half, 1), :] = odd[:, lanes]
 
 
-def call(kernel, outs, scratch, *args, scalars=0):
+def call(kernel, outs, scratch, *args, scalars=0, limit=12):
     vmem = pl.BlockSpec(memory_space=pltpu.VMEM)
     smem = pl.BlockSpec(memory_space=pltpu.SMEM)
-    shapes = [jax.ShapeDtypeStruct(s, F32) for s in outs]
     return pl.pallas_call(
         kernel,
-        out_shape=shapes,
+        out_shape=[jax.ShapeDtypeStruct(s, F32) for s in outs],
         in_specs=[smem] * scalars + [vmem] * (len(args) - scalars),
-        out_specs=[vmem] * len(shapes),
+        out_specs=[vmem] * len(outs),
         scratch_shapes=[pltpu.VMEM(s, F32) for s in scratch],
-        compiler_params=pltpu.CompilerParams(vmem_limit_bytes=40 * 1024 * 1024),
+        compiler_params=pltpu.CompilerParams(vmem_limit_bytes=limit * 1024 * 1024),
+    )(*args)
+
+
+def pack(*args):
+    return pl.pallas_call(
+        pack_kernel,
+        out_shape=[jax.ShapeDtypeStruct((16 * ROWS, 256), F32)] * 2,
+        in_specs=[pl.BlockSpec(memory_space=pltpu.HBM)] * 3,
+        out_specs=[pl.BlockSpec(memory_space=pltpu.VMEM)] * 2,
+        scratch_shapes=[pltpu.VMEM((512, 128), F32)] * 3 + [pltpu.SemaphoreType.DMA((3,))],
+        compiler_params=pltpu.CompilerParams(vmem_limit_bytes=4 * 1024 * 1024),
     )(*args)
 
 
@@ -511,7 +530,7 @@
     both = [(2 * i, 2 * i + 2) for i in range(boxes - 1)] + [(2 * i + 3, 2 * i + 1) for i in range(boxes - 1)]
 
     flat = [by_tiles(a) for a in (pressure_guess, right_side, coefficient)]
-    low, high = call(pack_kernel, [(16 * ROWS, 256)] * 2, [], *flat)
+    low, high = pack(*flat)
     from_left = lax.ppermute(high[16 * ROWS - EDGE :], "box", rightward)
     from_right = lax.ppermute(low[:EDGE], "box", leftward)
     low, high = lax.all_gather(low, "slab"), lax.all_gather(high, "slab")
@@ -533,17 +552,18 @@
     halo = lax.all_gather(lax.ppermute(send, ("box", "slab"), both), "slab")
 
     one, two = (N1, 8, 128), (N2, 8, 128)
-    *levels, send, message = call(
+    *levels, send, v2, f2, b2 = call(
         middle_kernel,
-        [one] * 6 + [two] * 4 + [(16, 8, 128), (2 * boxes, 128)],
-        [one, two, two, two, (128, 128)],
+        [one] * 6 + [two] * 4 + [(16, 8, 128)] + [two] * 3,
+        [one, (128, 128)],
         place,
         own,
         halo,
-        bottom,
         scalars=1,
     )
     beside = lax.ppermute(send, ("box", "slab"), both)
+    (rows,) = call(source_kernel, [(8, 128)], [], place, v2, f2, b2, *levels[6:9], bottom, scalars=1)
+    (message,) = call(spread_kernel, [(2 * boxes, 128)], [], rows, beside)
     spread = lax.all_to_all(message.reshape(boxes, 2, 128), "box", 0, 0)
     both_parts = jnp.concatenate([spread.reshape(2 * boxes, 128), beside.reshape(128, 128)], axis=0)
     gathered = lax.all_gather(both_parts, "slab")

time: 108 us -> 95.7 us (0.89)
  blocking collectives: 14.7 us -> 53.9 us
  starting transfers between devices: 32.8 us -> 7.83 us
  local copies, waits for them, and re-layouts: 22.7 us -> 2.87 us
  waiting for transfers between devices: 14.9 us -> 8.75 us
    all_to_all x0 -> x1, blocking collectives: none -> 40.6 us  [body(): spread = lax.all_to_all(message.reshape(boxes, 2, 128), 'box', 0, 0)]
    all_to_all x1 -> x0, starting transfers between devices: 25 us -> none  [body(): spread = lax.all_to_all(message.reshape(boxes, 2, 128), 'box', 0, 0)]
    unnamed x68 -> x6, local copies, waits for them, and re-layouts: 22.7 us -> 2.84 us
    all_to_all x1 -> x0, waiting for transfers between devices: 5.16 us -> none  [body(): spread = lax.all_to_all(message.reshape(boxes, 2, 128), 'box', 0, 0)]
    all_gather x1, blocking collectives: 3.55 us -> 2.09 us  [body(): gathered = lax.all_gather(both_parts, 'slab')]
    pallas_call x4 -> x6, Pallas kernels: 20.4 us -> 21.2 us  [the longest x5 20.6 us: call(): pl.pallas_call(kernel, out_shape=[jax.ShapeDtypeStruct(s, F32) for s in o...]
  transfers between devices with their start and end apart: 5 -> 4, of which waited for: 4 -> 3; matrix products, arithmetic and copies ran while one was open for 0% -> 0% of each run, Pallas kernels for 0% -> 1%
where the time goes in v2:
time: 95.7 us; the launch traced here: 95.4 us
  blocking collectives  53.9 us (56%)
  Pallas kernels  21.2 us (22%)
  waiting for transfers between devices  8.75 us (9%)
  starting transfers between devices  7.83 us (8%)
  local copies, waits for them, and re-layouts  2.87 us (3%)
    all_to_all x1, blocking collectives, body(): spread = lax.all_to_all(message.reshape(boxes, 2, 128), 'box', 0, 0)  40.6 us
    pallas_call x5, Pallas kernels, call(): pl.pallas_call(kernel, out_shape=[jax.ShapeDtypeStruct(s, F32) for s in o...  20.6 us
    all_gather x2, blocking collectives, body(): low, high = (lax.all_gather(low, 'slab'), lax.all_gather(high, 'slab'))  5.12 us
    ppermute x1, waiting for transfers between devices, body(): halo = lax.all_gather(lax.ppermute(send, ('box', 'slab'), both), 'slab')  4.46 us
    ppermute x1, starting transfers between devices, body(): from_left = lax.ppermute(high[16 * ROWS - EDGE:], 'box', rightward)  3.96 us
    all_gather x1, blocking collectives, body(): halo = lax.all_gather(jnp.stack([from_left, from_right]), 'slab')  3.84 us
    ppermute x1, waiting for transfers between devices, body(): beside = lax.ppermute(send, ('box', 'slab'), both)  3.63 us
    unnamed x6, local copies, waits for them, and re-layouts  2.84 us
  transfers between devices with their start and end apart: 4, of which 3 were waited for; matrix products, arithmetic and copies ran while one was open for 0% of the time, Pallas kernels for 1%

profile of v2, /device:TPU:1, one launch (start us, length us, event | category | flops | bytes accessed | tf_op | source)
XLA Modules:
  0.0 95.4 jit_solution(10524908680053008988)
XLA Ops:
  0.6 0.0 copy-start
  0.6 0.9 copy-done
  1.6 0.0 copy-start.1
  1.6 0.9 copy-done.1
  2.5 0.0 copy-start.2
  2.5 0.9 copy-done.2
  3.5 0.6 shard_map.50
  4.1 4.0 %collective-permute-start = (f32[184,256]{1,0:T(8,128)S(1)}, f32[184,256]{1,0:T(8,128)S(1)}, u32[]{:S(2)}, u32[]{:S(2)}) collective-permute-start(f32[184,256]{1,0:T(8,128)S(1)} %slice.6), channel_id=1, source_target_pairs={{0,2},{2,4},{4,6},{6,8},{8,10},{10,12},{12,14},{14,16},{16,18},{18... | collective-permute-start | bytes 565256 | tf_op jit(solution)/shard_map/ppermute | solution.py:534
  8.1 1.3 %collective-permute-start.1 = (f32[184,256]{1,0:T(8,128)S(1)}, f32[184,256]{1,0:T(8,128)S(1)}, u32[]{:S(2)}, u32[]{:S(2)}) collective-permute-start(f32[184,256]{1,0:T(8,128)S(1)} %slice.7), channel_id=1, source_target_pairs={{2,0},{4,2},{6,4},{8,6},{10,8},{12,10},{14,12},{16,14},{18,16},{20... | collective-permute-start | bytes 565256 | tf_op jit(solution)/shard_map/ppermute | solution.py:535
  9.4 2.9 %all-gather.1 = f32[640,256]{1,0:T(8,128)S(1)} all-gather(f32[320,256]{1,0:T(8,128)S(1)} %get-tuple-element.37), channel_id=3, replica_groups=mesh['box'=128,'slab'=2] {'slab'}, dimensions={0}, use_global_device_ids=true | all-gather | bytes 983040 | tf_op jit(solution)/shard_map/all_gather | solution.py:536
  12.3 0.1 pad_add_fusion.place
  12.3 2.3 %all-gather = f32[640,256]{1,0:T(8,128)S(1)} all-gather(f32[320,256]{1,0:T(8,128)S(1)} %get-tuple-element.36), channel_id=2, replica_groups=mesh['box'=128,'slab'=2] {'slab'}, dimensions={0}, use_global_device_ids=true | all-gather | bytes 983040 | tf_op jit(solution)/shard_map/all_gather | solution.py:536
  14.6 0.0 collective-permute-done
  14.6 0.7 collective-permute-done.1
  15.3 3.8 %all-gather.2 = f32[4,184,256]{2,1,0:T(8,128)S(1)} all-gather(f32[2,184,256]{2,1,0:T(8,128)S(1)} %pad_maximum_fusion), channel_id=4, replica_groups=mesh['box'=128,'slab'=2] {'slab'}, dimensions={0}, use_global_device_ids=true | all-gather | bytes 1130496 | tf_op jit(solution)/shard_map/all_gather | solution.py:537
  19.1 6.9 %shard_map.51 = (f32[50,8,256]{2,1,0:T(8,128)S(1)}, f32[50,8,256]{2,1,0:T(8,128)S(1)}, f32[50,8,256]{2,1,0:T(8,128)S(1)}, f32[50,8,256]{2,1,0:T(8,128)S(1)}, f32...) custom-call(s32[4]{0:T(128)S(1)} %pad_add_fusion.place, ...), custom_call_target="tpu_custom_call" | custom-call | tf_op jit(solution)/shard_map/pallas_call | solution.py:495
  26.0 1.3 %collective-permute-start.2 = (f32[33,8,128]{2,1,0:T(8,128)S(1)}, f32[33,8,128]{2,1,0:T(8,128)S(1)}, u32[]{:S(2)}, u32[]{:S(2)}) collective-permute-start(f32[33,8,128]{2,1,0:T(8,128)S(1)} %get-tuple-element.39), channel_id=1, source_target_pairs={{0,2},{2,4},{4,6},{6,8},{8,10},{10,12},{12,14},{14,16},{16,18},{18... | collective-permute-start | bytes 405512 | tf_op jit(solution)/shard_map/ppermute | solution.py:552
  27.3 4.5 %collective-permute-done.2 = f32[33,8,128]{2,1,0:T(8,128)S(1)} collective-permute-done((f32[33,8,128]{2,1,0:T(8,128)S(1)}, f32[33,8,128]{2,1,0:T(8,128)S(1)}, u32[]{:S(2)}, u32[]{:S(2)}) %collective-permute-start.2) | collective-permute-done | bytes 135200 | tf_op jit(solution)/shard_map/ppermute | solution.py:552
  31.8 2.2 %all-gather.3 = f32[66,8,128]{2,1,0:T(8,128)S(1)} all-gather(f32[33,8,128]{2,1,0:T(8,128)S(1)} %collective-permute-done.2), channel_id=5, replica_groups=mesh['box'=128,'slab'=2] {'slab'}, dimensions={0}, use_global_device_ids=true | all-gather | bytes 405504 | tf_op jit(solution)/shard_map/all_gather | solution.py:552
  34.0 2.2 %shard_map.52 = (f32[42,8,128]{2,1,0:T(8,128)S(1)}, f32[42,8,128]{2,1,0:T(8,128)S(1)}, f32[42,8,128]{2,1,0:T(8,128)S(1)}, f32[42,8,128]{2,1,0:T(8,128)S(1)}, f32...) custom-call(s32[4]{0:T(128)S(1)} %pad_add_fusion.place, ...), custom_call_target="tpu_custom_call" | custom-call | tf_op jit(solution)/shard_map/pallas_call | solution.py:495
  36.1 1.3 %collective-permute-start.3 = (f32[16,8,128]{2,1,0:T(8,128)S(1)}, f32[16,8,128]{2,1,0:T(8,128)S(1)}, u32[]{:S(2)}, u32[]{:S(2)}) collective-permute-start(f32[16,8,128]{2,1,0:T(8,128)S(1)} %get-tuple-element.47.refs_1_), channel_id=1, source_target_pairs={{0,2},{2,4},{4,6},{6,8},{8,10},{10,12},{12,14},{14,16},{16,18},{18... | collective-permute-start | bytes 196616 | tf_op jit(solution)/shard_map/ppermute | solution.py:564
  37.4 0.8 shard_map.53.rows
  38.2 3.6 %collective-permute-done.3.beside = f32[16,8,128]{2,1,0:T(8,128)S(1)} collective-permute-done((f32[16,8,128]{2,1,0:T(8,128)S(1)}, f32[16,8,128]{2,1,0:T(8,128)S(1)}, u32[]{:S(2)}, u32[]{:S(2)}) %collective-permute-start.3) | collective-permute-done | bytes 65568 | tf_op jit(solution)/shard_map/ppermute | solution.py:564
  41.8 40.6 %all_to_all.5 = f32[128,2,128]{2,1,0:T(2,128)S(1)} all-to-all(f32[128,2,128]{2,1,0:T(2,128)S(1)} %bitcast.42), channel_id=1, replica_groups=mesh['box'=128,'slab'=2] {'box'}, dimensions={0} | all-to-all | bytes 262144 | tf_op jit(solution)/shard_map/all_to_all | solution.py:567
  82.5 2.1 %all-gather.4 = f32[768,128]{1,0:T(8,128)S(1)} all-gather(f32[384,128]{1,0:T(8,128)S(1)} %pad_maximum_fusion.1), channel_id=6, replica_groups=mesh['box'=128,'slab'=2] {'slab'}, dimensions={0}, use_global_device_ids=true | all-gather | bytes 589824 | tf_op jit(solution)/shard_map/all_gather | solution.py:569
  84.6 10.8 %shard_map.55 = (f32[512,128]{1,0:T(8,128)}, f32[512,128]{1,0:T(8,128)}) custom-call(s32[4]{0:T(128)S(1)} %pad_add_fusion.place, f32[2,384,128]{2,1,0:T(8,128)S(1)} %bitcast.40, f32[16,8,128]{2,1,0:T(8,128)S(1)} %get-tuple-element.47.refs_1_, f32[42,8,128]{2,1,0:T(8,128)S(1)} %get-tuple-element.48.refs_2_, f32[42,8,128]{2,1,0:T(8,128)S(1)} %get-tuple-element.49.refs_3_, ...), custom_call_target="tpu_custom_call" | custom-call | tf_op jit(solution)/shard_map/pallas_call | solution.py:495
  (5 shorter events, 0.1 us)
Async XLA Ops:
  0.6 1.0 copy-start
  1.6 0.9 copy-start.1
  2.5 0.9 copy-start.2
  4.1 10.5 %collective-permute-start = (f32[184,256]{1,0:T(8,128)S(1)}, f32[184,256]{1,0:T(8,128)S(1)}, u32[]{:S(2)}, u32[]{:S(2)}) collective-permute-start(f32[184,256]{1,0:T(8,128)S(1)} %slice.6), channel_id=1, source_target_pairs={{0,2},{2,4},{4,6},{6,8},{8,10},{10,12},{12,14},{14,16},{16,18},{18... | collective-permute-start | bytes 565256 | tf_op jit(solution)/shard_map/ppermute | solution.py:534
  8.1 7.2 %collective-permute-start.1 = (f32[184,256]{1,0:T(8,128)S(1)}, f32[184,256]{1,0:T(8,128)S(1)}, u32[]{:S(2)}, u32[]{:S(2)}) collective-permute-start(f32[184,256]{1,0:T(8,128)S(1)} %slice.7), channel_id=1, source_target_pairs={{2,0},{4,2},{6,4},{8,6},{10,8},{12,10},{14,12},{16,14},{18,16},{20... | collective-permute-start | bytes 565256 | tf_op jit(solution)/shard_map/ppermute | solution.py:535
  26.0 5.8 %collective-permute-start.2 = (f32[33,8,128]{2,1,0:T(8,128)S(1)}, f32[33,8,128]{2,1,0:T(8,128)S(1)}, u32[]{:S(2)}, u32[]{:S(2)}) collective-permute-start(f32[33,8,128]{2,1,0:T(8,128)S(1)} %get-tuple-element.39), channel_id=1, source_target_pairs={{0,2},{2,4},{4,6},{6,8},{8,10},{10,12},{12,14},{14,16},{16,18},{18... | collective-permute-start | bytes 405512 | tf_op jit(solution)/shard_map/ppermute | solution.py:552
  36.1 5.7 %collective-permute-start.3 = (f32[16,8,128]{2,1,0:T(8,128)S(1)}, f32[16,8,128]{2,1,0:T(8,128)S(1)}, u32[]{:S(2)}, u32[]{:S(2)}) collective-permute-start(f32[16,8,128]{2,1,0:T(8,128)S(1)} %get-tuple-element.47.refs_1_), channel_id=1, source_target_pairs={{0,2},{2,4},{4,6},{6,8},{8,10},{10,12},{12,14},{14,16},{16,18},{18... | collective-permute-start | bytes 196616 | tf_op jit(solution)/shard_map/ppermute | solution.py:564

commit v3 on v2

--- a/solution.py
+++ b/solution.py
@@ -52,7 +52,7 @@
     return pl.ds((x // 8) * 16 + half * 8 + x % 8 + 64 * odd, 4, stride=128)
 
 
-def pack_kernel(g_hbm, r_hbm, c_hbm, low, high, g, r, c, sem):
+def pack_kernel(place, g_hbm, r_hbm, c_hbm, low, high, first, second, g, r, c, sem):
     copies = [pltpu.make_async_copy(a, b, sem.at[k]) for k, (a, b) in enumerate(((g_hbm, g), (r_hbm, r), (c_hbm, c)))]
     for copy in copies:
         copy.start()
@@ -73,6 +73,18 @@
             out[base + 12 : base + 16, lanes] = jnp.where(p0, fo, fe)
             out[base + 16 : base + 20, lanes] = jnp.where(p0, g[odd, :], g[even, :])
 
+    right_first = (place[1] & 1) == 1
+
+    @pl.when(right_first)
+    def _():
+        first[...] = high[16 * ROWS - EDGE :, :]
+        second[...] = low[:EDGE, :]
+
+    @pl.when(jnp.logical_not(right_first))
+    def _():
+        first[...] = low[:EDGE, :]
+        second[...] = high[16 * ROWS - EDGE :, :]
+
 
 def parity(i, shape, shift):
     return ((iota(shape, 1) + i + shift) & 1) == 0
@@ -121,12 +133,13 @@
     vR, bE, bO, pair_r, pair_b, tmp = refs[len(PACKED) + 3 :]
     lv = dict(outs, vR=vR)
     slab, box, boxes = place[0], place[1], place[2]
+    odd = box & 1
 
     def source(t, i):
         if i < H0:
-            return halo.at[t, 0], i * ROWS + (EDGE - H0 * ROWS)
+            return halo.at[t, odd], i * ROWS + (EDGE - H0 * ROWS)
         if i >= H0 + 32:
-            return halo.at[t, 1], (i - H0 - 32) * ROWS
+            return halo.at[t, 1 - odd], (i - H0 - 32) * ROWS
         x = i - H0
         return (lo.at[t], x * ROWS) if x < 16 else (hi.at[t], (x - 16) * ROWS)
 
@@ -280,8 +293,8 @@
     return factor * (4.0 * v + fy + fz) + (ax[i] + ax[i - 1])
 
 
-def middle_kernel(place, own, halo, v1, f1, ax1, ay1, az1, inv1, ax2, ay2, az2, inv2, send, v2, f2, b2, b1, tmp):
-    box, boxes = place[1], place[2]
+def middle_kernel(place, own, halo, bottom, v1, f1, ax1, ay1, az1, inv1, ax2, ay2, az2, inv2, send, message, v2, f2, b2, b1, tmp):
+    slab, box, boxes = place[0], place[1], place[2]
     w = H1 + 1
     b1[0:w] = halo[0, H1 : H1 + w]
     b1[w : w + 16] = own[16:32]
@@ -333,25 +346,17 @@
     send[0:8] = v2[8:16]
     send[8:16] = f2[8:16]
 
-
-def source_kernel(place, v2, f2, b2, ax2, ay2, az2, bottom, rows):
-    two, k2 = (f2, ax2, ay2, az2), 0.5 * 0.25**2
     pairs = []
     for k in range(4):
         parts = [
-            residual_plain(v2, *two, center_plain(b2, ax2, i, k2, 4, 64), i)
+            residual_plain(v2, *two[:4], center_plain(b2, ax2, i, k2, 4, 64), i)
             for i in (8 + 2 * k, 9 + 2 * k)
         ]
         pairs.append(parts[0] + parts[1])
-    source = bottom_row(pairs, place[0])
-    rows[...] = jnp.where((iota((8, 128), 0) & 1) == 0, source, bottom[...])
-
-
-def spread_kernel(rows, beside, message):
-    del beside
-    value = rows[...]
+    source = bottom_row(pairs, slab)
+    rows = jnp.where((iota((8, 128), 0) & 1) == 0, source, bottom[...])
     for k in range(message.shape[0] // 8):
-        message[8 * k : 8 * k + 8, :] = value
+        message[8 * k : 8 * k + 8, :] = rows
 
 
 def coarse_solve(n, source, coefficient, dref, qref, eref):
@@ -505,9 +510,9 @@
 def pack(*args):
     return pl.pallas_call(
         pack_kernel,
-        out_shape=[jax.ShapeDtypeStruct((16 * ROWS, 256), F32)] * 2,
-        in_specs=[pl.BlockSpec(memory_space=pltpu.HBM)] * 3,
-        out_specs=[pl.BlockSpec(memory_space=pltpu.VMEM)] * 2,
+        out_shape=[jax.ShapeDtypeStruct((rows, 256), F32) for rows in (16 * ROWS, 16 * ROWS, EDGE, EDGE)],
+        in_specs=[pl.BlockSpec(memory_space=pltpu.SMEM)] + [pl.BlockSpec(memory_space=pl.ANY)] * 3,
+        out_specs=[pl.BlockSpec(memory_space=pltpu.VMEM)] * 4,
         scratch_shapes=[pltpu.VMEM((512, 128), F32)] * 3 + [pltpu.SemaphoreType.DMA((3,))],
         compiler_params=pltpu.CompilerParams(vmem_limit_bytes=4 * 1024 * 1024),
     )(*args)
@@ -525,16 +530,16 @@
     boxes = lax.axis_size("box")
     slab, box = lax.axis_index("slab"), lax.axis_index("box")
     place = jnp.stack([slab, box, jnp.int32(boxes), jnp.int32(0)]).astype(jnp.int32)
-    rightward = [(i, i + 1) for i in range(boxes - 1)]
-    leftward = [(i + 1, i) for i in range(boxes - 1)]
     both = [(2 * i, 2 * i + 2) for i in range(boxes - 1)] + [(2 * i + 3, 2 * i + 1) for i in range(boxes - 1)]
 
     flat = [by_tiles(a) for a in (pressure_guess, right_side, coefficient)]
-    low, high = pack(*flat)
-    from_left = lax.ppermute(high[16 * ROWS - EDGE :], "box", rightward)
-    from_right = lax.ppermute(low[:EDGE], "box", leftward)
+    low, high, first, second = pack(place, *flat)
+    odd_pairs = [(i, i + 1) for i in range(1, boxes - 1, 2)]
+    even_pairs = [(i, i + 1) for i in range(0, boxes - 1, 2)]
+    first = lax.ppermute(first, "box", odd_pairs + [(j, i) for i, j in odd_pairs])
+    second = lax.ppermute(second, "box", even_pairs + [(j, i) for i, j in even_pairs])
     low, high = lax.all_gather(low, "slab"), lax.all_gather(high, "slab")
-    halo = lax.all_gather(jnp.stack([from_left, from_right]), "slab")
+    halo = lax.all_gather(jnp.stack([first, second]), "slab")
 
     plane = (N0, 8, 256)
     fine = call(
@@ -552,18 +557,17 @@
     halo = lax.all_gather(lax.ppermute(send, ("box", "slab"), both), "slab")
 
     one, two = (N1, 8, 128), (N2, 8, 128)
-    *levels, send, v2, f2, b2 = call(
+    *levels, send, message = call(
         middle_kernel,
-        [one] * 6 + [two] * 4 + [(16, 8, 128)] + [two] * 3,
-        [one, (128, 128)],
+        [one] * 6 + [two] * 4 + [(16, 8, 128), (2 * boxes, 128)],
+        [two] * 3 + [one, (128, 128)],
         place,
         own,
         halo,
+        bottom,
         scalars=1,
     )
     beside = lax.ppermute(send, ("box", "slab"), both)
-    (rows,) = call(source_kernel, [(8, 128)], [], place, v2, f2, b2, *levels[6:9], bottom, scalars=1)
-    (message,) = call(spread_kernel, [(2 * boxes, 128)], [], rows, beside)
     spread = lax.all_to_all(message.reshape(boxes, 2, 128), "box", 0, 0)
     both_parts = jnp.concatenate([spread.reshape(2 * boxes, 128), beside.reshape(128, 128)], axis=0)
     gathered = lax.all_gather(both_parts, "slab")

time: 95.7 us -> 104 us (1.087)
  blocking collectives: 53.9 us -> 13.8 us
  starting transfers between devices: 7.83 us -> 30.3 us
  local copies, waits for them, and re-layouts: 2.87 us -> 21.8 us
  waiting for transfers between devices: 8.75 us -> 14.2 us
    all_to_all x1 -> x0, blocking collectives: 40.6 us -> none  [body(): spread = lax.all_to_all(message.reshape(boxes, 2, 128), 'box', 0, 0)]
    all_to_all x0 -> x1, starting transfers between devices: none -> 22.5 us  [body(): spread = lax.all_to_all(message.reshape(boxes, 2, 128), 'box', 0, 0)]
    unnamed x6 -> x64, local copies, waits for them, and re-layouts: 2.84 us -> 21.8 us
    all_to_all x0 -> x1, waiting for transfers between devices: none -> 5.19 us  [body(): spread = lax.all_to_all(message.reshape(boxes, 2, 128), 'box', 0, 0)]
    all_gather x1, blocking collectives: 2.09 us -> 3.68 us  [body(): gathered = lax.all_gather(both_parts, 'slab')]
    all_gather x1, blocking collectives: 3.84 us -> 2.34 us  [body(): halo = lax.all_gather(jnp.stack([first, second]), 'slab')]
    pallas_call x5 -> x3, Pallas kernels: 20.6 us -> 19.9 us  [call(): pl.pallas_call(kernel, out_shape=[jax.ShapeDtypeStruct(s, F32) for s in o...]
  transfers between devices with their start and end apart: 4 -> 5, of which waited for: 3 -> 3; matrix products, arithmetic and copies ran while one was open for 0% -> 0% of each run, Pallas kernels for 1% -> 0%
where the time goes in v3:
time: 104 us; the launch traced here: 103 us
  starting transfers between devices  30.3 us (29%)
  local copies, waits for them, and re-layouts  21.8 us (21%)
  Pallas kernels  21 us (20%)
  waiting for transfers between devices  14.2 us (14%)
  blocking collectives  13.8 us (13%)
  other arithmetic  1.12 us (1%)
    all_to_all x1, starting transfers between devices, body(): spread = lax.all_to_all(message.reshape(boxes, 2, 128), 'box', 0, 0)  22.5 us
    unnamed x64, local copies, waits for them, and re-layouts  21.8 us
    pallas_call x3, Pallas kernels, call(): pl.pallas_call(kernel, out_shape=[jax.ShapeDtypeStruct(s, F32) for s in o...  19.9 us
    all_gather x2, blocking collectives, body(): low, high = (lax.all_gather(low, 'slab'), lax.all_gather(high, 'slab'))  5.39 us
    all_to_all x1, waiting for transfers between devices, body(): spread = lax.all_to_all(message.reshape(boxes, 2, 128), 'box', 0, 0)  5.19 us
    ppermute x1, starting transfers between devices, body(): lax.ppermute(second, 'box', even_pairs + [(j, i) for i, j in even_pairs])  4.57 us
    ppermute x1, waiting for transfers between devices, body(): beside = lax.ppermute(send, ('box', 'slab'), both)  4.57 us
    ppermute x1, waiting for transfers between devices, body(): halo = lax.all_gather(lax.ppermute(send, ('box', 'slab'), both), 'slab')  4.46 us
  transfers between devices with their start and end apart: 5, of which 3 were waited for; matrix products, arithmetic and copies ran while one was open for 0% of the time, Pallas kernels for 0%

profile of v3, /device:TPU:1, one launch (start us, length us, event | category | flops | bytes accessed | tf_op | source)
XLA Modules:
  0.0 103.1 jit_solution(15027064726186306531)
XLA Ops:
  0.7 0.9 copy-done.10
  1.7 0.9 copy-done.11
  2.6 0.9 copy-done.12
  3.6 1.2 %shard_map.50 = (f32[320,256]{1,0:T(8,128)S(1)}, f32[320,256]{1,0:T(8,128)S(1)}, f32[184,256]{1,0:T(8,128)S(1)}, f32[184,256]{1,0:T(8,128)S(1)}) custom-call(s32[4]{0:T(128)S(1)} %pad_add_fusion.place, f32[512,128]{1,0:T(8,128)S(1)} %bitcast.42, f32[512,128]{1,0:T(8,128)S(1)} %bitcast.43, f32[512,128]{1,0:T(8,128)S(1)} %bitcast.44), custom_call_target="tpu_custom_call" | custom-call | tf_op jit(solution)/shard_map/pallas_call | solution.py:511
  5.4 4.6 %collective-permute-start.1 = (f32[184,256]{1,0:T(8,128)S(1)}, f32[184,256]{1,0:T(8,128)S(1)}, u32[]{:S(2)}, u32[]{:S(2)}) collective-permute-start(f32[184,256]{1,0:T(8,128)S(1)} %get-tuple-element.39), channel_id=1, source_target_pairs={{0,2},{4,6},{8,10},{12,14},{16,18},{20,22},{24,26},{28,30},{32,34}... | collective-permute-start | bytes 565256 | tf_op jit(solution)/shard_map/ppermute | solution.py:540
  10.0 3.1 %all-gather = f32[640,256]{1,0:T(8,128)S(1)} all-gather(f32[320,256]{1,0:T(8,128)S(1)} %get-tuple-element.36), channel_id=2, replica_groups=mesh['box'=128,'slab'=2] {'slab'}, dimensions={0}, use_global_device_ids=true | all-gather | bytes 983040 | tf_op jit(solution)/shard_map/all_gather | solution.py:541
  13.1 2.3 %all-gather.1 = f32[640,256]{1,0:T(8,128)S(1)} all-gather(f32[320,256]{1,0:T(8,128)S(1)} %get-tuple-element.37), channel_id=3, replica_groups=mesh['box'=128,'slab'=2] {'slab'}, dimensions={0}, use_global_device_ids=true | all-gather | bytes 983040 | tf_op jit(solution)/shard_map/all_gather | solution.py:541
  15.4 2.3 %all-gather.2 = f32[4,184,256]{2,1,0:T(8,128)S(1)} all-gather(f32[2,184,256]{2,1,0:T(8,128)S(1)} %pad_maximum_fusion), channel_id=4, replica_groups=mesh['box'=128,'slab'=2] {'slab'}, dimensions={0}, use_global_device_ids=true | all-gather | bytes 1130496 | tf_op jit(solution)/shard_map/all_gather | solution.py:542
  17.8 6.8 %shard_map.51 = (f32[50,8,256]{2,1,0:T(8,128)S(1)}, f32[50,8,256]{2,1,0:T(8,128)S(1)}, f32[50,8,256]{2,1,0:T(8,128)S(1)}, f32[50,8,256]{2,1,0:T(8,128)S(1)}, f32...) custom-call(s32[4]{0:T(128)S(1)} %pad_add_fusion.place, ...), custom_call_target="tpu_custom_call" | custom-call | tf_op jit(solution)/shard_map/pallas_call | solution.py:500
  25.3 0.8 copy-done.6
  26.8 1.3 %collective-permute-start.2 = (f32[33,8,128]{2,1,0:T(8,128)S(1)}, f32[33,8,128]{2,1,0:T(8,128)S(1)}, u32[]{:S(2)}, u32[]{:S(2)}) collective-permute-start(f32[33,8,128]{2,1,0:T(8,128)S(1)} %get-tuple-element.41), channel_id=1, source_target_pairs={{0,2},{2,4},{4,6},{6,8},{8,10},{10,12},{12,14},{14,16},{16,18},{18... | collective-permute-start | bytes 405512 | tf_op jit(solution)/shard_map/ppermute | solution.py:557
  28.1 4.5 %collective-permute-done.2 = f32[33,8,128]{2,1,0:T(8,128)S(1)} collective-permute-done((f32[33,8,128]{2,1,0:T(8,128)S(1)}, f32[33,8,128]{2,1,0:T(8,128)S(1)}, u32[]{:S(2)}, u32[]{:S(2)}) %collective-permute-start.2) | collective-permute-done | bytes 135200 | tf_op jit(solution)/shard_map/ppermute | solution.py:557
  32.6 2.4 %all-gather.3 = f32[66,8,128]{2,1,0:T(8,128)S(1)} all-gather(f32[33,8,128]{2,1,0:T(8,128)S(1)} %collective-permute-done.2), channel_id=5, replica_groups=mesh['box'=128,'slab'=2] {'slab'}, dimensions={0}, use_global_device_ids=true | all-gather | bytes 405504 | tf_op jit(solution)/shard_map/all_gather | solution.py:557
  34.9 2.4 %shard_map.52 = (f32[42,8,128]{2,1,0:T(8,128)S(1)}, f32[42,8,128]{2,1,0:T(8,128)S(1)}, f32[42,8,128]{2,1,0:T(8,128)S(1)}, f32[42,8,128]{2,1,0:T(8,128)S(1)}, f32...) custom-call(s32[4]{0:T(128)S(1)} %pad_add_fusion.place, ...), custom_call_target="tpu_custom_call" | custom-call | tf_op jit(solution)/shard_map/pallas_call | solution.py:500
  43.9 22.5 %all-to-all-start = ((f32[128,2,128]{2,1,0:T(2,128)}), f32[128,2,128]{2,1,0:T(2,128)}, u32[]{:S(2)}, u32[]{:S(2)}) async-start(f32[128,2,128]{2,1,0:T(2,128)} %bitcast.45), calls=%async_computation | async-start | bytes 262144 | tf_op jit(solution)/shard_map/all_to_all | solution.py:571
  66.4 1.3 %collective-permute-start.3 = (f32[16,8,128]{2,1,0:T(8,128)}, f32[16,8,128]{2,1,0:T(8,128)}, u32[]{:S(2)}, u32[]{:S(2)}) collective-permute-start(f32[16,8,128]{2,1,0:T(8,128)} %copy-done.30), channel_id=1, source_target_pairs={{0,2},{2,4},{4,6},{6,8},{8,10},{10,12},{12,14},{14,16},{16,18},{18... | collective-permute-start | bytes 196616 | tf_op jit(solution)/shard_map/ppermute | solution.py:570
  67.7 4.6 %collective-permute-done.3 = f32[16,8,128]{2,1,0:T(8,128)} collective-permute-done((f32[16,8,128]{2,1,0:T(8,128)}, f32[16,8,128]{2,1,0:T(8,128)}, u32[]{:S(2)}, u32[]{:S(2)}) %collective-permute-start.3) | collective-permute-done | bytes 65568 | tf_op jit(solution)/shard_map/ppermute | solution.py:570
  72.2 5.2 %all-to-all-done = f32[128,2,128]{2,1,0:T(2,128)} async-done(((f32[128,2,128]{2,1,0:T(2,128)}), f32[128,2,128]{2,1,0:T(2,128)}, u32[]{:S(2)}, u32[]{:S(2)}) %all-to-all-start) | async-done | bytes 131104 | tf_op jit(solution)/shard_map/all_to_all | solution.py:571
  77.4 1.0 pad_maximum_fusion.1
  78.5 3.7 %all-gather.4 = f32[768,128]{1,0:T(8,128)S(1)} all-gather(f32[384,128]{1,0:T(8,128)S(1)} %pad_maximum_fusion.1), channel_id=6, replica_groups=mesh['box'=128,'slab'=2] {'slab'}, dimensions={0}, use_global_device_ids=true | all-gather | bytes 589824 | tf_op jit(solution)/shard_map/all_gather | solution.py:573
  82.2 1.0 copy-done.5
  83.2 1.0 copy-done.7
  84.2 1.0 copy-done.9
  85.2 0.9 copy-done.16
  86.1 0.9 copy-done.18
  87.0 0.9 copy-done.20
  87.9 0.9 copy-done.22
  88.8 0.9 copy-done.25
  89.7 0.9 copy-done.27
  90.6 0.9 copy-done.29
  91.5 0.8 copy-done.31
  92.4 10.7 %shard_map.53 = (f32[512,128]{1,0:T(8,128)}, f32[512,128]{1,0:T(8,128)}) custom-call(s32[4]{0:T(128)S(1)} %pad_add_fusion.place, f32[2,384,128]{2,1,0:T(8,128)S(1)} %bitcast.40, f32[16,8,128]{2,1,0:T(8,128)S(1)} %copy-done.31, f32[42,8,128]{2,1,0:T(8,128)S(1)} %get-tuple-element.45.refs_2_, f32[42,8,128]{2,1,0:T(8,128)S(1)} %copy-done.14, ...), custom_call_target="tpu_custom_call" | custom-call | tf_op jit(solution)/shard_map/pallas_call | solution.py:500
  (54 shorter events, 8.8 us)
Async XLA Ops:
  0.7 1.0 copy-start.10
  1.7 0.9 copy-start.11
  2.6 0.9 copy-start.12
  4.7 10.6 %collective-permute-start = (f32[184,256]{1,0:T(8,128)S(1)}, f32[184,256]{1,0:T(8,128)S(1)}, u32[]{:S(2)}, u32[]{:S(2)}) collective-permute-start(f32[184,256]{1,0:T(8,128)S(1)} %get-tuple-element.38), channel_id=1, source_target_pairs={{2,4},{6,8},{10,12},{14,16},{18,20},{22,24},{26,28},{30,32},{34,36... | collective-permute-start | bytes 565256 | tf_op jit(solution)/shard_map/ppermute | solution.py:539
  5.4 10.0 %collective-permute-start.1 = (f32[184,256]{1,0:T(8,128)S(1)}, f32[184,256]{1,0:T(8,128)S(1)}, u32[]{:S(2)}, u32[]{:S(2)}) collective-permute-start(f32[184,256]{1,0:T(8,128)S(1)} %get-tuple-element.39), channel_id=1, source_target_pairs={{0,2},{4,6},{8,10},{12,14},{16,18},{20,22},{24,26},{28,30},{32,34}... | collective-permute-start | bytes 565256 | tf_op jit(solution)/shard_map/ppermute | solution.py:540
  24.6 0.8 copy-start.4
  25.3 0.8 copy-start.6
  26.1 0.7 copy-start.8
  26.8 10.5 %copy-start = (f32[50,8,256]{2,1,0:T(8,128)}, f32[50,8,256]{2,1,0:T(8,128)S(1)}, u32[]{:S(2)}) copy-start(f32[50,8,256]{2,1,0:T(8,128)S(1)} %get-tuple-element.63.refs_20_) | copy-start | bytes 1228804
  26.8 10.5 %copy-start.2 = (f32[50,8,256]{2,1,0:T(8,128)}, f32[50,8,256]{2,1,0:T(8,128)S(1)}, u32[]{:S(2)}) copy-start(f32[50,8,256]{2,1,0:T(8,128)S(1)} %get-tuple-element.64.refs_21_) | copy-start | bytes 1228804
  26.8 5.7 %collective-permute-start.2 = (f32[33,8,128]{2,1,0:T(8,128)S(1)}, f32[33,8,128]{2,1,0:T(8,128)S(1)}, u32[]{:S(2)}, u32[]{:S(2)}) collective-permute-start(f32[33,8,128]{2,1,0:T(8,128)S(1)} %get-tuple-element.41), channel_id=1, source_target_pairs={{0,2},{2,4},{4,6},{6,8},{8,10},{10,12},{12,14},{14,16},{16,18},{18... | collective-permute-start | bytes 405512 | tf_op jit(solution)/shard_map/ppermute | solution.py:557
  37.3 0.7 copy-start.13
  38.0 0.7 copy-start.15
  38.7 0.7 copy-start.17
  39.4 0.7 copy-start.19
  40.0 0.7 copy-start.21
  43.9 33.6 %all-to-all-start = ((f32[128,2,128]{2,1,0:T(2,128)}), f32[128,2,128]{2,1,0:T(2,128)}, u32[]{:S(2)}, u32[]{:S(2)}) async-start(f32[128,2,128]{2,1,0:T(2,128)} %bitcast.45), calls=%async_computation | async-start | bytes 262144 | tf_op jit(solution)/shard_map/all_to_all | solution.py:571
  66.4 5.9 %collective-permute-start.3 = (f32[16,8,128]{2,1,0:T(8,128)}, f32[16,8,128]{2,1,0:T(8,128)}, u32[]{:S(2)}, u32[]{:S(2)}) collective-permute-start(f32[16,8,128]{2,1,0:T(8,128)} %copy-done.30), channel_id=1, source_target_pairs={{0,2},{2,4},{4,6},{6,8},{8,10},{10,12},{12,14},{14,16},{16,18},{18... | collective-permute-start | bytes 196616 | tf_op jit(solution)/shard_map/ppermute | solution.py:570
  77.4 4.7 %copy-start.3 = (f32[50,8,256]{2,1,0:T(8,128)S(1)}, f32[50,8,256]{2,1,0:T(8,128)}, u32[]{:S(2)}) copy-start(f32[50,8,256]{2,1,0:T(8,128)} %copy-done.2) | copy-start | bytes 1228804
  78.5 3.7 %copy-start.1 = (f32[50,8,256]{2,1,0:T(8,128)S(1)}, f32[50,8,256]{2,1,0:T(8,128)}, u32[]{:S(2)}) copy-start(f32[50,8,256]{2,1,0:T(8,128)} %copy-done) | copy-start | bytes 1228804
  78.5 3.7 %copy-start.14 = (f32[42,8,128]{2,1,0:T(8,128)S(1)}, f32[42,8,128]{2,1,0:T(8,128)}, u32[]{:S(2)}) copy-start(f32[42,8,128]{2,1,0:T(8,128)} %copy-done.13) | copy-start | bytes 516100
  82.2 1.0 copy-start.5
  83.2 1.0 copy-start.7
  84.2 1.0 copy-start.9
  85.2 0.9 copy-start.16
  86.1 0.9 copy-start.18
  87.0 0.9 copy-start.20
  87.9 0.9 copy-start.22
  88.8 0.9 copy-start.25
  89.7 0.9 copy-start.27
  90.6 0.9 copy-start.29
  91.5 0.8 copy-start.31
  (5 other events, 3.2 us)

commit v4 on v3

--- a/solution.py
+++ b/solution.py
@@ -420,27 +420,11 @@
     lax.fori_loop(0, ITERS, iterate, total(source, source))
 
 
-def last_kernel(boxes, place, *refs):
-    names = ("all", "own2", "v1", "f1", "ax1", "ay1", "az1", "inv1", "ax2", "ay2", "az2", "inv2")
-    given = dict(zip(names, refs))
-    refs = refs[len(names) :]
-    level0 = dict(zip(PACKED, refs))
-    refs = refs[len(PACKED) :]
-    out_v, out_r, vR, vB, v1, v2, f2, dref, qref, eref, wide, e0 = refs
-    slab, box = place[0], place[1]
-    gathered = given["all"]
-
+def coarse_kernel(boxes, place, gathered, e2, dref, qref, eref):
+    box = place[1]
     source = [gathered[t, pl.ds(0, boxes, stride=2), :] for t in range(2)]
     coefficient = [gathered[t, pl.ds(1, boxes, stride=2), :] for t in range(2)]
     coarse_solve(boxes, source, coefficient, dref, qref, eref)
-
-    base = 2 * boxes
-    for side, at in ((0, 0), (1, 16)):
-        for k in range(8):
-            v2[at + k] = gathered[side, base + 8 * k : base + 8 * k + 8, :]
-            f2[at + k] = gathered[side, base + 64 + 8 * k : base + 64 + 8 * k + 8, :]
-    v2[8:16] = given["own2"][0:8]
-    f2[8:16] = given["own2"][8:16]
     near = [eref[t, pl.ds(7 + box, 8), :] for t in range(2)]
     spread = one_hot((128, 512), lambda i, j: jnp.logical_and(((j >> 7) * 32) + ((j & 127) >> 1) == i, (j & 127) < 64))
     fine = [matmul(e, spread) for e in near]
@@ -448,7 +432,30 @@
     for i in range(N2):
         cell, k = (i // 2) // 4, (i // 2) % 4
         low, high = (f[cell : cell + 1, 128 * k : 128 * k + 128] for f in fine)
-        v2[i] = v2[i] + jnp.where(row < 2, low, jnp.where(row < 4, high, 0.0))
+        e2[i] = jnp.where(row < 2, low, jnp.where(row < 4, high, 0.0))
+
+
+def after_kernel(send, gathered, out):
+    del gathered
+    out[...] = send[...]
+
+
+def last_kernel(place, *refs):
+    names = ("e2", "beside", "own2", "v1", "f1", "ax1", "ay1", "az1", "inv1", "ax2", "ay2", "az2", "inv2")
+    given = dict(zip(names, refs))
+    refs = refs[len(names) :]
+    level0 = dict(zip(PACKED, refs))
+    refs = refs[len(PACKED) :]
+    out_v, out_r, vR, vB, v1, v2, f2, wide, e0 = refs
+    slab = place[0]
+    e2, beside, own2 = given["e2"], given["beside"], given["own2"]
+
+    for ref, part in ((v2, 0), (f2, 8)):
+        ref[0:8] = beside[0, part : part + 8]
+        ref[8:16] = own2[part : part + 8]
+        ref[16:24] = beside[1, part : part + 8]
+    for i in range(N2):
+        v2[i] = v2[i] + e2[i]
     two = (f2, given["ax2"], given["ay2"], given["az2"], given["inv2"])
     for k in range(2):
         sweep_plain(v2, *two, 0, 0, 1 + 2 * k, N2 - 1 - 2 * k)
@@ -567,18 +574,26 @@
         bottom,
         scalars=1,
     )
-    beside = lax.ppermute(send, ("box", "slab"), both)
-    spread = lax.all_to_all(message.reshape(boxes, 2, 128), "box", 0, 0)
-    both_parts = jnp.concatenate([spread.reshape(2 * boxes, 128), beside.reshape(128, 128)], axis=0)
-    gathered = lax.all_gather(both_parts, "slab")
-
-    flat_out = [(512, 128)] * 2
-    pressure, residual = call(
-        functools.partial(last_kernel, boxes),
-        flat_out,
-        [plane, plane, one, two, two, (2, boxes, 128), (2, boxes, 128), (2, boxes + 16, 128), (128, 128), (22, 8, 256)],
+    spread = lax.all_to_all(message.reshape(boxes, 2, 128), "box", 0, 0).reshape(2 * boxes, 128)
+    (late,) = call(after_kernel, [(16, 8, 128)], [], send, spread)
+    beside = lax.ppermute(late, ("box", "slab"), both)
+    gathered = lax.all_gather(spread, "slab")
+    (e2,) = call(
+        functools.partial(coarse_kernel, boxes),
+        [two],
+        [(2, boxes, 128), (2, boxes, 128), (2, boxes + 16, 128)],
         place,
         gathered,
+        scalars=1,
+    )
+    beside = lax.all_gather(beside, "slab")
+    pressure, residual = call(
+        last_kernel,
+        [(512, 128)] * 2,
+        [plane, plane, one, two, two, (128, 128), (22, 8, 256)],
+        place,
+        e2,
+        beside,
         send,
         *levels,
         *level0,

time: 104 us -> 88 us (0.85)
  blocking collectives: 13.8 us -> 49.9 us
  starting transfers between devices: 30.3 us -> 7.82 us
  local copies, waits for them, and re-layouts: 21.8 us -> 2.85 us
  waiting for transfers between devices: 14.2 us -> 4.46 us
    all_to_all x0 -> x1, blocking collectives: none -> 33.2 us  [body(): lax.all_to_all(message.reshape(boxes, 2, 128), 'box', 0, 0)]
    all_to_all x1 -> x0, starting transfers between devices: 22.5 us -> none  [body(): spread = lax.all_to_all(message.reshape(boxes, 2, 128), 'box', 0, 0)]
    unnamed x64 -> x6, local copies, waits for them, and re-layouts: 21.8 us -> 2.85 us
    all_to_all x1 -> x0, waiting for transfers between devices: 5.19 us -> none  [body(): spread = lax.all_to_all(message.reshape(boxes, 2, 128), 'box', 0, 0)]
    ppermute x1, waiting for transfers between devices: 4.57 us -> 0.01 us  [body(): beside = lax.ppermute(late, ('box', 'slab'), both)]
    all_gather x1 -> x2, blocking collectives: 3.68 us -> 6.61 us  [the longest x1 4.7 us: body(): gathered = lax.all_gather(spread, 'slab')]
    pallas_call x3 -> x5, Pallas kernels: 19.9 us -> 20.7 us  [call(): pl.pallas_call(kernel, out_shape=[jax.ShapeDtypeStruct(s, F32) for s in o...]
  transfers between devices with their start and end apart: 5 -> 4, of which waited for: 3 -> 1; matrix products, arithmetic and copies ran while one was open for 0% -> 0% of each run, Pallas kernels for 0% -> 5%
where the time goes in v4:
time: 88 us; the launch traced here: 87.7 us
  blocking collectives  49.9 us (57%)
  Pallas kernels  21.8 us (25%)
  starting transfers between devices  7.82 us (9%)
  waiting for transfers between devices  4.46 us (5%)
  local copies, waits for them, and re-layouts  2.85 us (3%)
    all_to_all x1, blocking collectives, body(): lax.all_to_all(message.reshape(boxes, 2, 128), 'box', 0, 0)  33.2 us
    pallas_call x5, Pallas kernels, call(): pl.pallas_call(kernel, out_shape=[jax.ShapeDtypeStruct(s, F32) for s in o...  20.7 us
    all_gather x2, blocking collectives, body(): low, high = (lax.all_gather(low, 'slab'), lax.all_gather(high, 'slab'))  5.39 us
    all_gather x1, blocking collectives, body(): gathered = lax.all_gather(spread, 'slab')  4.7 us
    ppermute x1, starting transfers between devices, body(): lax.ppermute(second, 'box', even_pairs + [(j, i) for i, j in even_pairs])  4.57 us
    ppermute x1, waiting for transfers between devices, body(): halo = lax.all_gather(lax.ppermute(send, ('box', 'slab'), both), 'slab')  4.46 us
    unnamed x6, local copies, waits for them, and re-layouts  2.85 us
    all_gather x1, blocking collectives, body(): halo = lax.all_gather(lax.ppermute(send, ('box', 'slab'), both), 'slab')  2.35 us
  transfers between devices with their start and end apart: 4, of which 1 were waited for; matrix products, arithmetic and copies ran while one was open for 0% of the time, Pallas kernels for 5%

profile of v4, /device:TPU:1, one launch (start us, length us, event | category | flops | bytes accessed | tf_op | source)
XLA Modules:
  0.0 87.7 jit_solution(3825487671165312319)
XLA Ops:
  0.6 0.1 pad_add_fusion.place
  0.7 0.0 copy-start
  0.7 0.9 %copy-done = f32[8,32,256]{2,1,0:T(8,128)S(1)} copy-done((f32[8,32,256]{2,1,0:T(8,128)S(1)}, f32[8,32,256]{2,1,0:T(8,128)}, u32[]{:S(2)}) %copy-start) | copy-done | bytes 262168
  1.7 0.0 copy-start.1
  1.7 0.9 %copy-done.1 = f32[8,32,256]{2,1,0:T(8,128)S(1)} copy-done((f32[8,32,256]{2,1,0:T(8,128)S(1)}, f32[8,32,256]{2,1,0:T(8,128)}, u32[]{:S(2)}) %copy-start.1) | copy-done | bytes 262168
  2.6 0.0 copy-start.2
  2.6 0.9 %copy-done.2 = f32[8,32,256]{2,1,0:T(8,128)S(1)} copy-done((f32[8,32,256]{2,1,0:T(8,128)S(1)}, f32[8,32,256]{2,1,0:T(8,128)}, u32[]{:S(2)}) %copy-start.2) | copy-done | bytes 262168
  3.6 1.2 %shard_map.50 = (f32[320,256]{1,0:T(8,128)S(1)}, f32[320,256]{1,0:T(8,128)S(1)}, f32[184,256]{1,0:T(8,128)S(1)}, f32[184,256]{1,0:T(8,128)S(1)}) custom-call(s32[4]{0:T(128)S(1)} %pad_add_fusion.place, f32[512,128]{1,0:T(8,128)S(1)} %bitcast.44, f32[512,128]{1,0:T(8,128)S(1)} %bitcast.45, f32[512,128]{1,0:T(8,128)S(1)} %bitcast.46), custom_call_target="tpu_custom_call" | custom-call | tf_op jit(solution)/shard_map/pallas_call | solution.py:518
  4.7 0.7 collective-permute-start
  5.4 4.6 %collective-permute-start.1 = (f32[184,256]{1,0:T(8,128)S(1)}, f32[184,256]{1,0:T(8,128)S(1)}, u32[]{:S(2)}, u32[]{:S(2)}) collective-permute-start(f32[184,256]{1,0:T(8,128)S(1)} %get-tuple-element.39), channel_id=1, source_target_pairs={{0,2},{4,6},{8,10},{12,14},{16,18},{20,22},{24,26},{28,30},{32,34}... | collective-permute-start | bytes 565256 | tf_op jit(solution)/shard_map/ppermute | solution.py:547
  10.0 3.1 %all-gather = f32[640,256]{1,0:T(8,128)S(1)} all-gather(f32[320,256]{1,0:T(8,128)S(1)} %get-tuple-element.36), channel_id=2, replica_groups=mesh['box'=128,'slab'=2] {'slab'}, dimensions={0}, use_global_device_ids=true | all-gather | bytes 983040 | tf_op jit(solution)/shard_map/all_gather | solution.py:548
  13.1 2.3 %all-gather.1 = f32[640,256]{1,0:T(8,128)S(1)} all-gather(f32[320,256]{1,0:T(8,128)S(1)} %get-tuple-element.37), channel_id=3, replica_groups=mesh['box'=128,'slab'=2] {'slab'}, dimensions={0}, use_global_device_ids=true | all-gather | bytes 983040 | tf_op jit(solution)/shard_map/all_gather | solution.py:548
  15.4 0.0 collective-permute-done
  15.4 0.0 collective-permute-done.1
  15.4 2.3 %all-gather.2 = f32[4,184,256]{2,1,0:T(8,128)S(1)} all-gather(f32[2,184,256]{2,1,0:T(8,128)S(1)} %pad_maximum_fusion), channel_id=4, replica_groups=mesh['box'=128,'slab'=2] {'slab'}, dimensions={0}, use_global_device_ids=true | all-gather | bytes 1130496 | tf_op jit(solution)/shard_map/all_gather | solution.py:549
  17.8 6.9 %shard_map.51 = (f32[50,8,256]{2,1,0:T(8,128)S(1)}, f32[50,8,256]{2,1,0:T(8,128)S(1)}, f32[50,8,256]{2,1,0:T(8,128)S(1)}, f32[50,8,256]{2,1,0:T(8,128)S(1)}, f32...) custom-call(s32[4]{0:T(128)S(1)} %pad_add_fusion.place, ...), custom_call_target="tpu_custom_call" | custom-call | tf_op jit(solution)/shard_map/pallas_call | solution.py:507
  24.7 1.3 %collective-permute-start.2 = (f32[33,8,128]{2,1,0:T(8,128)S(1)}, f32[33,8,128]{2,1,0:T(8,128)S(1)}, u32[]{:S(2)}, u32[]{:S(2)}) collective-permute-start(f32[33,8,128]{2,1,0:T(8,128)S(1)} %get-tuple-element.41), channel_id=1, source_target_pairs={{0,2},{2,4},{4,6},{6,8},{8,10},{10,12},{12,14},{14,16},{16,18},{18... | collective-permute-start | bytes 405512 | tf_op jit(solution)/shard_map/ppermute | solution.py:564
  26.0 4.5 %collective-permute-done.2 = f32[33,8,128]{2,1,0:T(8,128)S(1)} collective-permute-done((f32[33,8,128]{2,1,0:T(8,128)S(1)}, f32[33,8,128]{2,1,0:T(8,128)S(1)}, u32[]{:S(2)}, u32[]{:S(2)}) %collective-permute-start.2) | collective-permute-done | bytes 135200 | tf_op jit(solution)/shard_map/ppermute | solution.py:564
  30.4 2.3 %all-gather.3 = f32[66,8,128]{2,1,0:T(8,128)S(1)} all-gather(f32[33,8,128]{2,1,0:T(8,128)S(1)} %collective-permute-done.2), channel_id=5, replica_groups=mesh['box'=128,'slab'=2] {'slab'}, dimensions={0}, use_global_device_ids=true | all-gather | bytes 405504 | tf_op jit(solution)/shard_map/all_gather | solution.py:564
  32.8 2.4 %shard_map.52 = (f32[42,8,128]{2,1,0:T(8,128)S(1)}, f32[42,8,128]{2,1,0:T(8,128)S(1)}, f32[42,8,128]{2,1,0:T(8,128)S(1)}, f32[42,8,128]{2,1,0:T(8,128)S(1)}, f32...) custom-call(s32[4]{0:T(128)S(1)} %pad_add_fusion.place, ...), custom_call_target="tpu_custom_call" | custom-call | tf_op jit(solution)/shard_map/pallas_call | solution.py:507
  35.2 33.2 %all_to_all.5 = f32[128,2,128]{2,1,0:T(2,128)S(1)} all-to-all(f32[128,2,128]{2,1,0:T(2,128)S(1)} %bitcast.47), channel_id=1, replica_groups=mesh['box'=128,'slab'=2] {'box'}, dimensions={0} | all-to-all | bytes 262144 | tf_op jit(solution)/shard_map/all_to_all | solution.py:577
  68.4 1.3 %collective-permute-start.3 = (f32[16,8,128]{2,1,0:T(8,128)S(1)}, f32[16,8,128]{2,1,0:T(8,128)S(1)}, u32[]{:S(2)}, u32[]{:S(2)}) collective-permute-start(f32[16,8,128]{2,1,0:T(8,128)S(1)} %shard_map.54), channel_id=1, source_target_pairs={{0,2},{2,4},{4,6},{6,8},{8,10},{10,12},{12,14},{14,16},{16,18},{18... | collective-permute-start | bytes 196616 | tf_op jit(solution)/shard_map/ppermute | solution.py:579
  69.7 4.7 %all_gather.41.gathered = f32[2,256,128]{2,1,0:T(8,128)S(1)} all-gather(f32[1,256,128]{2,1,0:T(8,128)S(1)} %bitcast.41), channel_id=1, replica_groups=mesh['box'=128,'slab'=2] {'slab'}, dimensions={0}, use_global_device_ids=true | all-gather | bytes 393216 | tf_op jit(solution)/shard_map/all_gather | solution.py:580
  74.4 4.5 %shard_map.53.refs_0_ = f32[24,8,128]{2,1,0:T(8,128)S(1)} custom-call(s32[4]{0:T(128)S(1)} %pad_add_fusion.place, f32[2,256,128]{2,1,0:T(8,128)S(1)} %all_gather.41.gathered), custom_call_target="tpu_custom_call" | custom-call | tf_op jit(solution)/shard_map/pallas_call | solution.py:507
  79.0 0.0 collective-permute-done.3
  79.0 1.9 %all-gather.4 = f32[32,8,128]{2,1,0:T(8,128)S(1)} all-gather(f32[16,8,128]{2,1,0:T(8,128)S(1)} %collective-permute-done.3), channel_id=6, replica_groups=mesh['box'=128,'slab'=2] {'slab'}, dimensions={0}, use_global_device_ids=true | all-gather | bytes 196608 | tf_op jit(solution)/shard_map/all_gather | solution.py:589
  80.9 6.8 %shard_map.55 = (f32[512,128]{1,0:T(8,128)}, f32[512,128]{1,0:T(8,128)}) custom-call(s32[4]{0:T(128)S(1)} %pad_add_fusion.place, f32[24,8,128]{2,1,0:T(8,128)S(1)} %shard_map.53.refs_0_, f32[2,16,8,128]{3,2,1,0:T(8,128)S(1)} %bitcast.43, f32[16,8,128]{2,1,0:T(8,128)S(1)} %get-tuple-element.44.send.refs_2_, f32[42,8,128]{2,1,0:T(8,128)S(1)} %get-tuple-element.45.refs_3_, ...), custom_call_target="tpu_custom_call" | custom-call | tf_op jit(solution)/shard_map/pallas_call | solution.py:507
  (2 shorter events, 0.0 us)
Async XLA Ops:
  0.7 1.0 %copy-start = (f32[8,32,256]{2,1,0:T(8,128)S(1)}, f32[8,32,256]{2,1,0:T(8,128)}, u32[]{:S(2)}) copy-start(f32[8,32,256]{2,1,0:T(8,128)} %param.3) | copy-start | bytes 786436
  1.7 0.9 %copy-start.1 = (f32[8,32,256]{2,1,0:T(8,128)S(1)}, f32[8,32,256]{2,1,0:T(8,128)}, u32[]{:S(2)}) copy-start(f32[8,32,256]{2,1,0:T(8,128)} %param.4) | copy-start | bytes 786436
  2.6 0.9 %copy-start.2 = (f32[8,32,256]{2,1,0:T(8,128)S(1)}, f32[8,32,256]{2,1,0:T(8,128)}, u32[]{:S(2)}) copy-start(f32[8,32,256]{2,1,0:T(8,128)} %param.5) | copy-start | bytes 786436
  4.7 10.6 %collective-permute-start = (f32[184,256]{1,0:T(8,128)S(1)}, f32[184,256]{1,0:T(8,128)S(1)}, u32[]{:S(2)}, u32[]{:S(2)}) collective-permute-start(f32[184,256]{1,0:T(8,128)S(1)} %get-tuple-element.38), channel_id=1, source_target_pairs={{2,4},{6,8},{10,12},{14,16},{18,20},{22,24},{26,28},{30,32},{34,36... | collective-permute-start | bytes 565256 | tf_op jit(solution)/shard_map/ppermute | solution.py:546
  5.4 10.0 %collective-permute-start.1 = (f32[184,256]{1,0:T(8,128)S(1)}, f32[184,256]{1,0:T(8,128)S(1)}, u32[]{:S(2)}, u32[]{:S(2)}) collective-permute-start(f32[184,256]{1,0:T(8,128)S(1)} %get-tuple-element.39), channel_id=1, source_target_pairs={{0,2},{4,6},{8,10},{12,14},{16,18},{20,22},{24,26},{28,30},{32,34}... | collective-permute-start | bytes 565256 | tf_op jit(solution)/shard_map/ppermute | solution.py:547
  24.7 5.8 %collective-permute-start.2 = (f32[33,8,128]{2,1,0:T(8,128)S(1)}, f32[33,8,128]{2,1,0:T(8,128)S(1)}, u32[]{:S(2)}, u32[]{:S(2)}) collective-permute-start(f32[33,8,128]{2,1,0:T(8,128)S(1)} %get-tuple-element.41), channel_id=1, source_target_pairs={{0,2},{2,4},{4,6},{6,8},{8,10},{10,12},{12,14},{14,16},{16,18},{18... | collective-permute-start | bytes 405512 | tf_op jit(solution)/shard_map/ppermute | solution.py:564
  68.4 10.5 %collective-permute-start.3 = (f32[16,8,128]{2,1,0:T(8,128)S(1)}, f32[16,8,128]{2,1,0:T(8,128)S(1)}, u32[]{:S(2)}, u32[]{:S(2)}) collective-permute-start(f32[16,8,128]{2,1,0:T(8,128)S(1)} %shard_map.54), channel_id=1, source_target_pairs={{0,2},{2,4},{4,6},{6,8},{8,10},{10,12},{12,14},{14,16},{16,18},{18... | collective-permute-start | bytes 196616 | tf_op jit(solution)/shard_map/ppermute | solution.py:579

commit v5 on v4

--- a/solution.py
+++ b/solution.py
@@ -11,13 +11,14 @@
 F32 = jnp.float32
 BF16 = jnp.bfloat16
 
-H0 = 9
+H0 = 5
 H1 = 12
 N0 = 32 + 2 * H0
 N1 = 16 + 2 * (H1 + 1)
 N2 = 24
-ROWS = 20
-EDGE = 184
+ROWS = 24
+EDGE = H0 * ROWS
+SWEEP, FACES, RESTRICT, MERGE, FINISH = 10, 5, 4, 8, 99
 SEND1 = H1 + (H1 + 1) + 8
 
 
@@ -48,46 +49,83 @@
     return pltpu.roll(v, 1, axis)
 
 
+def planes(first, last, unroll, step, carry=0):
+    def pair(k, carry):
+        i = first + 2 * k
+        return step(i + 1, (first + 1) % 2, step(i, first % 2, carry))
+
+    count = (last - first) // 2
+    if unroll < count:
+        return lax.fori_loop(0, count, pair, carry, unroll=unroll)
+    for k in range(count):
+        carry = pair(k, carry)
+    return carry
+
+
+def my_place():
+    return lax.axis_index("slab"), lax.axis_index("box")
+
+
 def slab_rows(x, half, odd):
     return pl.ds((x // 8) * 16 + half * 8 + x % 8 + 64 * odd, 4, stride=128)
 
 
-def pack_kernel(place, g_hbm, r_hbm, c_hbm, low, high, first, second, g, r, c, sem):
-    copies = [pltpu.make_async_copy(a, b, sem.at[k]) for k, (a, b) in enumerate(((g_hbm, g), (r_hbm, r), (c_hbm, c)))]
+def pack_plane(g, r, c, x, rows, even_y, out, base):
+    p0 = even_y if x % 2 == 0 else jnp.logical_not(even_y)
+    for half in range(2):
+        lanes = slice(128 * half, 128 * half + 128)
+        even, odd = rows(half, 0), rows(half, 1)
+        out[base : base + 4, lanes] = c[even, :]
+        out[base + 4 : base + 8, lanes] = c[odd, :]
+        fe, fo = r[even, :], r[odd, :]
+        out[base + 8 : base + 12, lanes] = jnp.where(p0, fe, fo)
+        out[base + 12 : base + 16, lanes] = jnp.where(p0, fo, fe)
+        out[base + 16 : base + 20, lanes] = jnp.where(p0, g[odd, :], g[even, :])
+        out[base + 20 : base + 24, lanes] = jnp.zeros((4, 128), F32)
+
+
+def pack_kernel(g, r, c, low, high):
+    even_y = (iota((4, 128), 1) & 1) == 0
+    for x in range(32):
+        out, base = (low, x * ROWS) if x < 16 else (high, (x - 16) * ROWS)
+        pack_plane(g, r, c, x, functools.partial(slab_rows, x), even_y, out, base)
+
+
+def edge_kernel(g_hbm, r_hbm, c_hbm, first, second, *scratch):
+    left, right, sem = scratch[0:3], scratch[3:6], scratch[6]
+    copies = []
+    for k, source in enumerate((g_hbm, r_hbm, c_hbm)):
+        for side, (target, at) in enumerate(((left[k], 0), (right[k], 48))):
+            copies.append(
+                pltpu.make_async_copy(source.at[:, at : at + 16, :], target.reshape(8, 16, 128), sem.at[2 * k + side])
+            )
     for copy in copies:
         copy.start()
     for copy in copies:
         copy.wait()
     even_y = (iota((4, 128), 1) & 1) == 0
-    odd_y = jnp.logical_not(even_y)
-    for x in range(32):
-        out, base = (low, x * ROWS) if x < 16 else (high, (x - 16) * ROWS)
-        p0 = even_y if x % 2 == 0 else odd_y
-        for half in range(2):
-            lanes = slice(128 * half, 128 * half + 128)
-            even, odd = slab_rows(x, half, 0), slab_rows(x, half, 1)
-            out[base : base + 4, lanes] = c[even, :]
-            out[base + 4 : base + 8, lanes] = c[odd, :]
-            fe, fo = r[even, :], r[odd, :]
-            out[base + 8 : base + 12, lanes] = jnp.where(p0, fe, fo)
-            out[base + 12 : base + 16, lanes] = jnp.where(p0, fo, fe)
-            out[base + 16 : base + 20, lanes] = jnp.where(p0, g[odd, :], g[even, :])
-
-    right_first = (place[1] & 1) == 1
+
+    def pack(parts, start, out):
+        for k in range(H0):
+            x = start + k
+            rows = lambda half, odd, x=x: pl.ds(half * 8 + x % 8 + 16 * odd, 4, stride=32)
+            pack_plane(*parts, x, rows, even_y, out, k * ROWS)
+
+    right_first = (my_place()[1] & 1) == 1
 
     @pl.when(right_first)
     def _():
-        first[...] = high[16 * ROWS - EDGE :, :]
-        second[...] = low[:EDGE, :]
+        pack(right, 32 - H0, first)
+        pack(left, 0, second)
 
     @pl.when(jnp.logical_not(right_first))
     def _():
-        first[...] = low[:EDGE, :]
-        second[...] = high[16 * ROWS - EDGE :, :]
-
-
-def parity(i, shape, shift):
-    return ((iota(shape, 1) + i + shift) & 1) == 0
+        pack(left, 0, first)
+        pack(right, 32 - H0, second)
+
+
+def parity(odd):
+    return ((iota((8, 256), 1) + odd + 1) & 1) == 0
 
 
 def nsum_packed(lv, v, xa, xb, ya, yb, i, p):
@@ -100,8 +138,8 @@
 
 
 def sweep_packed(lv, red, first, last):
-    def body(i, carry):
-        p = parity(i, (8, 256), 1)
+    def step(i, odd, carry):
+        p = parity(odd)
         if red:
             n = nsum_packed(lv, lv["vB"], lv["xR"], lv["xB"], lv["yR"], lv["yB"], i, p)
             lv["vR"][i] = (lv["fR"][i] + n) * lv["iR"][i]
@@ -111,11 +149,11 @@
             lv["vB"][i] = (lv["fB"][i] + n) * lv["iB"][i]
         return carry
 
-    lax.fori_loop(first, last, body, 0, unroll=6)
-
-
-def residual_packed(lv, i):
-    p = parity(i, (8, 256), 1)
+    planes(first, last, SWEEP, step)
+
+
+def residual_packed(lv, i, odd):
+    p = parity(odd)
     n = nsum_packed(lv, lv["vB"], lv["xR"], lv["xB"], lv["yR"], lv["yB"], i, p)
     r_red = lv["fR"][i] - (lv["cR"][i] * lv["vR"][i] - n)
     q = jnp.logical_not(p)
@@ -127,38 +165,47 @@
 PACKED = ("vB", "fR", "fB", "xR", "xB", "yR", "yB", "s", "c", "iR", "iB", "cR", "cB")
 
 
-def fine_kernel(place, lo, hi, halo, *refs):
+def fine_kernel(boxes, lo, hi, halo, *refs):
     outs = dict(zip(PACKED, refs))
     own, send, bottom = refs[len(PACKED) : len(PACKED) + 3]
     vR, bE, bO, pair_r, pair_b, tmp = refs[len(PACKED) + 3 :]
     lv = dict(outs, vR=vR)
-    slab, box, boxes = place[0], place[1], place[2]
+    slab, box = my_place()
     odd = box & 1
-
-    def source(t, i):
-        if i < H0:
-            return halo.at[t, odd], i * ROWS + (EDGE - H0 * ROWS)
-        if i >= H0 + 32:
-            return halo.at[t, 1 - odd], (i - H0 - 32) * ROWS
-        x = i - H0
-        return (lo.at[t], x * ROWS) if x < 16 else (hi.at[t], (x - 16) * ROWS)
-
-    for i in range(N0):
-        for t in range(2):
-            ref, base = source(t, i)
-            for k, out in enumerate((bE, bO, lv["fR"], lv["fB"], lv["vB"])):
-                out[i, 4 * t : 4 * t + 4, :] = ref[base + 4 * k : base + 4 * k + 4, :]
-
     row, lane = iota((8, 256), 0), iota((8, 256), 1)
+    low_half = row < 4
+
+    def merge(part0, part1, count, first):
+        def step(k, carry):
+            base = pl.multiple_of(k * ROWS, 8) if not isinstance(k, int) else k * ROWS
+            i = first + k
+            for at, (low, high) in enumerate(((bE, bO), (lv["fR"], lv["fB"]), (lv["vB"], None))):
+                a, b = part0[pl.ds(base + 8 * at, 8), :], part1[pl.ds(base + 8 * at, 8), :]
+                low[i] = jnp.where(low_half, a, pltpu.roll(b, 4, 0))
+                if high is not None:
+                    high[i] = jnp.where(low_half, pltpu.roll(a, 4, 0), b)
+            return carry
+
+        lax.fori_loop(0, count, step, 0, unroll=min(count, MERGE))
+
+    merge(halo.at[0, odd], halo.at[1, odd], H0, 0)
+    merge(lo.at[0], lo.at[1], 16, H0)
+    merge(hi.at[0], hi.at[1], 16, H0 + 16)
+    merge(halo.at[0, 1 - odd], halo.at[1, 1 - odd], H0, H0 + 32)
+
     top, bot = row == 7, row == 0
     end, begin = lane == 255, lane == 0
 
-    def faces(i, carry):
-        p = parity(i, (8, 256), 1)
-        e, o = bE[i], bO[i]
-        fxe, fxo = 0.5 * (e + bE[i + 1]), 0.5 * (o + bO[i + 1])
+    def x_faces(i, p):
+        fxe, fxo = 0.5 * (bE[i] + bE[i + 1]), 0.5 * (bO[i] + bO[i + 1])
         lv["xR"][i] = jnp.where(p, fxe, fxo)
         lv["xB"][i] = jnp.where(p, fxo, fxe)
+        return fxe, fxo
+
+    def faces(i, odd, before):
+        p = parity(odd)
+        e, o = bE[i], bO[i]
+        fxe, fxo = x_faces(i, p)
         fye = 0.5 * (e + jnp.where(end, 0.0, up(e, 1)))
         fyo = 0.5 * (o + jnp.where(end, 0.0, up(o, 1)))
         gye = 0.5 * (e + jnp.where(begin, 0.0, down(e, 1)))
@@ -171,39 +218,32 @@
         below = 0.5 * (e + jnp.where(bot, 0.0, down(o, 0)))
         lv["s"][i] = s
         lv["c"][i] = jnp.where(top, 0.0, above)
-        ze, zo = fye + gye + (s + below), fyo + gyo + (s + above)
-        lv["cR"][i] = jnp.where(p, ze, zo)
-        lv["cB"][i] = jnp.where(p, zo, ze)
-        return carry
-
-    lax.fori_loop(0, N0 - 1, faces, 0, unroll=7)
-
-    def inverses(i, carry):
+        ce = fye + gye + (s + below) + (fxe + before[0])
+        co = fyo + gyo + (s + above) + (fxo + before[1])
+        cr, cb = jnp.where(p, ce, co), jnp.where(p, co, ce)
+        lv["cR"][i] = cr
+        lv["cB"][i] = cb
         x = box * 32 - H0 + i
         inside = jnp.logical_and(x >= 0, x < boxes * 32)
-        cr = lv["cR"][i] + (lv["xR"][i] + lv["xB"][i - 1])
-        cb = lv["cB"][i] + (lv["xB"][i] + lv["xR"][i - 1])
-        lv["cR"][i] = cr
-        lv["cB"][i] = cb
         lv["iR"][i] = jnp.where(inside, 1.0 / cr, 0.0)
         lv["iB"][i] = jnp.where(inside, 1.0 / cb, 0.0)
-        return carry
-
-    lax.fori_loop(1, N0 - 1, inverses, 0, unroll=6)
+        return fxe, fxo
+
+    planes(1, N0 - 1, FACES, faces, x_faces(0, parity(0)))
 
     for k in range(2):
         sweep_packed(lv, True, 1 + 2 * k, N0 - 1 - 2 * k)
         sweep_packed(lv, False, 2 + 2 * k, N0 - 2 - 2 * k)
 
     def restrict(j, carry):
-        a, b, _ = residual_packed(lv, H0 + 2 * j)
-        c, d, _ = residual_packed(lv, H0 + 1 + 2 * j)
         i = H0 + 2 * j
+        a, b, _ = residual_packed(lv, i, H0 % 2)
+        c, d, _ = residual_packed(lv, i + 1, (H0 + 1) % 2)
         pair_r[j] = (a + b) + (c + d)
         pair_b[j] = (bE[i] + bO[i]) + (bE[i + 1] + bO[i + 1])
         return carry
 
-    lax.fori_loop(0, 16, restrict, 0, unroll=4)
+    lax.fori_loop(0, 16, restrict, 0, unroll=RESTRICT)
 
     halve = one_hot((256, 128), lambda i, j: (i >> 1) == j)
     f1 = 0.125 * matmul(pair_r[...].reshape(128, 256), halve)
@@ -243,18 +283,23 @@
     top, bot = row == depth - 1, row == 0
     end, begin = lane == width - 1, lane == 0
     cell = jnp.logical_and(row < depth, lane < width)
-    for i in range(n - 1):
-        ax[i] = factor * (b[i] + b[i + 1])
-    for i in range(1, n - 1):
+    ax[0] = factor * (b[0] + b[1])
+
+    def step(i, odd, before):
         v = b[i]
+        fx = factor * (v + b[i + 1])
+        ax[i] = fx
         fy = factor * (v + jnp.where(end, 0.0, up(v, 1)))
         gy = factor * (v + jnp.where(begin, 0.0, down(v, 1)))
         fz = factor * (v + jnp.where(top, 0.0, up(v, 0)))
         gz = factor * (v + jnp.where(bot, 0.0, down(v, 0)))
         ay[i] = jnp.where(end, 0.0, fy)
         az[i] = jnp.where(top, 0.0, fz)
-        center = (fz + gz) + (ax[i] + ax[i - 1]) + (fy + gy)
+        center = (fz + gz) + (fx + before) + (fy + gy)
         inv[i] = jnp.where(jnp.logical_and(cell, inside(i)), 1.0 / center, 0.0)
+        return fx
+
+    planes(1, n - 1, 99, step, ax[0])
 
 
 def nsum_plain(v, ax, ay, az, i):
@@ -264,21 +309,25 @@
     return t + (az[i] * up(here, 0) + down(az[i] * here, 0))
 
 
+def colour(odd):
+    return ((iota((8, 128), 0) + iota((8, 128), 1) + odd) & 1) == 0
+
+
 def sweep_plain(v, f, ax, ay, az, inv, odd, shift, first, last):
-    row, lane = iota((8, 128), 0), iota((8, 128), 1)
-    even = ((row + lane) & 1) == 0
-    masks = (even, jnp.logical_not(even))
-    for i in range(first, last):
-        cells = masks[(i + shift + odd) % 2]
+    def step(i, plane_odd, carry):
+        cells = colour((plane_odd + shift + odd) % 2)
         v[i] = jnp.where(cells, (f[i] + nsum_plain(v, ax, ay, az, i)) * inv[i], v[i])
+        return carry
+
+    planes(first, last, 99, step)
 
 
 def first_plain(v, f, inv, shift, first, last):
-    row, lane = iota((8, 128), 0), iota((8, 128), 1)
-    even = ((row + lane) & 1) == 0
-    masks = (even, jnp.logical_not(even))
-    for i in range(first, last):
-        v[i] = jnp.where(masks[(i + shift) % 2], f[i] * inv[i], 0.0)
+    def step(i, plane_odd, carry):
+        v[i] = jnp.where(colour((plane_odd + shift) % 2), f[i] * inv[i], 0.0)
+        return carry
+
+    planes(first, last, 99, step)
 
 
 def residual_plain(v, f, ax, ay, az, center, i):
@@ -293,8 +342,8 @@
     return factor * (4.0 * v + fy + fz) + (ax[i] + ax[i - 1])
 
 
-def middle_kernel(place, own, halo, bottom, v1, f1, ax1, ay1, az1, inv1, ax2, ay2, az2, inv2, send, message, v2, f2, b2, b1, tmp):
-    slab, box, boxes = place[0], place[1], place[2]
+def middle_kernel(boxes, own, halo, bottom, v1, f1, ax1, ay1, az1, inv1, ax2, ay2, az2, inv2, send, message, v2, f2, b2, b1, tmp):
+    slab, box = my_place()
     w = H1 + 1
     b1[0:w] = halo[0, H1 : H1 + w]
     b1[w : w + 16] = own[16:32]
@@ -327,12 +376,15 @@
     sweep_plain(v1, *one, 1, 1, 2, N1 - 2)
     sweep_plain(v1, *one, 0, 1, 3, N1 - 3)
     sweep_plain(v1, *one, 1, 1, 4, N1 - 4)
+
+    def restrict(j, carry):
+        i = 5 + 2 * j
+        parts = [residual_plain(v1, *one[:4], center_plain(b1, ax1, k, k1, 8, 128), k) for k in (i, i + 1)]
+        tmp[8 * j : 8 * j + 8, :] = parts[0] + parts[1]
+        return carry
+
     for j in range(16):
-        parts = [
-            residual_plain(v1, *one[:4], center_plain(b1, ax1, i, k1, 8, 128), i)
-            for i in (5 + 2 * j, 6 + 2 * j)
-        ]
-        tmp[8 * j : 8 * j + 8, :] = parts[0] + parts[1]
+        restrict(j, 0)
     summed = tmp[pl.ds(0, 64, stride=2), :] + tmp[pl.ds(1, 64, stride=2), :]
     coarse = 0.125 * matmul(summed, one_hot((128, 128), lambda i, j: (i >> 1) == j))
     for j in range(16):
@@ -420,8 +472,8 @@
     lax.fori_loop(0, ITERS, iterate, total(source, source))
 
 
-def coarse_kernel(boxes, place, gathered, e2, dref, qref, eref):
-    box = place[1]
+def coarse_kernel(boxes, gathered, e2, dref, qref, eref):
+    box = my_place()[1]
     source = [gathered[t, pl.ds(0, boxes, stride=2), :] for t in range(2)]
     coefficient = [gathered[t, pl.ds(1, boxes, stride=2), :] for t in range(2)]
     coarse_solve(boxes, source, coefficient, dref, qref, eref)
@@ -435,19 +487,23 @@
         e2[i] = jnp.where(row < 2, low, jnp.where(row < 4, high, 0.0))
 
 
-def after_kernel(send, gathered, out):
+def after_kernel(send, black, gathered, out):
     del gathered
-    out[...] = send[...]
-
-
-def last_kernel(place, *refs):
+    out[0:16] = send[...]
+    start = jnp.where(my_place()[0] == 0, 32, H0)
+    for k in range(H0):
+        for half in range(2):
+            out[16 + 2 * k + half] = black[start + k, :, 128 * half : 128 * half + 128]
+
+
+def last_kernel(*refs):
     names = ("e2", "beside", "own2", "v1", "f1", "ax1", "ay1", "az1", "inv1", "ax2", "ay2", "az2", "inv2")
     given = dict(zip(names, refs))
     refs = refs[len(names) :]
     level0 = dict(zip(PACKED, refs))
     refs = refs[len(PACKED) :]
     out_v, out_r, vR, vB, v1, v2, f2, wide, e0 = refs
-    slab = place[0]
+    slab = my_place()[0]
     e2, beside, own2 = given["e2"], given["beside"], given["own2"]
 
     for ref, part in ((v2, 0), (f2, 8)):
@@ -477,52 +533,59 @@
     e0[...] = matmul(v1[10:32].reshape(176, 128), double).reshape(22, 8, 256)
     lv = dict(level0, vR=vR, vB=vB)
 
+    black = level0["vB"]
+
     def correct(j, carry):
         e = e0[j]
-        vB[3 + 2 * j] = level0["vB"][3 + 2 * j] + e
-        vB[4 + 2 * j] = level0["vB"][4 + 2 * j] + e
+        vB[2 * j - 1] = black[2 * j - 1] + e
+        vB[2 * j] = black[2 * j] + e
         return carry
 
-    lax.fori_loop(0, 22, correct, 0, unroll=2)
-    for k in range(2):
-        sweep_packed(lv, True, 5 + 2 * k, N0 - 5 - 2 * k)
-        sweep_packed(lv, False, 6 + 2 * k, N0 - 6 - 2 * k)
-
-    for x in range(32):
-        i = H0 + x
-        red, black, p = residual_packed(lv, i)
-        for out, a, b in ((out_v, vR[i], vB[i]), (out_r, red, black)):
-            even, odd = jnp.where(p, a, b), jnp.where(p, b, a)
-            even = jnp.where(slab == 0, even[0:4], even[4:8])
-            odd = jnp.where(slab == 0, odd[0:4], odd[4:8])
+    lax.fori_loop(3, 19, correct, 0, unroll=4)
+    for side, at in ((0, 0), (1, H0 + 32)):
+        for k in range(H0):
             for half in range(2):
                 lanes = slice(128 * half, 128 * half + 128)
-                out[slab_rows(x, half, 0), :] = even[:, lanes]
-                out[slab_rows(x, half, 1), :] = odd[:, lanes]
-
-
-def call(kernel, outs, scratch, *args, scalars=0, limit=12):
+                vB[at + k, :, lanes] = beside[side, 16 + 2 * k + half] + e0[(at + k + 1) // 2, :, lanes]
+    for k in range(2):
+        sweep_packed(lv, True, 1 + 2 * k, N0 - 1 - 2 * k)
+        sweep_packed(lv, False, 2 + 2 * k, N0 - 2 - 2 * k)
+
+
+    def finish(i, odd, carry):
+        x = i - H0
+        red, black, p = residual_packed(lv, i, odd)
+        for out, a, b in ((out_v, vR[i], vB[i]), (out_r, red, black)):
+            for at, whole in ((0, jnp.where(p, a, b)), (1, jnp.where(p, b, a))):
+                part = jnp.where(slab == 0, whole[0:4], whole[4:8])
+                for half in range(2):
+                    out[slab_rows(x, half, at), :] = part[:, 128 * half : 128 * half + 128]
+        return carry
+
+    planes(H0, H0 + 32, FINISH, finish)
+
+
+def call(kernel, outs, scratch, *args, limit=12):
     vmem = pl.BlockSpec(memory_space=pltpu.VMEM)
-    smem = pl.BlockSpec(memory_space=pltpu.SMEM)
     return pl.pallas_call(
         kernel,
         out_shape=[jax.ShapeDtypeStruct(s, F32) for s in outs],
-        in_specs=[smem] * scalars + [vmem] * (len(args) - scalars),
+        in_specs=[vmem] * len(args),
         out_specs=[vmem] * len(outs),
         scratch_shapes=[pltpu.VMEM(s, F32) for s in scratch],
         compiler_params=pltpu.CompilerParams(vmem_limit_bytes=limit * 1024 * 1024),
     )(*args)
 
 
-def pack(*args):
+def edges(*args):
     return pl.pallas_call(
-        pack_kernel,
-        out_shape=[jax.ShapeDtypeStruct((rows, 256), F32) for rows in (16 * ROWS, 16 * ROWS, EDGE, EDGE)],
-        in_specs=[pl.BlockSpec(memory_space=pltpu.SMEM)] + [pl.BlockSpec(memory_space=pl.ANY)] * 3,
-        out_specs=[pl.BlockSpec(memory_space=pltpu.VMEM)] * 4,
-        scratch_shapes=[pltpu.VMEM((512, 128), F32)] * 3 + [pltpu.SemaphoreType.DMA((3,))],
-        compiler_params=pltpu.CompilerParams(vmem_limit_bytes=4 * 1024 * 1024),
-    )(*args)
+        edge_kernel,
+        out_shape=[jax.ShapeDtypeStruct((EDGE, 256), F32)] * 2,
+        in_specs=[pl.BlockSpec(memory_space=pl.ANY)] * 3,
+        out_specs=[pl.BlockSpec(memory_space=pltpu.VMEM)] * 2,
+        scratch_shapes=[pltpu.VMEM((128, 128), F32)] * 6 + [pltpu.SemaphoreType.DMA((6,))],
+        compiler_params=pltpu.CompilerParams(vmem_limit_bytes=60 * 1024 * 1024),
+    )(*[a.reshape(8, 64, 128) for a in args])
 
 
 def by_tiles(a):
@@ -535,12 +598,11 @@
 
 def body(pressure_guess, right_side, coefficient):
     boxes = lax.axis_size("box")
-    slab, box = lax.axis_index("slab"), lax.axis_index("box")
-    place = jnp.stack([slab, box, jnp.int32(boxes), jnp.int32(0)]).astype(jnp.int32)
     both = [(2 * i, 2 * i + 2) for i in range(boxes - 1)] + [(2 * i + 3, 2 * i + 1) for i in range(boxes - 1)]
 
     flat = [by_tiles(a) for a in (pressure_guess, right_side, coefficient)]
-    low, high, first, second = pack(place, *flat)
+    first, second = edges(*flat)
+    low, high = call(pack_kernel, [(16 * ROWS, 256)] * 2, [], *flat)
     odd_pairs = [(i, i + 1) for i in range(1, boxes - 1, 2)]
     even_pairs = [(i, i + 1) for i in range(0, boxes - 1, 2)]
     first = lax.ppermute(first, "box", odd_pairs + [(j, i) for i, j in odd_pairs])
@@ -550,14 +612,12 @@
 
     plane = (N0, 8, 256)
     fine = call(
-        fine_kernel,
+        functools.partial(fine_kernel, boxes),
         [plane] * len(PACKED) + [(40, 8, 128), (SEND1, 8, 128), (8, 128)],
         [plane] * 3 + [(16, 8, 256)] * 2 + [(64, 128)],
-        place,
         low,
         high,
         halo,
-        scalars=1,
     )
     level0 = fine[: len(PACKED)]
     own, send, bottom = fine[len(PACKED) :]
@@ -565,39 +625,33 @@
 
     one, two = (N1, 8, 128), (N2, 8, 128)
     *levels, send, message = call(
-        middle_kernel,
+        functools.partial(middle_kernel, boxes),
         [one] * 6 + [two] * 4 + [(16, 8, 128), (2 * boxes, 128)],
         [two] * 3 + [one, (128, 128)],
-        place,
         own,
         halo,
         bottom,
-        scalars=1,
     )
     spread = lax.all_to_all(message.reshape(boxes, 2, 128), "box", 0, 0).reshape(2 * boxes, 128)
-    (late,) = call(after_kernel, [(16, 8, 128)], [], send, spread)
+    (late,) = call(after_kernel, [(16 + 2 * H0, 8, 128)], [], send, level0[0], spread)
     beside = lax.ppermute(late, ("box", "slab"), both)
     gathered = lax.all_gather(spread, "slab")
     (e2,) = call(
         functools.partial(coarse_kernel, boxes),
         [two],
         [(2, boxes, 128), (2, boxes, 128), (2, boxes + 16, 128)],
-        place,
         gathered,
-        scalars=1,
     )
     beside = lax.all_gather(beside, "slab")
     pressure, residual = call(
         last_kernel,
         [(512, 128)] * 2,
         [plane, plane, one, two, two, (128, 128), (22, 8, 256)],
-        place,
         e2,
         beside,
         send,
         *levels,
         *level0,
-        scalars=1,
     )
     return from_tiles(pressure), from_tiles(residual)
 

time: 88 us -> 81.2 us (0.923)
  local copies, waits for them, and re-layouts: 2.85 us -> 0.01 us
  Pallas kernels: 21.8 us -> 19.5 us
  blocking collectives: 49.9 us -> 48.1 us
    pallas_call x5 -> x6, Pallas kernels: 20.7 us -> 17.6 us  [call(): pl.pallas_call(kernel, out_shape=[jax.ShapeDtypeStruct(s, F32) for s in o...]
    unnamed x6, local copies, waits for them, and re-layouts: 2.85 us -> 0.01 us
    all_to_all x1, blocking collectives: 33.2 us -> 31.7 us  [body(): lax.all_to_all(message.reshape(boxes, 2, 128), 'box', 0, 0)]
  transfers between devices with their start and end apart: 4 -> 4, of which waited for: 1 -> 1; matrix products, arithmetic and copies ran while one was open for 0% -> 0% of each run, Pallas kernels for 5% -> 6%
where the time goes in v5:
time: 81.2 us; the launch traced here: 80.7 us
  blocking collectives  48.1 us (59%)
  Pallas kernels  19.5 us (24%)
  starting transfers between devices  7.83 us (10%)
  waiting for transfers between devices  4.47 us (6%)
    all_to_all x1, blocking collectives, body(): lax.all_to_all(message.reshape(boxes, 2, 128), 'box', 0, 0)  31.7 us
    pallas_call x6, Pallas kernels, call(): pl.pallas_call(kernel, out_shape=[jax.ShapeDtypeStruct(s, F32) for s in o...  17.6 us
    all_gather x2, blocking collectives, body(): low, high = (lax.all_gather(low, 'slab'), lax.all_gather(high, 'slab'))  5.59 us
    all_gather x1, blocking collectives, body(): gathered = lax.all_gather(spread, 'slab')  4.7 us
    ppermute x1, starting transfers between devices, body(): lax.ppermute(second, 'box', even_pairs + [(j, i) for i, j in even_pairs])  4.58 us
    ppermute x1, waiting for transfers between devices, body(): halo = lax.all_gather(lax.ppermute(send, ('box', 'slab'), both), 'slab')  4.46 us
    all_gather x1, blocking collectives, body(): halo = lax.all_gather(jnp.stack([first, second]), 'slab')  2.16 us
    all_gather x1, blocking collectives, body(): halo = lax.all_gather(lax.ppermute(send, ('box', 'slab'), both), 'slab')  1.99 us
  transfers between devices with their start and end apart: 4, of which 1 were waited for; matrix products, arithmetic and copies ran while one was open for 0% of the time, Pallas kernels for 6%

profile of v5, /device:TPU:1, one launch (start us, length us, event | category | flops | bytes accessed | tf_op | source)
XLA Modules:
  0.0 80.7 jit_solution(4065587995105932860)
XLA Ops:
  0.6 0.0 copy-start
  0.6 0.0 copy-start.1
  0.6 0.0 copy-start.2
  0.7 2.0 %shard_map.51 = (f32[120,256]{1,0:T(8,128)}, f32[120,256]{1,0:T(8,128)}) custom-call(f32[8,64,128]{2,1,0:T(8,128)} %bitcast.47, f32[8,64,128]{2,1,0:T(8,128)} %bitcast.49, f32[8,64,128]{2,1,0:T(8,128)} %bitcast.51), custom_call_target="tpu_custom_call" | custom-call | tf_op jit(solution)/shard_map/pallas_call | solution.py:581
  2.6 0.7 collective-permute-start
  3.3 4.6 %collective-permute-start.1 = (f32[120,256]{1,0:T(8,128)}, f32[120,256]{1,0:T(8,128)S(1)}, u32[]{:S(2)}, u32[]{:S(2)}) collective-permute-start(f32[120,256]{1,0:T(8,128)} %get-tuple-element.39), channel_id=1, source_target_pairs={{0,2},{4,6},{8,10},{12,14},{16,18},{20,22},{24,26},{28,30},{32,34}... | collective-permute-start | bytes 368648 | tf_op jit(solution)/shard_map/ppermute | solution.py:609
  7.9 0.0 copy-done
  7.9 0.0 copy-done.1
  7.9 0.0 copy-done.2
  7.9 0.5 shard_map.50
  8.4 3.2 %all-gather = f32[768,256]{1,0:T(8,128)S(1)} all-gather(f32[384,256]{1,0:T(8,128)S(1)} %get-tuple-element.36), channel_id=2, replica_groups=mesh['box'=128,'slab'=2] {'slab'}, dimensions={0}, use_global_device_ids=true | all-gather | bytes 1179648 | tf_op jit(solution)/shard_map/all_gather | solution.py:610
  11.7 2.4 %all-gather.1 = f32[768,256]{1,0:T(8,128)S(1)} all-gather(f32[384,256]{1,0:T(8,128)S(1)} %get-tuple-element.37), channel_id=3, replica_groups=mesh['box'=128,'slab'=2] {'slab'}, dimensions={0}, use_global_device_ids=true | all-gather | bytes 1179648 | tf_op jit(solution)/shard_map/all_gather | solution.py:610
  14.0 0.0 collective-permute-done
  14.0 0.0 collective-permute-done.1
  14.0 2.2 %all-gather.2 = f32[4,120,256]{2,1,0:T(8,128)S(1)} all-gather(f32[2,120,256]{2,1,0:T(8,128)S(1)} %pad_maximum_fusion), channel_id=4, replica_groups=mesh['box'=128,'slab'=2] {'slab'}, dimensions={0}, use_global_device_ids=true | all-gather | bytes 737280 | tf_op jit(solution)/shard_map/all_gather | solution.py:611
  16.2 5.2 %shard_map.52 = (f32[42,8,256]{2,1,0:T(8,128)S(1)}, f32[42,8,256]{2,1,0:T(8,128)S(1)}, f32[42,8,256]{2,1,0:T(8,128)S(1)}, f32[42,8,256]{2,1,0:T(8,128)S(1)}, f32...) custom-call(f32[2,384,256]{2,1,0:T(8,128)S(1)} %bitcast.41, ...), custom_call_target="tpu_custom_call" | custom-call | tf_op jit(solution)/shard_map/pallas_call | solution.py:570
  21.4 1.3 %collective-permute-start.2 = (f32[33,8,128]{2,1,0:T(8,128)S(1)}, f32[33,8,128]{2,1,0:T(8,128)S(1)}, u32[]{:S(2)}, u32[]{:S(2)}) collective-permute-start(f32[33,8,128]{2,1,0:T(8,128)S(1)} %get-tuple-element.41), channel_id=1, source_target_pairs={{0,2},{2,4},{4,6},{6,8},{8,10},{10,12},{12,14},{14,16},{16,18},{18... | collective-permute-start | bytes 405512 | tf_op jit(solution)/shard_map/ppermute | solution.py:624
  22.7 4.5 %collective-permute-done.2 = f32[33,8,128]{2,1,0:T(8,128)S(1)} collective-permute-done((f32[33,8,128]{2,1,0:T(8,128)S(1)}, f32[33,8,128]{2,1,0:T(8,128)S(1)}, u32[]{:S(2)}, u32[]{:S(2)}) %collective-permute-start.2) | collective-permute-done | bytes 135200 | tf_op jit(solution)/shard_map/ppermute | solution.py:624
  27.2 2.0 %all-gather.3 = f32[66,8,128]{2,1,0:T(8,128)S(1)} all-gather(f32[33,8,128]{2,1,0:T(8,128)S(1)} %collective-permute-done.2), channel_id=5, replica_groups=mesh['box'=128,'slab'=2] {'slab'}, dimensions={0}, use_global_device_ids=true | all-gather | bytes 405504 | tf_op jit(solution)/shard_map/all_gather | solution.py:624
  29.2 1.8 %shard_map.53 = (f32[42,8,128]{2,1,0:T(8,128)S(1)}, f32[42,8,128]{2,1,0:T(8,128)S(1)}, f32[42,8,128]{2,1,0:T(8,128)S(1)}, f32[42,8,128]{2,1,0:T(8,128)S(1)}, f32...) custom-call(f32[40,8,128]{2,1,0:T(8,128)S(1)} %get-tuple-element.40., ...), custom_call_target="tpu_custom_call" | custom-call | tf_op jit(solution)/shard_map/pallas_call | solution.py:570
  31.0 31.7 %all_to_all.5 = f32[128,2,128]{2,1,0:T(2,128)S(1)} all-to-all(f32[128,2,128]{2,1,0:T(2,128)S(1)} %bitcast.54), channel_id=1, replica_groups=mesh['box'=128,'slab'=2] {'box'}, dimensions={0} | all-to-all | bytes 262144 | tf_op jit(solution)/shard_map/all_to_all | solution.py:635
  62.7 1.3 %collective-permute-start.3 = (f32[26,8,128]{2,1,0:T(8,128)S(1)}, f32[26,8,128]{2,1,0:T(8,128)S(1)}, u32[]{:S(2)}, u32[]{:S(2)}) collective-permute-start(f32[26,8,128]{2,1,0:T(8,128)S(1)} %shard_map.55), channel_id=1, source_target_pairs={{0,2},{2,4},{4,6},{6,8},{8,10},{10,12},{12,14},{14,16},{16,18},{18... | collective-permute-start | bytes 319496 | tf_op jit(solution)/shard_map/ppermute | solution.py:637
  64.0 4.7 %all_gather.41.gathered = f32[2,256,128]{2,1,0:T(8,128)S(1)} all-gather(f32[1,256,128]{2,1,0:T(8,128)S(1)} %bitcast.45), channel_id=1, replica_groups=mesh['box'=128,'slab'=2] {'slab'}, dimensions={0}, use_global_device_ids=true | all-gather | bytes 393216 | tf_op jit(solution)/shard_map/all_gather | solution.py:638
  68.7 4.0 %shard_map.54.refs_0_ = f32[24,8,128]{2,1,0:T(8,128)S(1)} custom-call(f32[2,256,128]{2,1,0:T(8,128)S(1)} %all_gather.41.gathered), custom_call_target="tpu_custom_call" | custom-call | tf_op jit(solution)/shard_map/pallas_call | solution.py:570
  72.7 0.0 collective-permute-done.3
  72.7 2.0 %all-gather.4 = f32[52,8,128]{2,1,0:T(8,128)S(1)} all-gather(f32[26,8,128]{2,1,0:T(8,128)S(1)} %collective-permute-done.3), channel_id=6, replica_groups=mesh['box'=128,'slab'=2] {'slab'}, dimensions={0}, use_global_device_ids=true | all-gather | bytes 319488 | tf_op jit(solution)/shard_map/all_gather | solution.py:645
  74.7 6.0 %shard_map.56 = (f32[512,128]{1,0:T(8,128)}, f32[512,128]{1,0:T(8,128)}) custom-call(f32[24,8,128]{2,1,0:T(8,128)S(1)} %shard_map.54.refs_0_, f32[2,26,8,128]{3,2,1,0:T(8,128)S(1)} %bitcast.53, f32[16,8,128]{2,1,0:T(8,128)S(1)} %get-tuple-element.44.send.refs_2_, f32[42,8,128]{2,1,0:T(8,128)S(1)} %get-tuple-element.46.refs_3_, ...), custom_call_target="tpu_custom_call" | custom-call | tf_op jit(solution)/shard_map/pallas_call | solution.py:570
  (2 shorter events, 0.0 us)
Async XLA Ops:
  0.6 7.3 %copy-start = (f32[8,32,256]{2,1,0:T(8,128)S(1)}, f32[8,32,256]{2,1,0:T(8,128)}, u32[]{:S(2)}) copy-start(f32[8,32,256]{2,1,0:T(8,128)} %param.3) | copy-start | bytes 786436
  0.6 7.3 %copy-start.1 = (f32[8,32,256]{2,1,0:T(8,128)S(1)}, f32[8,32,256]{2,1,0:T(8,128)}, u32[]{:S(2)}) copy-start(f32[8,32,256]{2,1,0:T(8,128)} %param.4) | copy-start | bytes 786436
  0.6 7.3 %copy-start.2 = (f32[8,32,256]{2,1,0:T(8,128)S(1)}, f32[8,32,256]{2,1,0:T(8,128)}, u32[]{:S(2)}) copy-start(f32[8,32,256]{2,1,0:T(8,128)} %param.5) | copy-start | bytes 786436
  2.6 11.4 %collective-permute-start = (f32[120,256]{1,0:T(8,128)}, f32[120,256]{1,0:T(8,128)S(1)}, u32[]{:S(2)}, u32[]{:S(2)}) collective-permute-start(f32[120,256]{1,0:T(8,128)} %get-tuple-element.38), channel_id=1, source_target_pairs={{2,4},{6,8},{10,12},{14,16},{18,20},{22,24},{26,28},{30,32},{34,36... | collective-permute-start | bytes 368648 | tf_op jit(solution)/shard_map/ppermute | solution.py:608
  3.3 10.7 %collective-permute-start.1 = (f32[120,256]{1,0:T(8,128)}, f32[120,256]{1,0:T(8,128)S(1)}, u32[]{:S(2)}, u32[]{:S(2)}) collective-permute-start(f32[120,256]{1,0:T(8,128)} %get-tuple-element.39), channel_id=1, source_target_pairs={{0,2},{4,6},{8,10},{12,14},{16,18},{20,22},{24,26},{28,30},{32,34}... | collective-permute-start | bytes 368648 | tf_op jit(solution)/shard_map/ppermute | solution.py:609
  21.4 5.8 %collective-permute-start.2 = (f32[33,8,128]{2,1,0:T(8,128)S(1)}, f32[33,8,128]{2,1,0:T(8,128)S(1)}, u32[]{:S(2)}, u32[]{:S(2)}) collective-permute-start(f32[33,8,128]{2,1,0:T(8,128)S(1)} %get-tuple-element.41), channel_id=1, source_target_pairs={{0,2},{2,4},{4,6},{6,8},{8,10},{10,12},{12,14},{14,16},{16,18},{18... | collective-permute-start | bytes 405512 | tf_op jit(solution)/shard_map/ppermute | solution.py:624
  62.7 10.0 %collective-permute-start.3 = (f32[26,8,128]{2,1,0:T(8,128)S(1)}, f32[26,8,128]{2,1,0:T(8,128)S(1)}, u32[]{:S(2)}, u32[]{:S(2)}) collective-permute-start(f32[26,8,128]{2,1,0:T(8,128)S(1)} %shard_map.55), channel_id=1, source_target_pairs={{0,2},{2,4},{4,6},{6,8},{8,10},{10,12},{12,14},{14,16},{16,18},{18... | collective-permute-start | bytes 319496 | tf_op jit(solution)/shard_map/ppermute | solution.py:637

commit v6 on v5

--- a/solution.py
+++ b/solution.py
@@ -18,7 +18,7 @@
 N2 = 24
 ROWS = 24
 EDGE = H0 * ROWS
-SWEEP, FACES, RESTRICT, MERGE, FINISH = 10, 5, 4, 8, 99
+SWEEP, FACES, RESTRICT, MERGE, FINISH = 99, 99, 16, 16, 99
 SEND1 = H1 + (H1 + 1) + 8
 
 

time: 81.2 us -> 76.8 us (0.946)
  Pallas kernels: 19.5 us -> 15.1 us
    pallas_call x6, Pallas kernels: 17.6 us -> 13.1 us  [call(): pl.pallas_call(kernel, out_shape=[jax.ShapeDtypeStruct(s, F32) for s in o...]
where the time goes in v6:
time: 76.8 us; the launch traced here: 76.2 us
  blocking collectives  48.1 us (63%)
  Pallas kernels  15.1 us (20%)
  starting transfers between devices  7.83 us (10%)
  waiting for transfers between devices  4.47 us (6%)
    all_to_all x1, blocking collectives, body(): lax.all_to_all(message.reshape(boxes, 2, 128), 'box', 0, 0)  31.7 us
    pallas_call x6, Pallas kernels, call(): pl.pallas_call(kernel, out_shape=[jax.ShapeDtypeStruct(s, F32) for s in o...  13.1 us
    all_gather x2, blocking collectives, body(): low, high = (lax.all_gather(low, 'slab'), lax.all_gather(high, 'slab'))  5.59 us
    all_gather x1, blocking collectives, body(): gathered = lax.all_gather(spread, 'slab')  4.7 us
    ppermute x1, starting transfers between devices, body(): lax.ppermute(second, 'box', even_pairs + [(j, i) for i, j in even_pairs])  4.58 us
    ppermute x1, waiting for transfers between devices, body(): halo = lax.all_gather(lax.ppermute(send, ('box', 'slab'), both), 'slab')  4.46 us
    all_gather x1, blocking collectives, body(): halo = lax.all_gather(jnp.stack([first, second]), 'slab')  2.16 us
    all_gather x1, blocking collectives, body(): halo = lax.all_gather(lax.ppermute(send, ('box', 'slab'), both), 'slab')  1.99 us
  transfers between devices with their start and end apart: 4, of which 1 were waited for; matrix products, arithmetic and copies ran while one was open for 0% of the time, Pallas kernels for 6%

profile of v6, /device:TPU:1, one launch (start us, length us, event | category | flops | bytes accessed | tf_op | source)
XLA Modules:
  0.0 76.2 jit_solution(13447817318406503372)
XLA Ops:
  0.6 0.0 copy-start
  0.6 0.0 copy-start.1
  0.6 0.0 copy-start.2
  0.7 2.0 %shard_map.51 = (f32[120,256]{1,0:T(8,128)}, f32[120,256]{1,0:T(8,128)}) custom-call(f32[8,64,128]{2,1,0:T(8,128)} %bitcast.47, f32[8,64,128]{2,1,0:T(8,128)} %bitcast.49, f32[8,64,128]{2,1,0:T(8,128)} %bitcast.51), custom_call_target="tpu_custom_call" | custom-call | tf_op jit(solution)/shard_map/pallas_call | solution.py:581
  2.6 0.7 collective-permute-start
  3.3 4.6 %collective-permute-start.1 = (f32[120,256]{1,0:T(8,128)}, f32[120,256]{1,0:T(8,128)S(1)}, u32[]{:S(2)}, u32[]{:S(2)}) collective-permute-start(f32[120,256]{1,0:T(8,128)} %get-tuple-element.39), channel_id=1, source_target_pairs={{0,2},{4,6},{8,10},{12,14},{16,18},{20,22},{24,26},{28,30},{32,34}... | collective-permute-start | bytes 368648 | tf_op jit(solution)/shard_map/ppermute | solution.py:609
  7.9 0.0 copy-done
  7.9 0.0 copy-done.1
  7.9 0.0 copy-done.2
  7.9 0.5 shard_map.50
  8.4 3.2 %all-gather = f32[768,256]{1,0:T(8,128)S(1)} all-gather(f32[384,256]{1,0:T(8,128)S(1)} %get-tuple-element.36), channel_id=2, replica_groups=mesh['box'=128,'slab'=2] {'slab'}, dimensions={0}, use_global_device_ids=true | all-gather | bytes 1179648 | tf_op jit(solution)/shard_map/all_gather | solution.py:610
  11.7 2.4 %all-gather.1 = f32[768,256]{1,0:T(8,128)S(1)} all-gather(f32[384,256]{1,0:T(8,128)S(1)} %get-tuple-element.37), channel_id=3, replica_groups=mesh['box'=128,'slab'=2] {'slab'}, dimensions={0}, use_global_device_ids=true | all-gather | bytes 1179648 | tf_op jit(solution)/shard_map/all_gather | solution.py:610
  14.0 0.0 collective-permute-done
  14.0 0.0 collective-permute-done.1
  14.0 2.2 %all-gather.2 = f32[4,120,256]{2,1,0:T(8,128)S(1)} all-gather(f32[2,120,256]{2,1,0:T(8,128)S(1)} %pad_maximum_fusion), channel_id=4, replica_groups=mesh['box'=128,'slab'=2] {'slab'}, dimensions={0}, use_global_device_ids=true | all-gather | bytes 737280 | tf_op jit(solution)/shard_map/all_gather | solution.py:611
  16.2 2.8 %shard_map.52 = (f32[42,8,256]{2,1,0:T(8,128)S(1)}, f32[42,8,256]{2,1,0:T(8,128)S(1)}, f32[42,8,256]{2,1,0:T(8,128)S(1)}, f32[42,8,256]{2,1,0:T(8,128)S(1)}, f32...) custom-call(f32[2,384,256]{2,1,0:T(8,128)S(1)} %bitcast.41, ...), custom_call_target="tpu_custom_call" | custom-call | tf_op jit(solution)/shard_map/pallas_call | solution.py:570
  19.1 1.3 %collective-permute-start.2 = (f32[33,8,128]{2,1,0:T(8,128)S(1)}, f32[33,8,128]{2,1,0:T(8,128)S(1)}, u32[]{:S(2)}, u32[]{:S(2)}) collective-permute-start(f32[33,8,128]{2,1,0:T(8,128)S(1)} %get-tuple-element.41), channel_id=1, source_target_pairs={{0,2},{2,4},{4,6},{6,8},{8,10},{10,12},{12,14},{14,16},{16,18},{18... | collective-permute-start | bytes 405512 | tf_op jit(solution)/shard_map/ppermute | solution.py:624
  20.4 4.5 %collective-permute-done.2 = f32[33,8,128]{2,1,0:T(8,128)S(1)} collective-permute-done((f32[33,8,128]{2,1,0:T(8,128)S(1)}, f32[33,8,128]{2,1,0:T(8,128)S(1)}, u32[]{:S(2)}, u32[]{:S(2)}) %collective-permute-start.2) | collective-permute-done | bytes 135200 | tf_op jit(solution)/shard_map/ppermute | solution.py:624
  24.8 2.0 %all-gather.3 = f32[66,8,128]{2,1,0:T(8,128)S(1)} all-gather(f32[33,8,128]{2,1,0:T(8,128)S(1)} %collective-permute-done.2), channel_id=5, replica_groups=mesh['box'=128,'slab'=2] {'slab'}, dimensions={0}, use_global_device_ids=true | all-gather | bytes 405504 | tf_op jit(solution)/shard_map/all_gather | solution.py:624
  26.8 1.8 %shard_map.53 = (f32[42,8,128]{2,1,0:T(8,128)S(1)}, f32[42,8,128]{2,1,0:T(8,128)S(1)}, f32[42,8,128]{2,1,0:T(8,128)S(1)}, f32[42,8,128]{2,1,0:T(8,128)S(1)}, f32...) custom-call(f32[40,8,128]{2,1,0:T(8,128)S(1)} %get-tuple-element.40., ...), custom_call_target="tpu_custom_call" | custom-call | tf_op jit(solution)/shard_map/pallas_call | solution.py:570
  28.6 31.7 %all_to_all.5 = f32[128,2,128]{2,1,0:T(2,128)S(1)} all-to-all(f32[128,2,128]{2,1,0:T(2,128)S(1)} %bitcast.54), channel_id=1, replica_groups=mesh['box'=128,'slab'=2] {'box'}, dimensions={0} | all-to-all | bytes 262144 | tf_op jit(solution)/shard_map/all_to_all | solution.py:635
  60.3 1.3 %collective-permute-start.3 = (f32[26,8,128]{2,1,0:T(8,128)S(1)}, f32[26,8,128]{2,1,0:T(8,128)S(1)}, u32[]{:S(2)}, u32[]{:S(2)}) collective-permute-start(f32[26,8,128]{2,1,0:T(8,128)S(1)} %shard_map.55), channel_id=1, source_target_pairs={{0,2},{2,4},{4,6},{6,8},{8,10},{10,12},{12,14},{14,16},{16,18},{18... | collective-permute-start | bytes 319496 | tf_op jit(solution)/shard_map/ppermute | solution.py:637
  61.6 4.7 %all_gather.41.gathered = f32[2,256,128]{2,1,0:T(8,128)S(1)} all-gather(f32[1,256,128]{2,1,0:T(8,128)S(1)} %bitcast.45), channel_id=1, replica_groups=mesh['box'=128,'slab'=2] {'slab'}, dimensions={0}, use_global_device_ids=true | all-gather | bytes 393216 | tf_op jit(solution)/shard_map/all_gather | solution.py:638
  66.3 4.0 %shard_map.54.refs_0_ = f32[24,8,128]{2,1,0:T(8,128)S(1)} custom-call(f32[2,256,128]{2,1,0:T(8,128)S(1)} %all_gather.41.gathered), custom_call_target="tpu_custom_call" | custom-call | tf_op jit(solution)/shard_map/pallas_call | solution.py:570
  70.3 0.0 collective-permute-done.3
  70.3 2.0 %all-gather.4 = f32[52,8,128]{2,1,0:T(8,128)S(1)} all-gather(f32[26,8,128]{2,1,0:T(8,128)S(1)} %collective-permute-done.3), channel_id=6, replica_groups=mesh['box'=128,'slab'=2] {'slab'}, dimensions={0}, use_global_device_ids=true | all-gather | bytes 319488 | tf_op jit(solution)/shard_map/all_gather | solution.py:645
  72.3 3.9 %shard_map.56 = (f32[512,128]{1,0:T(8,128)}, f32[512,128]{1,0:T(8,128)}) custom-call(f32[24,8,128]{2,1,0:T(8,128)S(1)} %shard_map.54.refs_0_, f32[2,26,8,128]{3,2,1,0:T(8,128)S(1)} %bitcast.53, f32[16,8,128]{2,1,0:T(8,128)S(1)} %get-tuple-element.44.send.refs_2_, f32[42,8,128]{2,1,0:T(8,128)S(1)} %get-tuple-element.46.refs_3_, ...), custom_call_target="tpu_custom_call" | custom-call | tf_op jit(solution)/shard_map/pallas_call | solution.py:570
  (2 shorter events, 0.0 us)
Async XLA Ops:
  0.6 7.3 %copy-start = (f32[8,32,256]{2,1,0:T(8,128)S(1)}, f32[8,32,256]{2,1,0:T(8,128)}, u32[]{:S(2)}) copy-start(f32[8,32,256]{2,1,0:T(8,128)} %param.3) | copy-start | bytes 786436
  0.6 7.3 %copy-start.1 = (f32[8,32,256]{2,1,0:T(8,128)S(1)}, f32[8,32,256]{2,1,0:T(8,128)}, u32[]{:S(2)}) copy-start(f32[8,32,256]{2,1,0:T(8,128)} %param.4) | copy-start | bytes 786436
  0.6 7.3 %copy-start.2 = (f32[8,32,256]{2,1,0:T(8,128)S(1)}, f32[8,32,256]{2,1,0:T(8,128)}, u32[]{:S(2)}) copy-start(f32[8,32,256]{2,1,0:T(8,128)} %param.5) | copy-start | bytes 786436
  2.6 11.4 %collective-permute-start = (f32[120,256]{1,0:T(8,128)}, f32[120,256]{1,0:T(8,128)S(1)}, u32[]{:S(2)}, u32[]{:S(2)}) collective-permute-start(f32[120,256]{1,0:T(8,128)} %get-tuple-element.38), channel_id=1, source_target_pairs={{2,4},{6,8},{10,12},{14,16},{18,20},{22,24},{26,28},{30,32},{34,36... | collective-permute-start | bytes 368648 | tf_op jit(solution)/shard_map/ppermute | solution.py:608
  3.3 10.7 %collective-permute-start.1 = (f32[120,256]{1,0:T(8,128)}, f32[120,256]{1,0:T(8,128)S(1)}, u32[]{:S(2)}, u32[]{:S(2)}) collective-permute-start(f32[120,256]{1,0:T(8,128)} %get-tuple-element.39), channel_id=1, source_target_pairs={{0,2},{4,6},{8,10},{12,14},{16,18},{20,22},{24,26},{28,30},{32,34}... | collective-permute-start | bytes 368648 | tf_op jit(solution)/shard_map/ppermute | solution.py:609
  19.1 5.8 %collective-permute-start.2 = (f32[33,8,128]{2,1,0:T(8,128)S(1)}, f32[33,8,128]{2,1,0:T(8,128)S(1)}, u32[]{:S(2)}, u32[]{:S(2)}) collective-permute-start(f32[33,8,128]{2,1,0:T(8,128)S(1)} %get-tuple-element.41), channel_id=1, source_target_pairs={{0,2},{2,4},{4,6},{6,8},{8,10},{10,12},{12,14},{14,16},{16,18},{18... | collective-permute-start | bytes 405512 | tf_op jit(solution)/shard_map/ppermute | solution.py:624
  60.3 10.0 %collective-permute-start.3 = (f32[26,8,128]{2,1,0:T(8,128)S(1)}, f32[26,8,128]{2,1,0:T(8,128)S(1)}, u32[]{:S(2)}, u32[]{:S(2)}) collective-permute-start(f32[26,8,128]{2,1,0:T(8,128)S(1)} %shard_map.55), channel_id=1, source_target_pairs={{0,2},{2,4},{4,6},{6,8},{8,10},{10,12},{12,14},{14,16},{16,18},{18... | collective-permute-start | bytes 319496 | tf_op jit(solution)/shard_map/ppermute | solution.py:637

commit v7 on v6

--- a/solution.py
+++ b/solution.py
@@ -19,7 +19,8 @@
 ROWS = 24
 EDGE = H0 * ROWS
 SWEEP, FACES, RESTRICT, MERGE, FINISH = 99, 99, 16, 16, 99
-SEND1 = H1 + (H1 + 1) + 8
+SEND1 = H1 + (H1 + 1) + 4
+SEND2 = 16 + 2 * H0
 
 
 def matmul(x, m):
@@ -167,10 +168,10 @@
 
 def fine_kernel(boxes, lo, hi, halo, *refs):
     outs = dict(zip(PACKED, refs))
-    own, send, bottom = refs[len(PACKED) : len(PACKED) + 3]
-    vR, bE, bO, pair_r, pair_b, tmp = refs[len(PACKED) + 3 :]
+    own, first, second, bottom = refs[len(PACKED) : len(PACKED) + 4]
+    vR, bE, bO, pair_r, pair_b, tmp = refs[len(PACKED) + 4 :]
     lv = dict(outs, vR=vR)
-    slab, box = my_place()
+    box = my_place()[1]
     odd = box & 1
     row, lane = iota((8, 256), 0), iota((8, 256), 1)
     low_half = row < 4
@@ -255,26 +256,23 @@
         tmp[8 * k : 8 * k + 8, :] = own[16 + 2 * k] + own[17 + 2 * k]
     summed = tmp[pl.ds(0, 32, stride=2), :] + tmp[pl.ds(1, 32, stride=2), :]
     halve = one_hot((128, 128), lambda i, j: (i >> 1) == j)
-    b2 = 0.125 * matmul(summed, halve)
-    own[32:40] = jnp.zeros((8, 8, 128), F32)
-    for k in range(8):
-        own[32 + k, 0:4, :] = b2[4 * k : 4 * k + 4]
-    bottom[...] = bottom_row([own[32 + 2 * k] + own[33 + 2 * k] for k in range(4)], slab)
-
-    first = jnp.where(slab == 0, 1, 0)
-    send[0:H1] = own[pl.ds(first * (16 - H1), H1)]
-    send[H1 : 2 * H1 + 1] = own[pl.ds(16 + first * (15 - H1), H1 + 1)]
-    send[2 * H1 + 1 :] = own[32:40]
-
-
-def bottom_row(pairs, slab):
+    own[32:36] = (0.125 * matmul(summed, halve)).reshape(4, 8, 128)
+    bottom[...] = bottom_row([own[32 + k] + pltpu.roll(own[32 + k], 4, 0) for k in range(4)])
+
+    for out, right in ((first, odd), (second, 1 - odd)):
+        out[0:H1] = own[pl.ds(right * (16 - H1), H1)]
+        out[H1 : 2 * H1 + 1] = own[pl.ds(16 + right * (15 - H1), H1 + 1)]
+        out[2 * H1 + 1 :] = own[32:36]
+
+
+def bottom_row(pairs):
     total = None
     for k, plane in enumerate(pairs):
         spread = one_hot((128, 128), lambda i, j, k=k: jnp.logical_and((i >> 1) + 32 * k == j, i < 64))
         part = matmul(plane, spread)
         total = part if total is None else total + part
     low, high = total[0:1] + total[1:2], total[2:3] + total[3:4]
-    row = 0.125 * jnp.where(slab == 0, low, high)
+    row = 0.125 * jnp.where(my_place()[0] == 0, low, high)
     return jnp.broadcast_to(row, (8, 128))
 
 
@@ -342,20 +340,30 @@
     return factor * (4.0 * v + fy + fz) + (ax[i] + ax[i - 1])
 
 
-def middle_kernel(boxes, own, halo, bottom, v1, f1, ax1, ay1, az1, inv1, ax2, ay2, az2, inv2, send, message, v2, f2, b2, b1, tmp):
-    slab, box = my_place()
+def middle_kernel(boxes, own, first, second, bottom, v1, f1, ax1, ay1, az1, inv1, ax2, ay2, az2, inv2, send, message, v2, f2, b2, b1, tmp):
+    box = my_place()[1]
     w = H1 + 1
-    b1[0:w] = halo[0, H1 : H1 + w]
+    swapped = (box & 1) == 1
+
+    def received(k, count):
+        one, two = first[k : k + count], second[k : k + count]
+        return jnp.where(swapped, two, one), jnp.where(swapped, one, two)
+
+    left, right = received(H1, w)
+    b1[0:w] = left
     b1[w : w + 16] = own[16:32]
-    b1[w + 16 :] = halo[1, H1 : H1 + w]
+    b1[w + 16 :] = right
+    left, right = received(0, H1)
     f1[0:1] = jnp.zeros((1, 8, 128), F32)
-    f1[1 : 1 + H1] = halo[0, 0:H1]
+    f1[1 : 1 + H1] = left
     f1[w : w + 16] = own[0:16]
-    f1[w + 16 : w + 16 + H1] = halo[1, 0:H1]
+    f1[w + 16 : w + 16 + H1] = right
     f1[N1 - 1 :] = jnp.zeros((1, 8, 128), F32)
-    b2[0:8] = halo[0, H1 + w :]
-    b2[8:16] = own[32:40]
-    b2[16:24] = halo[1, H1 + w :]
+    left, right = received(H1 + w, 4)
+    b2[...] = jnp.zeros(b2.shape, F32)
+    for at, part in ((0, left), (8, own[32:36]), (16, right)):
+        for k in range(8):
+            b2[at + k, 0:4, :] = part[k // 2, 4 * (k % 2) : 4 * (k % 2) + 4]
     v1[...] = jnp.zeros(v1.shape, F32)
     v2[...] = jnp.zeros(v2.shape, F32)
     f2[...] = jnp.zeros(f2.shape, F32)
@@ -405,7 +413,7 @@
             for i in (8 + 2 * k, 9 + 2 * k)
         ]
         pairs.append(parts[0] + parts[1])
-    source = bottom_row(pairs, slab)
+    source = bottom_row(pairs)
     rows = jnp.where((iota((8, 128), 0) & 1) == 0, source, bottom[...])
     for k in range(message.shape[0] // 8):
         message[8 * k : 8 * k + 8, :] = rows
@@ -487,29 +495,36 @@
         e2[i] = jnp.where(row < 2, low, jnp.where(row < 4, high, 0.0))
 
 
-def after_kernel(send, black, gathered, out):
+def after_kernel(send, black, gathered, first, second):
     del gathered
-    out[0:16] = send[...]
-    start = jnp.where(my_place()[0] == 0, 32, H0)
-    for k in range(H0):
-        for half in range(2):
-            out[16 + 2 * k + half] = black[start + k, :, 128 * half : 128 * half + 128]
+    odd = my_place()[1] & 1
+    for out, right in ((first, odd), (second, 1 - odd)):
+        out[0:16] = send[...]
+        start = H0 + right * (32 - H0)
+        for k in range(H0):
+            for half in range(2):
+                out[16 + 2 * k + half] = black[start + k, :, 128 * half : 128 * half + 128]
 
 
 def last_kernel(*refs):
-    names = ("e2", "beside", "own2", "v1", "f1", "ax1", "ay1", "az1", "inv1", "ax2", "ay2", "az2", "inv2")
+    names = ("e2", "first", "second", "own2", "v1", "f1", "ax1", "ay1", "az1", "inv1", "ax2", "ay2", "az2", "inv2")
     given = dict(zip(names, refs))
     refs = refs[len(names) :]
     level0 = dict(zip(PACKED, refs))
     refs = refs[len(PACKED) :]
     out_v, out_r, vR, vB, v1, v2, f2, wide, e0 = refs
-    slab = my_place()[0]
-    e2, beside, own2 = given["e2"], given["beside"], given["own2"]
+    slab, box = my_place()
+    e2, first, second, own2 = given["e2"], given["first"], given["second"], given["own2"]
+    swapped = (box & 1) == 1
+
+    def received(side, k, count):
+        one, two = (first, second) if side == 0 else (second, first)
+        return jnp.where(swapped, two[k : k + count], one[k : k + count])
 
     for ref, part in ((v2, 0), (f2, 8)):
-        ref[0:8] = beside[0, part : part + 8]
+        ref[0:8] = received(0, part, 8)
         ref[8:16] = own2[part : part + 8]
-        ref[16:24] = beside[1, part : part + 8]
+        ref[16:24] = received(1, part, 8)
     for i in range(N2):
         v2[i] = v2[i] + e2[i]
     two = (f2, given["ax2"], given["ay2"], given["az2"], given["inv2"])
@@ -546,7 +561,7 @@
         for k in range(H0):
             for half in range(2):
                 lanes = slice(128 * half, 128 * half + 128)
-                vB[at + k, :, lanes] = beside[side, 16 + 2 * k + half] + e0[(at + k + 1) // 2, :, lanes]
+                vB[at + k, :, lanes] = received(side, 16 + 2 * k + half, 1)[0] + e0[(at + k + 1) // 2, :, lanes]
     for k in range(2):
         sweep_packed(lv, True, 1 + 2 * k, N0 - 1 - 2 * k)
         sweep_packed(lv, False, 2 + 2 * k, N0 - 2 - 2 * k)
@@ -596,32 +611,34 @@
     return a.reshape(8, 4, 2, 8, 128).transpose(0, 1, 3, 2, 4).reshape(8, 32, 256)
 
 
+def exchange(first, second):
+    boxes = lax.axis_size("box")
+    odd = [(i, i + 1) for i in range(1, boxes - 1, 2)]
+    even = [(i, i + 1) for i in range(0, boxes - 1, 2)]
+    return [lax.ppermute(x, "box", p + [(j, i) for i, j in p]) for x, p in ((first, odd), (second, even))]
+
+
 def body(pressure_guess, right_side, coefficient):
     boxes = lax.axis_size("box")
-    both = [(2 * i, 2 * i + 2) for i in range(boxes - 1)] + [(2 * i + 3, 2 * i + 1) for i in range(boxes - 1)]
-
     flat = [by_tiles(a) for a in (pressure_guess, right_side, coefficient)]
     first, second = edges(*flat)
     low, high = call(pack_kernel, [(16 * ROWS, 256)] * 2, [], *flat)
-    odd_pairs = [(i, i + 1) for i in range(1, boxes - 1, 2)]
-    even_pairs = [(i, i + 1) for i in range(0, boxes - 1, 2)]
-    first = lax.ppermute(first, "box", odd_pairs + [(j, i) for i, j in odd_pairs])
-    second = lax.ppermute(second, "box", even_pairs + [(j, i) for i, j in even_pairs])
+    first, second = exchange(first, second)
     low, high = lax.all_gather(low, "slab"), lax.all_gather(high, "slab")
     halo = lax.all_gather(jnp.stack([first, second]), "slab")
 
     plane = (N0, 8, 256)
     fine = call(
         functools.partial(fine_kernel, boxes),
-        [plane] * len(PACKED) + [(40, 8, 128), (SEND1, 8, 128), (8, 128)],
+        [plane] * len(PACKED) + [(36, 8, 128), (SEND1, 8, 128), (SEND1, 8, 128), (8, 128)],
         [plane] * 3 + [(16, 8, 256)] * 2 + [(64, 128)],
         low,
         high,
         halo,
     )
     level0 = fine[: len(PACKED)]
-    own, send, bottom = fine[len(PACKED) :]
-    halo = lax.all_gather(lax.ppermute(send, ("box", "slab"), both), "slab")
+    own, first, second, bottom = fine[len(PACKED) :]
+    first, second = exchange(first, second)
 
     one, two = (N1, 8, 128), (N2, 8, 128)
     *levels, send, message = call(
@@ -629,12 +646,12 @@
         [one] * 6 + [two] * 4 + [(16, 8, 128), (2 * boxes, 128)],
         [two] * 3 + [one, (128, 128)],
         own,
-        halo,
+        first,
+        second,
         bottom,
     )
     spread = lax.all_to_all(message.reshape(boxes, 2, 128), "box", 0, 0).reshape(2 * boxes, 128)
-    (late,) = call(after_kernel, [(16 + 2 * H0, 8, 128)], [], send, level0[0], spread)
-    beside = lax.ppermute(late, ("box", "slab"), both)
+    first, second = exchange(*call(after_kernel, [(SEND2, 8, 128)] * 2, [], send, level0[0], spread))
     gathered = lax.all_gather(spread, "slab")
     (e2,) = call(
         functools.partial(coarse_kernel, boxes),
@@ -642,13 +659,13 @@
         [(2, boxes, 128), (2, boxes, 128), (2, boxes + 16, 128)],
         gathered,
     )
-    beside = lax.all_gather(beside, "slab")
     pressure, residual = call(
         last_kernel,
         [(512, 128)] * 2,
         [plane, plane, one, two, two, (128, 128), (22, 8, 256)],
         e2,
-        beside,
+        first,
+        second,
         send,
         *levels,
         *level0,

time: 76.8 us -> 74.1 us (0.965)
  blocking collectives: 48.1 us -> 42.9 us
  starting transfers between devices: 7.83 us -> 11.7 us
  waiting for transfers between devices: 4.47 us -> 3 us
    all_gather x2 -> x0, blocking collectives: 3.95 us -> none  [the longest x1 1.99 us: body(): halo = lax.all_gather(lax.ppermute(send, ('box', 'slab'), both), 'slab')]
    ppermute x4 -> x6, starting transfers between devices: 7.83 us -> 11.7 us  [exchange(): lax.ppermute(x, 'box', p + [(j, i) for i, j in p])]
    ppermute x4 -> x6, waiting for transfers between devices: 4.47 us -> 3 us  [exchange(): lax.ppermute(x, 'box', p + [(j, i) for i, j in p])]
    all_to_all x1, blocking collectives: 31.7 us -> 30.7 us  [body(): lax.all_to_all(message.reshape(boxes, 2, 128), 'box', 0, 0)]
  transfers between devices with their start and end apart: 4 -> 6, of which waited for: 1 -> 1; matrix products, arithmetic and copies ran while one was open for 0% -> 0% of each run, Pallas kernels for 6% -> 6%
where the time goes in v7:
time: 74.1 us; the launch traced here: 73.5 us
  blocking collectives  42.9 us (58%)
  Pallas kernels  15.1 us (20%)
  starting transfers between devices  11.7 us (16%)
  waiting for transfers between devices  3 us (4%)
    all_to_all x1, blocking collectives, body(): lax.all_to_all(message.reshape(boxes, 2, 128), 'box', 0, 0)  30.7 us
    pallas_call x6, Pallas kernels, call(): pl.pallas_call(kernel, out_shape=[jax.ShapeDtypeStruct(s, F32) for s in o...  13.2 us
    ppermute x6, starting transfers between devices, exchange(): lax.ppermute(x, 'box', p + [(j, i) for i, j in p])  11.7 us
    all_gather x2, blocking collectives, body(): low, high = (lax.all_gather(low, 'slab'), lax.all_gather(high, 'slab'))  5.59 us
    all_gather x1, blocking collectives, body(): gathered = lax.all_gather(spread, 'slab')  4.53 us
    ppermute x6, waiting for transfers between devices, exchange(): lax.ppermute(x, 'box', p + [(j, i) for i, j in p])  3 us
    all_gather x1, blocking collectives, body(): halo = lax.all_gather(jnp.stack([first, second]), 'slab')  2.16 us
    pallas_call x1, Pallas kernels, edges(): pl.pallas_call(edge_kernel, out_shape=[jax.ShapeDtypeStruct((EDGE, 256),...  1.98 us
  transfers between devices with their start and end apart: 6, of which 1 were waited for; matrix products, arithmetic and copies ran while one was open for 0% of the time, Pallas kernels for 6%

profile of v7, /device:TPU:1, one launch (start us, length us, event | category | flops | bytes accessed | tf_op | source)
XLA Modules:
  0.0 73.5 jit_solution(18280372823751850822)
XLA Ops:
  0.6 0.0 copy-start
  0.6 0.0 copy-start.1
  0.6 0.0 copy-start.2
  0.7 2.0 %shard_map.51 = (f32[120,256]{1,0:T(8,128)}, f32[120,256]{1,0:T(8,128)}) custom-call(f32[8,64,128]{2,1,0:T(8,128)} %bitcast.44, f32[8,64,128]{2,1,0:T(8,128)} %bitcast.46, f32[8,64,128]{2,1,0:T(8,128)} %bitcast.48), custom_call_target="tpu_custom_call" | custom-call | tf_op jit(solution)/shard_map/pallas_call | solution.py:596
  2.6 0.7 collective-permute-start
  3.3 4.6 %collective-permute-start.1 = (f32[120,256]{1,0:T(8,128)}, f32[120,256]{1,0:T(8,128)S(1)}, u32[]{:S(2)}, u32[]{:S(2)}) collective-permute-start(f32[120,256]{1,0:T(8,128)} %get-tuple-element.42), channel_id=1, source_target_pairs={{0,2},{4,6},{8,10},{12,14},{16,18},{20,22},{24,26},{28,30},{32,34}... | collective-permute-start | bytes 368648 | tf_op jit(solution)/shard_map/ppermute | solution.py:618
  7.9 0.0 copy-done
  7.9 0.0 copy-done.1
  7.9 0.0 copy-done.2
  7.9 0.5 shard_map.50
  8.4 3.2 %all-gather = f32[768,256]{1,0:T(8,128)S(1)} all-gather(f32[384,256]{1,0:T(8,128)S(1)} %get-tuple-element.39), channel_id=2, replica_groups=mesh['box'=128,'slab'=2] {'slab'}, dimensions={0}, use_global_device_ids=true | all-gather | bytes 1179648 | tf_op jit(solution)/shard_map/all_gather | solution.py:627
  11.7 2.4 %all-gather.1 = f32[768,256]{1,0:T(8,128)S(1)} all-gather(f32[384,256]{1,0:T(8,128)S(1)} %get-tuple-element.40), channel_id=3, replica_groups=mesh['box'=128,'slab'=2] {'slab'}, dimensions={0}, use_global_device_ids=true | all-gather | bytes 1179648 | tf_op jit(solution)/shard_map/all_gather | solution.py:627
  14.0 0.0 collective-permute-done
  14.0 0.0 collective-permute-done.1
  14.0 2.2 %all-gather.2 = f32[4,120,256]{2,1,0:T(8,128)S(1)} all-gather(f32[2,120,256]{2,1,0:T(8,128)S(1)} %pad_maximum_fusion), channel_id=4, replica_groups=mesh['box'=128,'slab'=2] {'slab'}, dimensions={0}, use_global_device_ids=true | all-gather | bytes 737280 | tf_op jit(solution)/shard_map/all_gather | solution.py:628
  16.2 2.8 %shard_map.52 = (f32[42,8,256]{2,1,0:T(8,128)S(1)}, f32[42,8,256]{2,1,0:T(8,128)S(1)}, f32[42,8,256]{2,1,0:T(8,128)S(1)}, f32[42,8,256]{2,1,0:T(8,128)S(1)}, f32...) custom-call(f32[2,384,256]{2,1,0:T(8,128)S(1)} %bitcast.39, ...), custom_call_target="tpu_custom_call" | custom-call | tf_op jit(solution)/shard_map/pallas_call | solution.py:585
  19.0 0.7 collective-permute-start.2
  19.7 3.5 %collective-permute-start.3 = (f32[29,8,128]{2,1,0:T(8,128)S(1)}, f32[29,8,128]{2,1,0:T(8,128)S(1)}, u32[]{:S(2)}, u32[]{:S(2)}) collective-permute-start(f32[29,8,128]{2,1,0:T(8,128)S(1)} %get-tuple-element.45), channel_id=1, source_target_pairs={{0,2},{4,6},{8,10},{12,14},{16,18},{20,22},{24,26},{28,30},{32,34}... | collective-permute-start | bytes 356360 | tf_op jit(solution)/shard_map/ppermute | solution.py:618
  23.2 0.0 collective-permute-done.2.first
  23.2 3.0 %collective-permute-done.3.second = f32[29,8,128]{2,1,0:T(8,128)S(1)} collective-permute-done((f32[29,8,128]{2,1,0:T(8,128)S(1)}, f32[29,8,128]{2,1,0:T(8,128)S(1)}, u32[]{:S(2)}, u32[]{:S(2)}) %collective-permute-start.3) | collective-permute-done | bytes 118816 | tf_op jit(solution)/shard_map/ppermute | solution.py:618
  26.2 1.8 %shard_map.53 = (f32[42,8,128]{2,1,0:T(8,128)S(1)}, f32[42,8,128]{2,1,0:T(8,128)S(1)}, f32[42,8,128]{2,1,0:T(8,128)S(1)}, f32[42,8,128]{2,1,0:T(8,128)S(1)}, f32...) custom-call(f32[36,8,128]{2,1,0:T(8,128)S(1)} %get-tuple-element.43., ...), custom_call_target="tpu_custom_call" | custom-call | tf_op jit(solution)/shard_map/pallas_call | solution.py:585
  28.0 30.7 %all_to_all.5 = f32[128,2,128]{2,1,0:T(2,128)S(1)} all-to-all(f32[128,2,128]{2,1,0:T(2,128)S(1)} %bitcast.50), channel_id=1, replica_groups=mesh['box'=128,'slab'=2] {'box'}, dimensions={0} | all-to-all | bytes 262144 | tf_op jit(solution)/shard_map/all_to_all | solution.py:653
  58.7 0.7 collective-permute-start.4
  59.4 1.7 %collective-permute-start.5 = (f32[26,8,128]{2,1,0:T(8,128)S(1)}, f32[26,8,128]{2,1,0:T(8,128)S(1)}, u32[]{:S(2)}, u32[]{:S(2)}) collective-permute-start(f32[26,8,128]{2,1,0:T(8,128)S(1)} %get-tuple-element.51), channel_id=1, source_target_pairs={{0,2},{4,6},{8,10},{12,14},{16,18},{20,22},{24,26},{28,30},{32,34}... | collective-permute-start | bytes 319496 | tf_op jit(solution)/shard_map/ppermute | solution.py:618
  61.0 4.5 %all_gather.27.gathered = f32[2,256,128]{2,1,0:T(8,128)S(1)} all-gather(f32[1,256,128]{2,1,0:T(8,128)S(1)} %bitcast.43), channel_id=1, replica_groups=mesh['box'=128,'slab'=2] {'slab'}, dimensions={0}, use_global_device_ids=true | all-gather | bytes 393216 | tf_op jit(solution)/shard_map/all_gather | solution.py:655
  65.6 4.0 %shard_map.54.refs_0_ = f32[24,8,128]{2,1,0:T(8,128)S(1)} custom-call(f32[2,256,128]{2,1,0:T(8,128)S(1)} %all_gather.27.gathered), custom_call_target="tpu_custom_call" | custom-call | tf_op jit(solution)/shard_map/pallas_call | solution.py:585
  69.6 0.0 collective-permute-done.4.refs_1_
  69.6 0.0 collective-permute-done.5.refs_2_
  69.6 3.9 %shard_map.56 = (f32[512,128]{1,0:T(8,128)}, f32[512,128]{1,0:T(8,128)}) custom-call(f32[24,8,128]{2,1,0:T(8,128)S(1)} %shard_map.54.refs_0_, f32[26,8,128]{2,1,0:T(8,128)S(1)} %collective-permute-done.4.refs_1_, f32[26,8,128]{2,1,0:T(8,128)S(1)} %collective-permute-done.5.refs_2_, f32[16,8,128]{2,1,0:T(8,128)S(1)} %get-tuple-element.48.send.refs_3_, ...), custom_call_target="tpu_custom_call" | custom-call | tf_op jit(solution)/shard_map/pallas_call | solution.py:585
  (2 shorter events, 0.0 us)
Async XLA Ops:
  0.6 7.3 %copy-start = (f32[8,32,256]{2,1,0:T(8,128)S(1)}, f32[8,32,256]{2,1,0:T(8,128)}, u32[]{:S(2)}) copy-start(f32[8,32,256]{2,1,0:T(8,128)} %param.3) | copy-start | bytes 786436
  0.6 7.3 %copy-start.1 = (f32[8,32,256]{2,1,0:T(8,128)S(1)}, f32[8,32,256]{2,1,0:T(8,128)}, u32[]{:S(2)}) copy-start(f32[8,32,256]{2,1,0:T(8,128)} %param.4) | copy-start | bytes 786436
  0.6 7.3 %copy-start.2 = (f32[8,32,256]{2,1,0:T(8,128)S(1)}, f32[8,32,256]{2,1,0:T(8,128)}, u32[]{:S(2)}) copy-start(f32[8,32,256]{2,1,0:T(8,128)} %param.5) | copy-start | bytes 786436
  2.6 11.4 %collective-permute-start = (f32[120,256]{1,0:T(8,128)}, f32[120,256]{1,0:T(8,128)S(1)}, u32[]{:S(2)}, u32[]{:S(2)}) collective-permute-start(f32[120,256]{1,0:T(8,128)} %get-tuple-element.41), channel_id=1, source_target_pairs={{2,4},{6,8},{10,12},{14,16},{18,20},{22,24},{26,28},{30,32},{34,36... | collective-permute-start | bytes 368648 | tf_op jit(solution)/shard_map/ppermute | solution.py:618
  3.3 10.7 %collective-permute-start.1 = (f32[120,256]{1,0:T(8,128)}, f32[120,256]{1,0:T(8,128)S(1)}, u32[]{:S(2)}, u32[]{:S(2)}) collective-permute-start(f32[120,256]{1,0:T(8,128)} %get-tuple-element.42), channel_id=1, source_target_pairs={{0,2},{4,6},{8,10},{12,14},{16,18},{20,22},{24,26},{28,30},{32,34}... | collective-permute-start | bytes 368648 | tf_op jit(solution)/shard_map/ppermute | solution.py:618
  19.0 4.1 %collective-permute-start.2 = (f32[29,8,128]{2,1,0:T(8,128)S(1)}, f32[29,8,128]{2,1,0:T(8,128)S(1)}, u32[]{:S(2)}, u32[]{:S(2)}) collective-permute-start(f32[29,8,128]{2,1,0:T(8,128)S(1)} %get-tuple-element.44), channel_id=1, source_target_pairs={{2,4},{6,8},{10,12},{14,16},{18,20},{22,24},{26,28},{30,32},{34,36... | collective-permute-start | bytes 356360 | tf_op jit(solution)/shard_map/ppermute | solution.py:618
  19.7 6.4 %collective-permute-start.3 = (f32[29,8,128]{2,1,0:T(8,128)S(1)}, f32[29,8,128]{2,1,0:T(8,128)S(1)}, u32[]{:S(2)}, u32[]{:S(2)}) collective-permute-start(f32[29,8,128]{2,1,0:T(8,128)S(1)} %get-tuple-element.45), channel_id=1, source_target_pairs={{0,2},{4,6},{8,10},{12,14},{16,18},{20,22},{24,26},{28,30},{32,34}... | collective-permute-start | bytes 356360 | tf_op jit(solution)/shard_map/ppermute | solution.py:618
  58.7 10.9 %collective-permute-start.4 = (f32[26,8,128]{2,1,0:T(8,128)S(1)}, f32[26,8,128]{2,1,0:T(8,128)S(1)}, u32[]{:S(2)}, u32[]{:S(2)}) collective-permute-start(f32[26,8,128]{2,1,0:T(8,128)S(1)} %get-tuple-element.50), channel_id=1, source_target_pairs={{2,4},{6,8},{10,12},{14,16},{18,20},{22,24},{26,28},{30,32},{34,36... | collective-permute-start | bytes 319496 | tf_op jit(solution)/shard_map/ppermute | solution.py:618
  59.4 10.2 %collective-permute-start.5 = (f32[26,8,128]{2,1,0:T(8,128)S(1)}, f32[26,8,128]{2,1,0:T(8,128)S(1)}, u32[]{:S(2)}, u32[]{:S(2)}) collective-permute-start(f32[26,8,128]{2,1,0:T(8,128)S(1)} %get-tuple-element.51), channel_id=1, source_target_pairs={{0,2},{4,6},{8,10},{12,14},{16,18},{20,22},{24,26},{28,30},{32,34}... | collective-permute-start | bytes 319496 | tf_op jit(solution)/shard_map/ppermute | solution.py:618

commit v8 on v7

--- a/solution.py
+++ b/solution.py
@@ -16,11 +16,12 @@
 N0 = 32 + 2 * H0
 N1 = 16 + 2 * (H1 + 1)
 N2 = 24
-ROWS = 24
-EDGE = H0 * ROWS
-SWEEP, FACES, RESTRICT, MERGE, FINISH = 99, 99, 16, 16, 99
+ROWS = 20
+EDGE = 96
+EDGE_F, EDGE_V = 8 * H0, 16 * H0 - 8
+SWEEP, FACES, RESTRICT, FINISH = 99, 99, 16, 99
 SEND1 = H1 + (H1 + 1) + 4
-SEND2 = 16 + 2 * H0
+SEND2 = 4 + 2 * H0
 
 
 def matmul(x, m):
@@ -71,58 +72,70 @@
     return pl.ds((x // 8) * 16 + half * 8 + x % 8 + 64 * odd, 4, stride=128)
 
 
-def pack_plane(g, r, c, x, rows, even_y, out, base):
+def pack_plane(g, r, c, x, rows, even_y, out, b_at, f_at, v_at):
     p0 = even_y if x % 2 == 0 else jnp.logical_not(even_y)
     for half in range(2):
         lanes = slice(128 * half, 128 * half + 128)
         even, odd = rows(half, 0), rows(half, 1)
-        out[base : base + 4, lanes] = c[even, :]
-        out[base + 4 : base + 8, lanes] = c[odd, :]
-        fe, fo = r[even, :], r[odd, :]
-        out[base + 8 : base + 12, lanes] = jnp.where(p0, fe, fo)
-        out[base + 12 : base + 16, lanes] = jnp.where(p0, fo, fe)
-        out[base + 16 : base + 20, lanes] = jnp.where(p0, g[odd, :], g[even, :])
-        out[base + 20 : base + 24, lanes] = jnp.zeros((4, 128), F32)
-
-
-def pack_kernel(g, r, c, low, high):
+        out[b_at : b_at + 4, lanes] = c[even, :]
+        out[b_at + 4 : b_at + 8, lanes] = c[odd, :]
+        if f_at is not None:
+            fe, fo = r[even, :], r[odd, :]
+            out[f_at : f_at + 4, lanes] = jnp.where(p0, fe, fo)
+            out[f_at + 4 : f_at + 8, lanes] = jnp.where(p0, fo, fe)
+        out[v_at : v_at + 4, lanes] = jnp.where(p0, g[odd, :], g[even, :])
+
+
+def pack_edge(parts, right, rows, even_y, out):
+    for k in range(H0):
+        x = 32 - H0 + k if right else k
+        f_at = k - 1 if right else k
+        f_at = EDGE_F + 8 * f_at if 0 <= f_at < H0 - 1 else None
+        pack_plane(*parts, x, functools.partial(rows, x), even_y, out, 8 * k, f_at, EDGE_V + 4 * k)
+    out[EDGE_V + 4 * H0 :, :] = jnp.zeros((EDGE - EDGE_V - 4 * H0, 256), F32)
+
+
+def pack_kernel(g, r, c, low, high, second):
     even_y = (iota((4, 128), 1) & 1) == 0
+    swapped = (my_place()[1] & 1) == 1
+
+    @pl.when(swapped)
+    def _():
+        pack_edge((g, r, c), False, slab_rows, even_y, second)
+
+    @pl.when(jnp.logical_not(swapped))
+    def _():
+        pack_edge((g, r, c), True, slab_rows, even_y, second)
+
     for x in range(32):
         out, base = (low, x * ROWS) if x < 16 else (high, (x - 16) * ROWS)
-        pack_plane(g, r, c, x, functools.partial(slab_rows, x), even_y, out, base)
-
-
-def edge_kernel(g_hbm, r_hbm, c_hbm, first, second, *scratch):
-    left, right, sem = scratch[0:3], scratch[3:6], scratch[6]
-    copies = []
-    for k, source in enumerate((g_hbm, r_hbm, c_hbm)):
-        for side, (target, at) in enumerate(((left[k], 0), (right[k], 48))):
-            copies.append(
-                pltpu.make_async_copy(source.at[:, at : at + 16, :], target.reshape(8, 16, 128), sem.at[2 * k + side])
-            )
+        pack_plane(g, r, c, x, functools.partial(slab_rows, x), even_y, out, base, base + 8, base + 16)
+
+
+def edge_kernel(g_hbm, r_hbm, c_hbm, first, *scratch):
+    parts, sem = scratch[0:3], scratch[3]
+    odd = my_place()[1] & 1
+    at = pl.multiple_of(48 * odd, 16)
+    copies = [
+        pltpu.make_async_copy(source.at[:, pl.ds(at, 16), :], target.reshape(8, 16, 128), sem.at[k])
+        for k, (source, target) in enumerate(zip((g_hbm, r_hbm, c_hbm), parts))
+    ]
     for copy in copies:
         copy.start()
     for copy in copies:
         copy.wait()
     even_y = (iota((4, 128), 1) & 1) == 0
 
-    def pack(parts, start, out):
-        for k in range(H0):
-            x = start + k
-            rows = lambda half, odd, x=x: pl.ds(half * 8 + x % 8 + 16 * odd, 4, stride=32)
-            pack_plane(*parts, x, rows, even_y, out, k * ROWS)
-
-    right_first = (my_place()[1] & 1) == 1
-
-    @pl.when(right_first)
+    def rows(x, half, second_z):
+        return pl.ds(half * 8 + x % 8 + 16 * second_z, 4, stride=32)
+
+    @pl.when(odd == 1)
     def _():
-        pack(right, 32 - H0, first)
-        pack(left, 0, second)
-
-    @pl.when(jnp.logical_not(right_first))
+        pack_edge(parts, True, rows, even_y, first)
+
+    @pl.when(odd == 0)
     def _():
-        pack(left, 0, first)
-        pack(right, 32 - H0, second)
+        pack_edge(parts, False, rows, even_y, first)
 
 
 def parity(odd):
@@ -176,23 +189,28 @@
     row, lane = iota((8, 256), 0), iota((8, 256), 1)
     low_half = row < 4
 
-    def merge(part0, part1, count, first):
-        def step(k, carry):
-            base = pl.multiple_of(k * ROWS, 8) if not isinstance(k, int) else k * ROWS
-            i = first + k
-            for at, (low, high) in enumerate(((bE, bO), (lv["fR"], lv["fB"]), (lv["vB"], None))):
-                a, b = part0[pl.ds(base + 8 * at, 8), :], part1[pl.ds(base + 8 * at, 8), :]
-                low[i] = jnp.where(low_half, a, pltpu.roll(b, 4, 0))
-                if high is not None:
-                    high[i] = jnp.where(low_half, pltpu.roll(a, 4, 0), b)
-            return carry
-
-        lax.fori_loop(0, count, step, 0, unroll=min(count, MERGE))
-
-    merge(halo.at[0, odd], halo.at[1, odd], H0, 0)
-    merge(lo.at[0], lo.at[1], 16, H0)
-    merge(hi.at[0], hi.at[1], 16, H0 + 16)
-    merge(halo.at[0, 1 - odd], halo.at[1, 1 - odd], H0, H0 + 32)
+    def merge(parts, at, i, low, high):
+        a, b = (part[at : at + 8, :] for part in parts)
+        low[i] = jnp.where(low_half, a, pltpu.roll(b, 4, 0))
+        high[i] = jnp.where(low_half, pltpu.roll(a, 4, 0), b)
+
+    def stack(parts, at, i, out):
+        for t in range(2):
+            out[i, 4 * t : 4 * t + 4, :] = parts[t][at : at + 4, :]
+
+    for x in range(32):
+        source, base = (lo, x * ROWS) if x < 16 else (hi, (x - 16) * ROWS)
+        parts = source.at[0], source.at[1]
+        merge(parts, base, H0 + x, bE, bO)
+        merge(parts, base + 8, H0 + x, lv["fR"], lv["fB"])
+        stack(parts, base + 16, H0 + x, lv["vB"])
+    for side, at in ((odd, 0), (1 - odd, H0 + 32)):
+        parts = halo.at[0, side], halo.at[1, side]
+        for k in range(H0):
+            merge(parts, 8 * k, at + k, bE, bO)
+            stack(parts, EDGE_V + 4 * k, at + k, lv["vB"])
+        for k in range(H0 - 1):
+            merge(parts, EDGE_F + 8 * k, (1 if at == 0 else at) + k, lv["fR"], lv["fB"])
 
     top, bot = row == 7, row == 0
     end, begin = lane == 255, lane == 0
@@ -340,7 +358,7 @@
     return factor * (4.0 * v + fy + fz) + (ax[i] + ax[i - 1])
 
 
-def middle_kernel(boxes, own, first, second, bottom, v1, f1, ax1, ay1, az1, inv1, ax2, ay2, az2, inv2, send, message, v2, f2, b2, b1, tmp):
+def middle_kernel(boxes, own, first, second, bottom, v1, f1, ax1, ay1, az1, inv1, ax2, ay2, az2, inv2, send, compact, message, v2, f2, b2, b1, tmp):
     box = my_place()[1]
     w = H1 + 1
     swapped = (box & 1) == 1
@@ -405,6 +423,9 @@
     sweep_plain(v2, *two, 1, 0, 7, 17)
     send[0:8] = v2[8:16]
     send[8:16] = f2[8:16]
+    for k in range(4):
+        both = [pltpu.roll(ref[9 + 2 * k], 4, 0) + ref[8 + 2 * k] for ref in (v2, f2)]
+        compact[k] = both[0] + pltpu.roll(both[1], 64, 1)
 
     pairs = []
     for k in range(4):
@@ -477,7 +498,7 @@
             dref[t] = q[t] + beta * d[t]
         return later
 
-    lax.fori_loop(0, ITERS, iterate, total(source, source))
+    lax.fori_loop(0, ITERS, iterate, total(source, source), unroll=True)
 
 
 def coarse_kernel(boxes, gathered, e2, dref, qref, eref):
@@ -495,15 +516,15 @@
         e2[i] = jnp.where(row < 2, low, jnp.where(row < 4, high, 0.0))
 
 
-def after_kernel(send, black, gathered, first, second):
+def after_kernel(compact, black, gathered, first, second):
     del gathered
     odd = my_place()[1] & 1
     for out, right in ((first, odd), (second, 1 - odd)):
-        out[0:16] = send[...]
+        out[0:4] = compact[...]
         start = H0 + right * (32 - H0)
         for k in range(H0):
             for half in range(2):
-                out[16 + 2 * k + half] = black[start + k, :, 128 * half : 128 * half + 128]
+                out[4 + 2 * k + half] = black[start + k, :, 128 * half : 128 * half + 128]
 
 
 def last_kernel(*refs):
@@ -521,10 +542,15 @@
         one, two = (first, second) if side == 0 else (second, first)
         return jnp.where(swapped, two[k : k + count], one[k : k + count])
 
-    for ref, part in ((v2, 0), (f2, 8)):
-        ref[0:8] = received(0, part, 8)
-        ref[8:16] = own2[part : part + 8]
-        ref[16:24] = received(1, part, 8)
+    v2[8:16] = own2[0:8]
+    f2[8:16] = own2[8:16]
+    quarter = jnp.logical_and(iota((8, 128), 0) < 4, iota((8, 128), 1) < 64)
+    for side, at in ((0, 0), (1, 16)):
+        four = received(side, 0, 4)
+        for k in range(4):
+            for ref, plane in ((v2, four[k]), (f2, pltpu.roll(four[k], 64, 1))):
+                ref[at + 2 * k] = jnp.where(quarter, plane, 0.0)
+                ref[at + 2 * k + 1] = jnp.where(quarter, pltpu.roll(plane, 4, 0), 0.0)
     for i in range(N2):
         v2[i] = v2[i] + e2[i]
     two = (f2, given["ax2"], given["ay2"], given["az2"], given["inv2"])
@@ -561,7 +587,7 @@
         for k in range(H0):
             for half in range(2):
                 lanes = slice(128 * half, 128 * half + 128)
-                vB[at + k, :, lanes] = received(side, 16 + 2 * k + half, 1)[0] + e0[(at + k + 1) // 2, :, lanes]
+                vB[at + k, :, lanes] = received(side, 4 + 2 * k + half, 1)[0] + e0[(at + k + 1) // 2, :, lanes]
     for k in range(2):
         sweep_packed(lv, True, 1 + 2 * k, N0 - 1 - 2 * k)
         sweep_packed(lv, False, 2 + 2 * k, N0 - 2 - 2 * k)
@@ -595,10 +621,10 @@
 def edges(*args):
     return pl.pallas_call(
         edge_kernel,
-        out_shape=[jax.ShapeDtypeStruct((EDGE, 256), F32)] * 2,
+        out_shape=jax.ShapeDtypeStruct((EDGE, 256), F32),
         in_specs=[pl.BlockSpec(memory_space=pl.ANY)] * 3,
-        out_specs=[pl.BlockSpec(memory_space=pltpu.VMEM)] * 2,
-        scratch_shapes=[pltpu.VMEM((128, 128), F32)] * 6 + [pltpu.SemaphoreType.DMA((6,))],
+        out_specs=pl.BlockSpec(memory_space=pltpu.VMEM),
+        scratch_shapes=[pltpu.VMEM((128, 128), F32)] * 3 + [pltpu.SemaphoreType.DMA((3,))],
         compiler_params=pltpu.CompilerParams(vmem_limit_bytes=60 * 1024 * 1024),
     )(*[a.reshape(8, 64, 128) for a in args])
 
@@ -621,8 +647,8 @@
 def body(pressure_guess, right_side, coefficient):
     boxes = lax.axis_size("box")
     flat = [by_tiles(a) for a in (pressure_guess, right_side, coefficient)]
-    first, second = edges(*flat)
-    low, high = call(pack_kernel, [(16 * ROWS, 256)] * 2, [], *flat)
+    first = edges(*flat)
+    low, high, second = call(pack_kernel, [(16 * ROWS, 256)] * 2 + [(EDGE, 256)], [], *flat)
     first, second = exchange(first, second)
     low, high = lax.all_gather(low, "slab"), lax.all_gather(high, "slab")
     halo = lax.all_gather(jnp.stack([first, second]), "slab")
@@ -641,9 +667,9 @@
     first, second = exchange(first, second)
 
     one, two = (N1, 8, 128), (N2, 8, 128)
-    *levels, send, message = call(
+    *levels, send, compact, message = call(
         functools.partial(middle_kernel, boxes),
-        [one] * 6 + [two] * 4 + [(16, 8, 128), (2 * boxes, 128)],
+        [one] * 6 + [two] * 4 + [(16, 8, 128), (4, 8, 128), (2 * boxes, 128)],
         [two] * 3 + [one, (128, 128)],
         own,
         first,
@@ -651,7 +677,7 @@
         bottom,
     )
     spread = lax.all_to_all(message.reshape(boxes, 2, 128), "box", 0, 0).reshape(2 * boxes, 128)
-    first, second = exchange(*call(after_kernel, [(SEND2, 8, 128)] * 2, [], send, level0[0], spread))
+    first, second = exchange(*call(after_kernel, [(SEND2, 8, 128)] * 2, [], compact, level0[0], spread))
     gathered = lax.all_gather(spread, "slab")
     (e2,) = call(
         functools.partial(coarse_kernel, boxes),

time: 74.1 us -> 73.2 us (0.988)
  no operation moved by 1% of the time
where the time goes in v8:
time: 73.2 us; the launch traced here: 72.7 us
  blocking collectives  42.5 us (58%)
  Pallas kernels  14.7 us (20%)
  starting transfers between devices  11.7 us (16%)
  waiting for transfers between devices  3.01 us (4%)
  between operations  0.75 us (1%)
    all_to_all x1, blocking collectives, body(): lax.all_to_all(message.reshape(boxes, 2, 128), 'box', 0, 0)  30.3 us
    pallas_call x6, Pallas kernels, call(): pl.pallas_call(kernel, out_shape=[jax.ShapeDtypeStruct(s, F32) for s in o...  13 us
    ppermute x6, starting transfers between devices, exchange(): lax.ppermute(x, 'box', p + [(j, i) for i, j in p])  11.7 us
    all_gather x2, blocking collectives, body(): low, high = (lax.all_gather(low, 'slab'), lax.all_gather(high, 'slab'))  5.39 us
    all_gather x1, blocking collectives, body(): gathered = lax.all_gather(spread, 'slab')  4.71 us
    ppermute x6, waiting for transfers between devices, exchange(): lax.ppermute(x, 'box', p + [(j, i) for i, j in p])  3.01 us
    all_gather x1, blocking collectives, body(): halo = lax.all_gather(jnp.stack([first, second]), 'slab')  2.09 us
    pallas_call x1, Pallas kernels, edges(): pl.pallas_call(edge_kernel, out_shape=jax.ShapeDtypeStruct((EDGE, 256), F...  1.73 us
  transfers between devices with their start and end apart: 6, of which 1 were waited for; matrix products, arithmetic and copies ran while one was open for 0% of the time, Pallas kernels for 6%

profile of v8, /device:TPU:1, one launch (start us, length us, event | category | flops | bytes accessed | tf_op | source)
XLA Modules:
  0.0 72.7 jit_solution(12625929749446208400)
XLA Ops:
  0.6 0.0 copy-start
  0.6 0.0 copy-start.1
  0.6 0.0 copy-start.2
  0.7 1.7 %shard_map.51 = f32[96,256]{1,0:T(8,128)} custom-call(f32[8,64,128]{2,1,0:T(8,128)} %bitcast.44, f32[8,64,128]{2,1,0:T(8,128)} %bitcast.46, f32[8,64,128]{2,1,0:T(8,128)} %bitcast.48), custom_call_target="tpu_custom_call" | custom-call | tf_op jit(solution)/shard_map/pallas_call | solution.py:622
  2.4 0.7 collective-permute-start
  3.1 0.0 copy-done
  3.1 0.0 copy-done.1
  3.1 0.0 copy-done.2
  3.1 0.6 shard_map.50
  3.7 4.6 %collective-permute-start.1 = (f32[96,256]{1,0:T(8,128)S(1)}, f32[96,256]{1,0:T(8,128)S(1)}, u32[]{:S(2)}, u32[]{:S(2)}) collective-permute-start(f32[96,256]{1,0:T(8,128)S(1)} %get-tuple-element.41), channel_id=1, source_target_pairs={{0,2},{4,6},{8,10},{12,14},{16,18},{20,22},{24,26},{28,30},{32,34}... | collective-permute-start | bytes 294920 | tf_op jit(solution)/shard_map/ppermute | solution.py:644
  8.3 3.1 %all-gather = f32[640,256]{1,0:T(8,128)S(1)} all-gather(f32[320,256]{1,0:T(8,128)S(1)} %get-tuple-element.39), channel_id=2, replica_groups=mesh['box'=128,'slab'=2] {'slab'}, dimensions={0}, use_global_device_ids=true | all-gather | bytes 983040 | tf_op jit(solution)/shard_map/all_gather | solution.py:653
  11.4 2.3 %all-gather.1 = f32[640,256]{1,0:T(8,128)S(1)} all-gather(f32[320,256]{1,0:T(8,128)S(1)} %get-tuple-element.40), channel_id=3, replica_groups=mesh['box'=128,'slab'=2] {'slab'}, dimensions={0}, use_global_device_ids=true | all-gather | bytes 983040 | tf_op jit(solution)/shard_map/all_gather | solution.py:653
  13.7 0.0 collective-permute-done
  13.7 0.0 collective-permute-done.1
  13.7 2.1 %all-gather.2 = f32[4,96,256]{2,1,0:T(8,128)S(1)} all-gather(f32[2,96,256]{2,1,0:T(8,128)S(1)} %pad_maximum_fusion), channel_id=4, replica_groups=mesh['box'=128,'slab'=2] {'slab'}, dimensions={0}, use_global_device_ids=true | all-gather | bytes 589824 | tf_op jit(solution)/shard_map/all_gather | solution.py:654
  15.8 2.9 %shard_map.52 = (f32[42,8,256]{2,1,0:T(8,128)S(1)}, f32[42,8,256]{2,1,0:T(8,128)S(1)}, f32[42,8,256]{2,1,0:T(8,128)S(1)}, f32[42,8,256]{2,1,0:T(8,128)S(1)}, f32...) custom-call(f32[2,320,256]{2,1,0:T(8,128)S(1)} %bitcast.39, ...), custom_call_target="tpu_custom_call" | custom-call | tf_op jit(solution)/shard_map/pallas_call | solution.py:611
  18.7 0.7 collective-permute-start.2
  19.3 3.5 %collective-permute-start.3 = (f32[29,8,128]{2,1,0:T(8,128)S(1)}, f32[29,8,128]{2,1,0:T(8,128)S(1)}, u32[]{:S(2)}, u32[]{:S(2)}) collective-permute-start(f32[29,8,128]{2,1,0:T(8,128)S(1)} %get-tuple-element.44), channel_id=1, source_target_pairs={{0,2},{4,6},{8,10},{12,14},{16,18},{20,22},{24,26},{28,30},{32,34}... | collective-permute-start | bytes 356360 | tf_op jit(solution)/shard_map/ppermute | solution.py:644
  22.8 0.0 collective-permute-done.2.first
  22.8 3.0 %collective-permute-done.3.second = f32[29,8,128]{2,1,0:T(8,128)S(1)} collective-permute-done((f32[29,8,128]{2,1,0:T(8,128)S(1)}, f32[29,8,128]{2,1,0:T(8,128)S(1)}, u32[]{:S(2)}, u32[]{:S(2)}) %collective-permute-start.3) | collective-permute-done | bytes 118816 | tf_op jit(solution)/shard_map/ppermute | solution.py:644
  25.8 1.9 %shard_map.53 = (f32[42,8,128]{2,1,0:T(8,128)S(1)}, f32[42,8,128]{2,1,0:T(8,128)S(1)}, f32[42,8,128]{2,1,0:T(8,128)S(1)}, f32[42,8,128]{2,1,0:T(8,128)S(1)}, f32...) custom-call(f32[36,8,128]{2,1,0:T(8,128)S(1)} %get-tuple-element.42., ...), custom_call_target="tpu_custom_call" | custom-call | tf_op jit(solution)/shard_map/pallas_call | solution.py:611
  27.6 30.3 %all_to_all.5 = f32[128,2,128]{2,1,0:T(2,128)S(1)} all-to-all(f32[128,2,128]{2,1,0:T(2,128)S(1)} %bitcast.50), channel_id=1, replica_groups=mesh['box'=128,'slab'=2] {'box'}, dimensions={0} | all-to-all | bytes 262144 | tf_op jit(solution)/shard_map/all_to_all | solution.py:679
  58.0 0.7 collective-permute-start.4
  58.6 1.7 %collective-permute-start.5 = (f32[14,8,128]{2,1,0:T(8,128)S(1)}, f32[14,8,128]{2,1,0:T(8,128)S(1)}, u32[]{:S(2)}, u32[]{:S(2)}) collective-permute-start(f32[14,8,128]{2,1,0:T(8,128)S(1)} %get-tuple-element.50), channel_id=1, source_target_pairs={{0,2},{4,6},{8,10},{12,14},{16,18},{20,22},{24,26},{28,30},{32,34}... | collective-permute-start | bytes 172040 | tf_op jit(solution)/shard_map/ppermute | solution.py:644
  60.3 4.7 %all_gather.27.gathered = f32[2,256,128]{2,1,0:T(8,128)S(1)} all-gather(f32[1,256,128]{2,1,0:T(8,128)S(1)} %bitcast.43), channel_id=1, replica_groups=mesh['box'=128,'slab'=2] {'slab'}, dimensions={0}, use_global_device_ids=true | all-gather | bytes 393216 | tf_op jit(solution)/shard_map/all_gather | solution.py:681
  65.0 3.7 %shard_map.54.refs_0_ = f32[24,8,128]{2,1,0:T(8,128)S(1)} custom-call(f32[2,256,128]{2,1,0:T(8,128)S(1)} %all_gather.27.gathered), custom_call_target="tpu_custom_call" | custom-call | tf_op jit(solution)/shard_map/pallas_call | solution.py:611
  68.7 0.0 collective-permute-done.4.refs_1_
  68.7 0.0 collective-permute-done.5.refs_2_
  68.7 4.0 %shard_map.56 = (f32[512,128]{1,0:T(8,128)}, f32[512,128]{1,0:T(8,128)}) custom-call(f32[24,8,128]{2,1,0:T(8,128)S(1)} %shard_map.54.refs_0_, f32[14,8,128]{2,1,0:T(8,128)S(1)} %collective-permute-done.4.refs_1_, f32[14,8,128]{2,1,0:T(8,128)S(1)} %collective-permute-done.5.refs_2_, f32[16,8,128]{2,1,0:T(8,128)S(1)} %get-tuple-element.51.refs_3_, ...), custom_call_target="tpu_custom_call" | custom-call | tf_op jit(solution)/shard_map/pallas_call | solution.py:611
  (2 shorter events, 0.0 us)
Async XLA Ops:
  0.6 2.4 %copy-start = (f32[8,32,256]{2,1,0:T(8,128)S(1)}, f32[8,32,256]{2,1,0:T(8,128)}, u32[]{:S(2)}) copy-start(f32[8,32,256]{2,1,0:T(8,128)} %param.3) | copy-start | bytes 786436
  0.6 2.4 %copy-start.1 = (f32[8,32,256]{2,1,0:T(8,128)S(1)}, f32[8,32,256]{2,1,0:T(8,128)}, u32[]{:S(2)}) copy-start(f32[8,32,256]{2,1,0:T(8,128)} %param.4) | copy-start | bytes 786436
  0.6 2.4 %copy-start.2 = (f32[8,32,256]{2,1,0:T(8,128)S(1)}, f32[8,32,256]{2,1,0:T(8,128)}, u32[]{:S(2)}) copy-start(f32[8,32,256]{2,1,0:T(8,128)} %param.5) | copy-start | bytes 786436
  2.4 11.3 %collective-permute-start = (f32[96,256]{1,0:T(8,128)}, f32[96,256]{1,0:T(8,128)S(1)}, u32[]{:S(2)}, u32[]{:S(2)}) collective-permute-start(f32[96,256]{1,0:T(8,128)} %shard_map.51), channel_id=1, source_target_pairs={{2,4},{6,8},{10,12},{14,16},{18,20},{22,24},{26,28},{30,32},{34,36... | collective-permute-start | bytes 294920 | tf_op jit(solution)/shard_map/ppermute | solution.py:644
  3.7 10.0 %collective-permute-start.1 = (f32[96,256]{1,0:T(8,128)S(1)}, f32[96,256]{1,0:T(8,128)S(1)}, u32[]{:S(2)}, u32[]{:S(2)}) collective-permute-start(f32[96,256]{1,0:T(8,128)S(1)} %get-tuple-element.41), channel_id=1, source_target_pairs={{0,2},{4,6},{8,10},{12,14},{16,18},{20,22},{24,26},{28,30},{32,34}... | collective-permute-start | bytes 294920 | tf_op jit(solution)/shard_map/ppermute | solution.py:644
  18.7 4.1 %collective-permute-start.2 = (f32[29,8,128]{2,1,0:T(8,128)S(1)}, f32[29,8,128]{2,1,0:T(8,128)S(1)}, u32[]{:S(2)}, u32[]{:S(2)}) collective-permute-start(f32[29,8,128]{2,1,0:T(8,128)S(1)} %get-tuple-element.43), channel_id=1, source_target_pairs={{2,4},{6,8},{10,12},{14,16},{18,20},{22,24},{26,28},{30,32},{34,36... | collective-permute-start | bytes 356360 | tf_op jit(solution)/shard_map/ppermute | solution.py:644
  19.3 6.4 %collective-permute-start.3 = (f32[29,8,128]{2,1,0:T(8,128)S(1)}, f32[29,8,128]{2,1,0:T(8,128)S(1)}, u32[]{:S(2)}, u32[]{:S(2)}) collective-permute-start(f32[29,8,128]{2,1,0:T(8,128)S(1)} %get-tuple-element.44), channel_id=1, source_target_pairs={{0,2},{4,6},{8,10},{12,14},{16,18},{20,22},{24,26},{28,30},{32,34}... | collective-permute-start | bytes 356360 | tf_op jit(solution)/shard_map/ppermute | solution.py:644
  58.0 10.7 %collective-permute-start.4 = (f32[14,8,128]{2,1,0:T(8,128)S(1)}, f32[14,8,128]{2,1,0:T(8,128)S(1)}, u32[]{:S(2)}, u32[]{:S(2)}) collective-permute-start(f32[14,8,128]{2,1,0:T(8,128)S(1)} %get-tuple-element.49), channel_id=1, source_target_pairs={{2,4},{6,8},{10,12},{14,16},{18,20},{22,24},{26,28},{30,32},{34,36... | collective-permute-start | bytes 172040 | tf_op jit(solution)/shard_map/ppermute | solution.py:644
  58.6 10.0 %collective-permute-start.5 = (f32[14,8,128]{2,1,0:T(8,128)S(1)}, f32[14,8,128]{2,1,0:T(8,128)S(1)}, u32[]{:S(2)}, u32[]{:S(2)}) collective-permute-start(f32[14,8,128]{2,1,0:T(8,128)S(1)} %get-tuple-element.50), channel_id=1, source_target_pairs={{0,2},{4,6},{8,10},{12,14},{16,18},{20,22},{24,26},{28,30},{32,34}... | collective-permute-start | bytes 172040 | tf_op jit(solution)/shard_map/ppermute | solution.py:644

commit v9 on v8

--- a/solution.py
+++ b/solution.py
@@ -440,73 +440,80 @@
         message[8 * k : 8 * k + 8, :] = rows
 
 
-def coarse_solve(n, source, coefficient, dref, qref, eref):
-    row, lane = iota((n, 128), 0), iota((n, 128), 1)
+def coarse_solve(source, coefficient, dref, sref, rref, eref):
+    shape = source[0].shape
+    groups = shape[0]
+    group, row, lane = (iota(shape, k) for k in range(3))
     factor = 0.5 * 0.25**3
-    last = jnp.logical_and(row == n - 1, lane >= 96)
-    first = jnp.logical_and(row == 0, lane < 32)
+    last = jnp.logical_and(jnp.logical_and(group == groups - 1, row == 7), lane >= 96)
+    first = jnp.logical_and(jnp.logical_and(group == 0, row == 0), lane < 32)
     inner_hi, inner_lo = lane < 96, lane >= 32
     end, begin = (lane & 31) == 31, (lane & 31) == 0
 
+    def lanes(v, shift):
+        return pltpu.roll(v.reshape(8 * groups, 128), shift, 1).reshape(shape)
+
     def xp(v):
-        a = pltpu.roll(v, 96, 1)
-        return jnp.where(inner_hi, a, up(a, 0))
+        a = lanes(v, 96)
+        return jnp.where(inner_hi, a, jnp.concatenate([a[1:], up(a[0], 0)[None]], axis=0))
 
     def xm(v):
-        a = pltpu.roll(v, 32, 1)
-        return jnp.where(inner_lo, a, down(a, 0))
+        a = lanes(v, 32)
+        return jnp.where(inner_lo, a, jnp.concatenate([down(a[groups - 1], 0)[None], a[:-1]], axis=0))
 
     ax, ay, center = [], [], []
     az = factor * (coefficient[0] + coefficient[1])
     for b in coefficient:
         fx = factor * (b + jnp.where(last, 0.0, xp(b)))
         gx = factor * (b + jnp.where(first, 0.0, xm(b)))
-        fy = factor * (b + jnp.where(end, 0.0, up(b, 1)))
-        gy = factor * (b + jnp.where(begin, 0.0, down(b, 1)))
+        fy = factor * (b + jnp.where(end, 0.0, lanes(b, 127)))
+        gy = factor * (b + jnp.where(begin, 0.0, lanes(b, 1)))
         ax.append(jnp.where(last, 0.0, fx))
         ay.append(jnp.where(end, 0.0, fy))
         center.append((factor * b + az) + (fx + gx) + (fy + gy))
 
     def total(u, w):
-        s = u[0] * w[0] + u[1] * w[1]
+        s = jnp.sum(u[0] * w[0] + u[1] * w[1], axis=0)
         return jnp.sum(jnp.sum(s, axis=0, keepdims=True), axis=1, keepdims=True)
 
-    for t in range(2):
-        dref[t] = source[t]
-        qref[t] = source[t]
-        eref[t, 8 : 8 + n] = jnp.zeros((n, 128), F32)
-        eref[t, 0:8] = jnp.zeros((8, 128), F32)
-        eref[t, 8 + n :] = jnp.zeros((8, 128), F32)
-
-    def iterate(k, now):
-        d = (dref[0], dref[1])
+    before = alpha = None
+    for k in range(ITERS):
+        r = [source[t] if k == 0 else rref[t] for t in range(2)]
         w = []
         for t in range(2):
-            v = d[t]
-            s = ax[t] * xp(v) + xm(ax[t] * v)
-            s = s + (ay[t] * up(v, 1) + down(ay[t] * v, 1))
-            w.append(center[t] * v - (s + az * d[1 - t]))
-        alpha = now / total(d, w)
-        q = []
+            v = r[t]
+            n = ax[t] * xp(v) + xm(ax[t] * v)
+            n = n + (ay[t] * lanes(v, 127) + lanes(ay[t] * v, 1))
+            w.append(center[t] * v - (n + az * r[1 - t]))
+        rr, below = total(r, r), total(r, w)
+        if k > 0:
+            beta = rr / before
+            below = below - beta * (rr / alpha)
+        alpha = rr / below
+        before = rr
         for t in range(2):
-            eref[t, 8 : 8 + n] = eref[t, 8 : 8 + n] + alpha * d[t]
-            q.append(qref[t] - alpha * w[t])
-            qref[t] = q[t]
-        later = total(q, q)
-        beta = later / now
-        for t in range(2):
-            dref[t] = q[t] + beta * d[t]
-        return later
-
-    lax.fori_loop(0, ITERS, iterate, total(source, source), unroll=True)
-
-
-def coarse_kernel(boxes, gathered, e2, dref, qref, eref):
+            d, image = (r[t], w[t]) if k == 0 else (r[t] + beta * dref[t], w[t] + beta * sref[t])
+            eref[t] = alpha * d if k == 0 else eref[t] + alpha * d
+            if k < ITERS - 1:
+                dref[t] = d
+                sref[t] = image
+                rref[t] = r[t] - alpha * image
+
+
+def coarse_kernel(boxes, gathered, e2, dref, sref, rref, eref, ordered):
     box = my_place()[1]
-    source = [gathered[t, pl.ds(0, boxes, stride=2), :] for t in range(2)]
-    coefficient = [gathered[t, pl.ds(1, boxes, stride=2), :] for t in range(2)]
-    coarse_solve(boxes, source, coefficient, dref, qref, eref)
-    near = [eref[t, pl.ds(7 + box, 8), :] for t in range(2)]
+    groups = boxes // 8
+
+    def load(t, at):
+        return jnp.stack([gathered[t, pl.ds(2 * g + at, 8, stride=2 * groups), :] for g in range(groups)])
+
+    coarse_solve([load(t, 0) for t in range(2)], [load(t, 1) for t in range(2)], dref, sref, rref, eref)
+    for t in range(2):
+        ordered[t, 0:8] = jnp.zeros((8, 128), F32)
+        ordered[t, 8 + boxes :] = jnp.zeros((8, 128), F32)
+        for g in range(groups):
+            ordered[t, pl.ds(8 + g, 8, stride=groups), :] = eref[t, g]
+    near = [ordered[t, pl.ds(7 + box, 8), :] for t in range(2)]
     spread = one_hot((128, 512), lambda i, j: jnp.logical_and(((j >> 7) * 32) + ((j & 127) >> 1) == i, (j & 127) < 64))
     fine = [matmul(e, spread) for e in near]
     row = iota((8, 128), 0)
@@ -682,7 +689,7 @@
     (e2,) = call(
         functools.partial(coarse_kernel, boxes),
         [two],
-        [(2, boxes, 128), (2, boxes, 128), (2, boxes + 16, 128)],
+        [(2, boxes // 8, 8, 128)] * 4 + [(2, boxes + 16, 128)],
         gathered,
     )
     pressure, residual = call(

time: 73.2 us -> 72.5 us (level)
  transfers between devices with their start and end apart: 6 -> 6, of which waited for: 1 -> 1; matrix products, arithmetic and copies ran while one was open for 0% -> 0% of each run, Pallas kernels for 6% -> 5%
where the time goes in v9:
time: 72.5 us; the launch traced here: 72 us
  blocking collectives  42.5 us (59%)
  Pallas kernels  14 us (19%)
  starting transfers between devices  11.7 us (16%)
  waiting for transfers between devices  3.01 us (4%)
  between operations  0.75 us (1%)
    all_to_all x1, blocking collectives, body(): lax.all_to_all(message.reshape(boxes, 2, 128), 'box', 0, 0)  30.3 us
    pallas_call x6, Pallas kernels, call(): pl.pallas_call(kernel, out_shape=[jax.ShapeDtypeStruct(s, F32) for s in o...  12.3 us
    ppermute x6, starting transfers between devices, exchange(): lax.ppermute(x, 'box', p + [(j, i) for i, j in p])  11.7 us
    all_gather x2, blocking collectives, body(): low, high = (lax.all_gather(low, 'slab'), lax.all_gather(high, 'slab'))  5.39 us
    all_gather x1, blocking collectives, body(): gathered = lax.all_gather(spread, 'slab')  4.71 us
    ppermute x6, waiting for transfers between devices, exchange(): lax.ppermute(x, 'box', p + [(j, i) for i, j in p])  3.01 us
    all_gather x1, blocking collectives, body(): halo = lax.all_gather(jnp.stack([first, second]), 'slab')  2.09 us
    pallas_call x1, Pallas kernels, edges(): pl.pallas_call(edge_kernel, out_shape=jax.ShapeDtypeStruct((EDGE, 256), F...  1.73 us
  transfers between devices with their start and end apart: 6, of which 1 were waited for; matrix products, arithmetic and copies ran while one was open for 0% of the time, Pallas kernels for 5%

profile of v9, /device:TPU:1, one launch (start us, length us, event | category | flops | bytes accessed | tf_op | source)
XLA Modules:
  0.0 72.0 jit_solution(11835368131943010901)
XLA Ops:
  0.6 0.0 copy-start
  0.6 0.0 copy-start.1
  0.6 0.0 copy-start.2
  0.7 1.7 %shard_map.51 = f32[96,256]{1,0:T(8,128)} custom-call(f32[8,64,128]{2,1,0:T(8,128)} %bitcast.44, f32[8,64,128]{2,1,0:T(8,128)} %bitcast.46, f32[8,64,128]{2,1,0:T(8,128)} %bitcast.48), custom_call_target="tpu_custom_call" | custom-call | tf_op jit(solution)/shard_map/pallas_call | solution.py:629
  2.4 0.7 collective-permute-start
  3.1 0.0 copy-done
  3.1 0.0 copy-done.1
  3.1 0.0 copy-done.2
  3.1 0.6 shard_map.50
  3.7 4.6 %collective-permute-start.1 = (f32[96,256]{1,0:T(8,128)S(1)}, f32[96,256]{1,0:T(8,128)S(1)}, u32[]{:S(2)}, u32[]{:S(2)}) collective-permute-start(f32[96,256]{1,0:T(8,128)S(1)} %get-tuple-element.41), channel_id=1, source_target_pairs={{0,2},{4,6},{8,10},{12,14},{16,18},{20,22},{24,26},{28,30},{32,34}... | collective-permute-start | bytes 294920 | tf_op jit(solution)/shard_map/ppermute | solution.py:651
  8.3 3.1 %all-gather = f32[640,256]{1,0:T(8,128)S(1)} all-gather(f32[320,256]{1,0:T(8,128)S(1)} %get-tuple-element.39), channel_id=2, replica_groups=mesh['box'=128,'slab'=2] {'slab'}, dimensions={0}, use_global_device_ids=true | all-gather | bytes 983040 | tf_op jit(solution)/shard_map/all_gather | solution.py:660
  11.4 2.3 %all-gather.1 = f32[640,256]{1,0:T(8,128)S(1)} all-gather(f32[320,256]{1,0:T(8,128)S(1)} %get-tuple-element.40), channel_id=3, replica_groups=mesh['box'=128,'slab'=2] {'slab'}, dimensions={0}, use_global_device_ids=true | all-gather | bytes 983040 | tf_op jit(solution)/shard_map/all_gather | solution.py:660
  13.7 0.0 collective-permute-done
  13.7 0.0 collective-permute-done.1
  13.7 2.1 %all-gather.2 = f32[4,96,256]{2,1,0:T(8,128)S(1)} all-gather(f32[2,96,256]{2,1,0:T(8,128)S(1)} %pad_maximum_fusion), channel_id=4, replica_groups=mesh['box'=128,'slab'=2] {'slab'}, dimensions={0}, use_global_device_ids=true | all-gather | bytes 589824 | tf_op jit(solution)/shard_map/all_gather | solution.py:661
  15.8 2.9 %shard_map.52 = (f32[42,8,256]{2,1,0:T(8,128)S(1)}, f32[42,8,256]{2,1,0:T(8,128)S(1)}, f32[42,8,256]{2,1,0:T(8,128)S(1)}, f32[42,8,256]{2,1,0:T(8,128)S(1)}, f32...) custom-call(f32[2,320,256]{2,1,0:T(8,128)S(1)} %bitcast.39, ...), custom_call_target="tpu_custom_call" | custom-call | tf_op jit(solution)/shard_map/pallas_call | solution.py:618
  18.7 0.7 collective-permute-start.2
  19.3 3.5 %collective-permute-start.3 = (f32[29,8,128]{2,1,0:T(8,128)S(1)}, f32[29,8,128]{2,1,0:T(8,128)S(1)}, u32[]{:S(2)}, u32[]{:S(2)}) collective-permute-start(f32[29,8,128]{2,1,0:T(8,128)S(1)} %get-tuple-element.44), channel_id=1, source_target_pairs={{0,2},{4,6},{8,10},{12,14},{16,18},{20,22},{24,26},{28,30},{32,34}... | collective-permute-start | bytes 356360 | tf_op jit(solution)/shard_map/ppermute | solution.py:651
  22.8 0.0 collective-permute-done.2.first
  22.8 3.0 %collective-permute-done.3.second = f32[29,8,128]{2,1,0:T(8,128)S(1)} collective-permute-done((f32[29,8,128]{2,1,0:T(8,128)S(1)}, f32[29,8,128]{2,1,0:T(8,128)S(1)}, u32[]{:S(2)}, u32[]{:S(2)}) %collective-permute-start.3) | collective-permute-done | bytes 118816 | tf_op jit(solution)/shard_map/ppermute | solution.py:651
  25.8 1.9 %shard_map.53 = (f32[42,8,128]{2,1,0:T(8,128)S(1)}, f32[42,8,128]{2,1,0:T(8,128)S(1)}, f32[42,8,128]{2,1,0:T(8,128)S(1)}, f32[42,8,128]{2,1,0:T(8,128)S(1)}, f32...) custom-call(f32[36,8,128]{2,1,0:T(8,128)S(1)} %get-tuple-element.42., ...), custom_call_target="tpu_custom_call" | custom-call | tf_op jit(solution)/shard_map/pallas_call | solution.py:618
  27.6 30.3 %all_to_all.5 = f32[128,2,128]{2,1,0:T(2,128)S(1)} all-to-all(f32[128,2,128]{2,1,0:T(2,128)S(1)} %bitcast.50), channel_id=1, replica_groups=mesh['box'=128,'slab'=2] {'box'}, dimensions={0} | all-to-all | bytes 262144 | tf_op jit(solution)/shard_map/all_to_all | solution.py:686
  58.0 0.7 collective-permute-start.4
  58.6 1.7 %collective-permute-start.5 = (f32[14,8,128]{2,1,0:T(8,128)S(1)}, f32[14,8,128]{2,1,0:T(8,128)S(1)}, u32[]{:S(2)}, u32[]{:S(2)}) collective-permute-start(f32[14,8,128]{2,1,0:T(8,128)S(1)} %get-tuple-element.50), channel_id=1, source_target_pairs={{0,2},{4,6},{8,10},{12,14},{16,18},{20,22},{24,26},{28,30},{32,34}... | collective-permute-start | bytes 172040 | tf_op jit(solution)/shard_map/ppermute | solution.py:651
  60.3 4.7 %all_gather.27.gathered = f32[2,256,128]{2,1,0:T(8,128)S(1)} all-gather(f32[1,256,128]{2,1,0:T(8,128)S(1)} %bitcast.43), channel_id=1, replica_groups=mesh['box'=128,'slab'=2] {'slab'}, dimensions={0}, use_global_device_ids=true | all-gather | bytes 393216 | tf_op jit(solution)/shard_map/all_gather | solution.py:688
  65.0 2.9 %shard_map.54.refs_0_ = f32[24,8,128]{2,1,0:T(8,128)S(1)} custom-call(f32[2,256,128]{2,1,0:T(8,128)S(1)} %all_gather.27.gathered), custom_call_target="tpu_custom_call" | custom-call | tf_op jit(solution)/shard_map/pallas_call | solution.py:618
  67.9 0.0 collective-permute-done.4.refs_1_
  68.0 0.0 collective-permute-done.5.refs_2_
  68.0 4.0 %shard_map.56 = (f32[512,128]{1,0:T(8,128)}, f32[512,128]{1,0:T(8,128)}) custom-call(f32[24,8,128]{2,1,0:T(8,128)S(1)} %shard_map.54.refs_0_, f32[14,8,128]{2,1,0:T(8,128)S(1)} %collective-permute-done.4.refs_1_, f32[14,8,128]{2,1,0:T(8,128)S(1)} %collective-permute-done.5.refs_2_, f32[16,8,128]{2,1,0:T(8,128)S(1)} %get-tuple-element.51.refs_3_, ...), custom_call_target="tpu_custom_call" | custom-call | tf_op jit(solution)/shard_map/pallas_call | solution.py:618
  (2 shorter events, 0.0 us)
Async XLA Ops:
  0.6 2.4 %copy-start = (f32[8,32,256]{2,1,0:T(8,128)S(1)}, f32[8,32,256]{2,1,0:T(8,128)}, u32[]{:S(2)}) copy-start(f32[8,32,256]{2,1,0:T(8,128)} %param.3) | copy-start | bytes 786436
  0.6 2.4 %copy-start.1 = (f32[8,32,256]{2,1,0:T(8,128)S(1)}, f32[8,32,256]{2,1,0:T(8,128)}, u32[]{:S(2)}) copy-start(f32[8,32,256]{2,1,0:T(8,128)} %param.4) | copy-start | bytes 786436
  0.6 2.4 %copy-start.2 = (f32[8,32,256]{2,1,0:T(8,128)S(1)}, f32[8,32,256]{2,1,0:T(8,128)}, u32[]{:S(2)}) copy-start(f32[8,32,256]{2,1,0:T(8,128)} %param.5) | copy-start | bytes 786436
  2.4 11.3 %collective-permute-start = (f32[96,256]{1,0:T(8,128)}, f32[96,256]{1,0:T(8,128)S(1)}, u32[]{:S(2)}, u32[]{:S(2)}) collective-permute-start(f32[96,256]{1,0:T(8,128)} %shard_map.51), channel_id=1, source_target_pairs={{2,4},{6,8},{10,12},{14,16},{18,20},{22,24},{26,28},{30,32},{34,36... | collective-permute-start | bytes 294920 | tf_op jit(solution)/shard_map/ppermute | solution.py:651
  3.7 10.0 %collective-permute-start.1 = (f32[96,256]{1,0:T(8,128)S(1)}, f32[96,256]{1,0:T(8,128)S(1)}, u32[]{:S(2)}, u32[]{:S(2)}) collective-permute-start(f32[96,256]{1,0:T(8,128)S(1)} %get-tuple-element.41), channel_id=1, source_target_pairs={{0,2},{4,6},{8,10},{12,14},{16,18},{20,22},{24,26},{28,30},{32,34}... | collective-permute-start | bytes 294920 | tf_op jit(solution)/shard_map/ppermute | solution.py:651
  18.7 4.1 %collective-permute-start.2 = (f32[29,8,128]{2,1,0:T(8,128)S(1)}, f32[29,8,128]{2,1,0:T(8,128)S(1)}, u32[]{:S(2)}, u32[]{:S(2)}) collective-permute-start(f32[29,8,128]{2,1,0:T(8,128)S(1)} %get-tuple-element.43), channel_id=1, source_target_pairs={{2,4},{6,8},{10,12},{14,16},{18,20},{22,24},{26,28},{30,32},{34,36... | collective-permute-start | bytes 356360 | tf_op jit(solution)/shard_map/ppermute | solution.py:651
  19.3 6.4 %collective-permute-start.3 = (f32[29,8,128]{2,1,0:T(8,128)S(1)}, f32[29,8,128]{2,1,0:T(8,128)S(1)}, u32[]{:S(2)}, u32[]{:S(2)}) collective-permute-start(f32[29,8,128]{2,1,0:T(8,128)S(1)} %get-tuple-element.44), channel_id=1, source_target_pairs={{0,2},{4,6},{8,10},{12,14},{16,18},{20,22},{24,26},{28,30},{32,34}... | collective-permute-start | bytes 356360 | tf_op jit(solution)/shard_map/ppermute | solution.py:651
  58.0 10.0 %collective-permute-start.4 = (f32[14,8,128]{2,1,0:T(8,128)S(1)}, f32[14,8,128]{2,1,0:T(8,128)S(1)}, u32[]{:S(2)}, u32[]{:S(2)}) collective-permute-start(f32[14,8,128]{2,1,0:T(8,128)S(1)} %get-tuple-element.49), channel_id=1, source_target_pairs={{2,4},{6,8},{10,12},{14,16},{18,20},{22,24},{26,28},{30,32},{34,36... | collective-permute-start | bytes 172040 | tf_op jit(solution)/shard_map/ppermute | solution.py:651
  58.6 9.3 %collective-permute-start.5 = (f32[14,8,128]{2,1,0:T(8,128)S(1)}, f32[14,8,128]{2,1,0:T(8,128)S(1)}, u32[]{:S(2)}, u32[]{:S(2)}) collective-permute-start(f32[14,8,128]{2,1,0:T(8,128)S(1)} %get-tuple-element.50), channel_id=1, source_target_pairs={{0,2},{4,6},{8,10},{12,14},{16,18},{20,22},{24,26},{28,30},{32,34}... | collective-permute-start | bytes 172040 | tf_op jit(solution)/shard_map/ppermute | solution.py:651

commit v10 on v9

--- a/solution.py
+++ b/solution.py
@@ -179,108 +179,125 @@
 PACKED = ("vB", "fR", "fB", "xR", "xB", "yR", "yB", "s", "c", "iR", "iB", "cR", "cB")
 
 
-def fine_kernel(boxes, lo, hi, halo, *refs):
-    outs = dict(zip(PACKED, refs))
-    own, first, second, bottom = refs[len(PACKED) : len(PACKED) + 4]
-    vR, bE, bO, pair_r, pair_b, tmp = refs[len(PACKED) + 4 :]
-    lv = dict(outs, vR=vR)
-    box = my_place()[1]
-    odd = box & 1
+FINE = PACKED + ("bE", "bO")
+
+
+def stack(parts, at, i, out):
+    for t in range(2):
+        out[i, 4 * t : 4 * t + 4, :] = parts[t][at : at + 4, :]
+
+
+def merge(parts, at, i, low, high):
+    low_half = iota((8, 256), 0) < 4
+    a, b = (part[at : at + 8, :] for part in parts)
+    low[i] = jnp.where(low_half, a, pltpu.roll(b, 4, 0))
+    high[i] = jnp.where(low_half, pltpu.roll(a, 4, 0), b)
+
+
+def x_values(lv, i):
+    return 0.5 * (lv["bE"][i] + lv["bE"][i + 1]), 0.5 * (lv["bO"][i] + lv["bO"][i + 1])
+
+
+def x_faces(lv, i, p):
+    fxe, fxo = x_values(lv, i)
+    lv["xR"][i] = jnp.where(p, fxe, fxo)
+    lv["xB"][i] = jnp.where(p, fxo, fxe)
+    return fxe, fxo
+
+
+def faces(lv, i, before, inside=None):
     row, lane = iota((8, 256), 0), iota((8, 256), 1)
-    low_half = row < 4
-
-    def merge(parts, at, i, low, high):
-        a, b = (part[at : at + 8, :] for part in parts)
-        low[i] = jnp.where(low_half, a, pltpu.roll(b, 4, 0))
-        high[i] = jnp.where(low_half, pltpu.roll(a, 4, 0), b)
-
-    def stack(parts, at, i, out):
-        for t in range(2):
-            out[i, 4 * t : 4 * t + 4, :] = parts[t][at : at + 4, :]
-
+    top, bot = row == 7, row == 0
+    end, begin = lane == 255, lane == 0
+    p = parity(i % 2)
+    e, o = lv["bE"][i], lv["bO"][i]
+    fxe, fxo = x_faces(lv, i, p)
+    fye = 0.5 * (e + jnp.where(end, 0.0, up(e, 1)))
+    fyo = 0.5 * (o + jnp.where(end, 0.0, up(o, 1)))
+    gye = 0.5 * (e + jnp.where(begin, 0.0, down(e, 1)))
+    gyo = 0.5 * (o + jnp.where(begin, 0.0, down(o, 1)))
+    yr, yb = jnp.where(p, fye, fyo), jnp.where(p, fyo, fye)
+    lv["yR"][i] = jnp.where(end, 0.0, yr)
+    lv["yB"][i] = jnp.where(end, 0.0, yb)
+    s = 0.5 * (e + o)
+    above = 0.5 * (o + jnp.where(top, 0.0, up(e, 0)))
+    below = 0.5 * (e + jnp.where(bot, 0.0, down(o, 0)))
+    lv["s"][i] = s
+    lv["c"][i] = jnp.where(top, 0.0, above)
+    ce = fye + gye + (s + below) + (fxe + before[0])
+    co = fyo + gyo + (s + above) + (fxo + before[1])
+    cr, cb = jnp.where(p, ce, co), jnp.where(p, co, ce)
+    lv["cR"][i] = cr
+    lv["cB"][i] = cb
+    ir, ib = 1.0 / cr, 1.0 / cb
+    lv["iR"][i] = ir if inside is None else jnp.where(inside, ir, 0.0)
+    lv["iB"][i] = ib if inside is None else jnp.where(inside, ib, 0.0)
+    return fxe, fxo
+
+
+def own_kernel(lo, hi, *refs):
+    lv = dict(zip(FINE, refs))
+    coarse, bottom, pair_b, tmp = refs[len(FINE) :]
     for x in range(32):
         source, base = (lo, x * ROWS) if x < 16 else (hi, (x - 16) * ROWS)
         parts = source.at[0], source.at[1]
-        merge(parts, base, H0 + x, bE, bO)
+        merge(parts, base, H0 + x, lv["bE"], lv["bO"])
         merge(parts, base + 8, H0 + x, lv["fR"], lv["fB"])
         stack(parts, base + 16, H0 + x, lv["vB"])
+    before = x_values(lv, H0)
+    for i in range(H0 + 1, H0 + 31):
+        before = faces(lv, i, before)
+
+    bE, bO = lv["bE"], lv["bO"]
+    for j in range(16):
+        i = H0 + 2 * j
+        pair_b[j] = (bE[i] + bO[i]) + (bE[i + 1] + bO[i + 1])
+    halve = one_hot((256, 128), lambda i, j: (i >> 1) == j)
+    coarse[0:16] = (0.125 * matmul(pair_b[...].reshape(128, 256), halve)).reshape(16, 8, 128)
+    for k in range(8):
+        tmp[8 * k : 8 * k + 8, :] = coarse[2 * k] + coarse[2 * k + 1]
+    summed = tmp[pl.ds(0, 32, stride=2), :] + tmp[pl.ds(1, 32, stride=2), :]
+    halve = one_hot((128, 128), lambda i, j: (i >> 1) == j)
+    coarse[16:20] = (0.125 * matmul(summed, halve)).reshape(4, 8, 128)
+    bottom[...] = bottom_row([coarse[16 + k] + pltpu.roll(coarse[16 + k], 4, 0) for k in range(4)])
+
+
+def fine_kernel(boxes, halo, coarse, *refs):
+    refs = refs[len(FINE) :]
+    lv = dict(zip(FINE, refs))
+    f1, first, second, vR, pair_r = refs[len(FINE) :]
+    lv["vR"] = vR
+    box = my_place()[1]
+    odd = box & 1
     for side, at in ((odd, 0), (1 - odd, H0 + 32)):
         parts = halo.at[0, side], halo.at[1, side]
         for k in range(H0):
-            merge(parts, 8 * k, at + k, bE, bO)
+            merge(parts, 8 * k, at + k, lv["bE"], lv["bO"])
             stack(parts, EDGE_V + 4 * k, at + k, lv["vB"])
         for k in range(H0 - 1):
             merge(parts, EDGE_F + 8 * k, (1 if at == 0 else at) + k, lv["fR"], lv["fB"])
-
-    top, bot = row == 7, row == 0
-    end, begin = lane == 255, lane == 0
-
-    def x_faces(i, p):
-        fxe, fxo = 0.5 * (bE[i] + bE[i + 1]), 0.5 * (bO[i] + bO[i + 1])
-        lv["xR"][i] = jnp.where(p, fxe, fxo)
-        lv["xB"][i] = jnp.where(p, fxo, fxe)
-        return fxe, fxo
-
-    def faces(i, odd, before):
-        p = parity(odd)
-        e, o = bE[i], bO[i]
-        fxe, fxo = x_faces(i, p)
-        fye = 0.5 * (e + jnp.where(end, 0.0, up(e, 1)))
-        fyo = 0.5 * (o + jnp.where(end, 0.0, up(o, 1)))
-        gye = 0.5 * (e + jnp.where(begin, 0.0, down(e, 1)))
-        gyo = 0.5 * (o + jnp.where(begin, 0.0, down(o, 1)))
-        yr, yb = jnp.where(p, fye, fyo), jnp.where(p, fyo, fye)
-        lv["yR"][i] = jnp.where(end, 0.0, yr)
-        lv["yB"][i] = jnp.where(end, 0.0, yb)
-        s = 0.5 * (e + o)
-        above = 0.5 * (o + jnp.where(top, 0.0, up(e, 0)))
-        below = 0.5 * (e + jnp.where(bot, 0.0, down(o, 0)))
-        lv["s"][i] = s
-        lv["c"][i] = jnp.where(top, 0.0, above)
-        ce = fye + gye + (s + below) + (fxe + before[0])
-        co = fyo + gyo + (s + above) + (fxo + before[1])
-        cr, cb = jnp.where(p, ce, co), jnp.where(p, co, ce)
-        lv["cR"][i] = cr
-        lv["cB"][i] = cb
-        x = box * 32 - H0 + i
-        inside = jnp.logical_and(x >= 0, x < boxes * 32)
-        lv["iR"][i] = jnp.where(inside, 1.0 / cr, 0.0)
-        lv["iB"][i] = jnp.where(inside, 1.0 / cb, 0.0)
-        return fxe, fxo
-
-    planes(1, N0 - 1, FACES, faces, x_faces(0, parity(0)))
+    before = x_faces(lv, 0, parity(0))
+    for i in range(1, H0 + 1):
+        before = faces(lv, i, before, None if i == H0 else box > 0)
+    before = x_values(lv, H0 + 30)
+    for i in range(H0 + 31, N0 - 1):
+        before = faces(lv, i, before, None if i == H0 + 31 else box < boxes - 1)
 
     for k in range(2):
         sweep_packed(lv, True, 1 + 2 * k, N0 - 1 - 2 * k)
         sweep_packed(lv, False, 2 + 2 * k, N0 - 2 - 2 * k)
-
-    def restrict(j, carry):
+    for j in range(16):
         i = H0 + 2 * j
         a, b, _ = residual_packed(lv, i, H0 % 2)
         c, d, _ = residual_packed(lv, i + 1, (H0 + 1) % 2)
         pair_r[j] = (a + b) + (c + d)
-        pair_b[j] = (bE[i] + bO[i]) + (bE[i + 1] + bO[i + 1])
-        return carry
-
-    lax.fori_loop(0, 16, restrict, 0, unroll=RESTRICT)
-
     halve = one_hot((256, 128), lambda i, j: (i >> 1) == j)
-    f1 = 0.125 * matmul(pair_r[...].reshape(128, 256), halve)
-    b1 = 0.125 * matmul(pair_b[...].reshape(128, 256), halve)
-    own[0:16] = f1.reshape(16, 8, 128)
-    own[16:32] = b1.reshape(16, 8, 128)
-
-    for k in range(8):
-        tmp[8 * k : 8 * k + 8, :] = own[16 + 2 * k] + own[17 + 2 * k]
-    summed = tmp[pl.ds(0, 32, stride=2), :] + tmp[pl.ds(1, 32, stride=2), :]
-    halve = one_hot((128, 128), lambda i, j: (i >> 1) == j)
-    own[32:36] = (0.125 * matmul(summed, halve)).reshape(4, 8, 128)
-    bottom[...] = bottom_row([own[32 + k] + pltpu.roll(own[32 + k], 4, 0) for k in range(4)])
+    f1[...] = (0.125 * matmul(pair_r[...].reshape(128, 256), halve)).reshape(16, 8, 128)
 
     for out, right in ((first, odd), (second, 1 - odd)):
-        out[0:H1] = own[pl.ds(right * (16 - H1), H1)]
-        out[H1 : 2 * H1 + 1] = own[pl.ds(16 + right * (15 - H1), H1 + 1)]
-        out[2 * H1 + 1 :] = own[32:36]
+        out[0:H1] = f1[pl.ds(right * (16 - H1), H1)]
+        out[H1 : 2 * H1 + 1] = coarse[pl.ds(right * (15 - H1), H1 + 1)]
+        out[2 * H1 + 1 :] = coarse[16:20]
 
 
 def bottom_row(pairs):
@@ -358,7 +375,7 @@
     return factor * (4.0 * v + fy + fz) + (ax[i] + ax[i - 1])
 
 
-def middle_kernel(boxes, own, first, second, bottom, v1, f1, ax1, ay1, az1, inv1, ax2, ay2, az2, inv2, send, compact, message, v2, f2, b2, b1, tmp):
+def middle_kernel(boxes, source, coarse, first, second, bottom, v1, f1, ax1, ay1, az1, inv1, ax2, ay2, az2, inv2, send, compact, message, v2, f2, b2, b1, tmp):
     box = my_place()[1]
     w = H1 + 1
     swapped = (box & 1) == 1
@@ -369,17 +386,17 @@
 
     left, right = received(H1, w)
     b1[0:w] = left
-    b1[w : w + 16] = own[16:32]
+    b1[w : w + 16] = coarse[0:16]
     b1[w + 16 :] = right
     left, right = received(0, H1)
     f1[0:1] = jnp.zeros((1, 8, 128), F32)
     f1[1 : 1 + H1] = left
-    f1[w : w + 16] = own[0:16]
+    f1[w : w + 16] = source[...]
     f1[w + 16 : w + 16 + H1] = right
     f1[N1 - 1 :] = jnp.zeros((1, 8, 128), F32)
     left, right = received(H1 + w, 4)
     b2[...] = jnp.zeros(b2.shape, F32)
-    for at, part in ((0, left), (8, own[32:36]), (16, right)):
+    for at, part in ((0, left), (8, coarse[16:20]), (16, right)):
         for k in range(8):
             b2[at + k, 0:4, :] = part[k // 2, 4 * (k % 2) : 4 * (k % 2) + 4]
     v1[...] = jnp.zeros(v1.shape, F32)
@@ -412,9 +429,9 @@
     for j in range(16):
         restrict(j, 0)
     summed = tmp[pl.ds(0, 64, stride=2), :] + tmp[pl.ds(1, 64, stride=2), :]
-    coarse = 0.125 * matmul(summed, one_hot((128, 128), lambda i, j: (i >> 1) == j))
+    restricted = 0.125 * matmul(summed, one_hot((128, 128), lambda i, j: (i >> 1) == j))
     for j in range(16):
-        f2[4 + j, 0:4, :] = coarse[4 * j : 4 * j + 4]
+        f2[4 + j, 0:4, :] = restricted[4 * j : 4 * j + 4]
 
     two = (f2, ax2, ay2, az2, inv2)
     first_plain(v2, f2, inv2, 0, 4, 20)
@@ -434,8 +451,7 @@
             for i in (8 + 2 * k, 9 + 2 * k)
         ]
         pairs.append(parts[0] + parts[1])
-    source = bottom_row(pairs)
-    rows = jnp.where((iota((8, 128), 0) & 1) == 0, source, bottom[...])
+    rows = jnp.where((iota((8, 128), 0) & 1) == 0, bottom_row(pairs), bottom[...])
     for k in range(message.shape[0] // 8):
         message[8 * k : 8 * k + 8, :] = rows
 
@@ -613,13 +629,14 @@
     planes(H0, H0 + 32, FINISH, finish)
 
 
-def call(kernel, outs, scratch, *args, limit=12):
+def call(kernel, outs, scratch, *args, limit=12, aliases=()):
     vmem = pl.BlockSpec(memory_space=pltpu.VMEM)
     return pl.pallas_call(
         kernel,
         out_shape=[jax.ShapeDtypeStruct(s, F32) for s in outs],
         in_specs=[vmem] * len(args),
         out_specs=[vmem] * len(outs),
+        input_output_aliases=dict(aliases),
         scratch_shapes=[pltpu.VMEM(s, F32) for s in scratch],
         compiler_params=pltpu.CompilerParams(vmem_limit_bytes=limit * 1024 * 1024),
     )(*args)
@@ -661,16 +678,24 @@
     halo = lax.all_gather(jnp.stack([first, second]), "slab")
 
     plane = (N0, 8, 256)
+    *arrays, coarse, bottom = call(
+        own_kernel,
+        [plane] * len(FINE) + [(20, 8, 128), (8, 128)],
+        [(16, 8, 256), (64, 128)],
+        low,
+        high,
+    )
     fine = call(
         functools.partial(fine_kernel, boxes),
-        [plane] * len(PACKED) + [(36, 8, 128), (SEND1, 8, 128), (SEND1, 8, 128), (8, 128)],
-        [plane] * 3 + [(16, 8, 256)] * 2 + [(64, 128)],
-        low,
-        high,
+        [plane] * len(FINE) + [(16, 8, 128), (SEND1, 8, 128), (SEND1, 8, 128)],
+        [plane, (16, 8, 256)],
         halo,
+        coarse,
+        *arrays,
+        aliases=[(2 + k, k) for k in range(len(FINE))],
     )
     level0 = fine[: len(PACKED)]
-    own, first, second, bottom = fine[len(PACKED) :]
+    source, first, second = fine[len(FINE) :]
     first, second = exchange(first, second)
 
     one, two = (N1, 8, 128), (N2, 8, 128)
@@ -678,7 +703,8 @@
         functools.partial(middle_kernel, boxes),
         [one] * 6 + [two] * 4 + [(16, 8, 128), (4, 8, 128), (2 * boxes, 128)],
         [two] * 3 + [one, (128, 128)],
-        own,
+        source,
+        coarse,
         first,
         second,
         bottom,

time: 72.5 us -> 71.6 us (0.988)
  blocking collectives: 42.5 us -> 41.7 us
    all_to_all x1, blocking collectives: 30.3 us -> 29.5 us  [body(): lax.all_to_all(message.reshape(boxes, 2, 128), 'box', 0, 0)]
    pallas_call x6 -> x7, Pallas kernels: 12.3 us -> 12.2 us  [call(): pl.pallas_call(kernel, out_shape=[jax.ShapeDtypeStruct(s, F32) for s in o...]
  transfers between devices with their start and end apart: 6 -> 6, of which waited for: 1 -> 1; matrix products, arithmetic and copies ran while one was open for 0% -> 0% of each run, Pallas kernels for 5% -> 6%
where the time goes in v10:
time: 71.6 us; the launch traced here: 71.1 us
  blocking collectives  41.7 us (58%)
  Pallas kernels  13.9 us (19%)
  starting transfers between devices  11.7 us (16%)
  waiting for transfers between devices  3 us (4%)
  between operations  0.78 us (1%)
    all_to_all x1, blocking collectives, body(): lax.all_to_all(message.reshape(boxes, 2, 128), 'box', 0, 0)  29.5 us
    pallas_call x7, Pallas kernels, call(): pl.pallas_call(kernel, out_shape=[jax.ShapeDtypeStruct(s, F32) for s in o...  12.2 us
    ppermute x6, starting transfers between devices, exchange(): lax.ppermute(x, 'box', p + [(j, i) for i, j in p])  11.7 us
    all_gather x2, blocking collectives, body(): low, high = (lax.all_gather(low, 'slab'), lax.all_gather(high, 'slab'))  5.39 us
    all_gather x1, blocking collectives, body(): gathered = lax.all_gather(spread, 'slab')  4.72 us
    ppermute x6, waiting for transfers between devices, exchange(): lax.ppermute(x, 'box', p + [(j, i) for i, j in p])  3 us
    all_gather x1, blocking collectives, body(): halo = lax.all_gather(jnp.stack([first, second]), 'slab')  2.09 us
    pallas_call x1, Pallas kernels, edges(): pl.pallas_call(edge_kernel, out_shape=jax.ShapeDtypeStruct((EDGE, 256), F...  1.73 us
  transfers between devices with their start and end apart: 6, of which 1 were waited for; matrix products, arithmetic and copies ran while one was open for 0% of the time, Pallas kernels for 6%

profile of v10, /device:TPU:1, one launch (start us, length us, event | category | flops | bytes accessed | tf_op | source)
XLA Modules:
  0.0 71.1 jit_solution(17434472060107138493)
XLA Ops:
  0.6 0.0 copy-start
  0.6 0.0 copy-start.1
  0.6 0.0 copy-start.2
  0.7 1.7 %shard_map.50 = f32[96,256]{1,0:T(8,128)} custom-call(f32[8,64,128]{2,1,0:T(8,128)} %bitcast.44, f32[8,64,128]{2,1,0:T(8,128)} %bitcast.46, f32[8,64,128]{2,1,0:T(8,128)} %bitcast.48), custom_call_target="tpu_custom_call" | custom-call | tf_op jit(solution)/shard_map/pallas_call | solution.py:646
  2.4 0.7 collective-permute-start
  3.1 0.0 copy-done
  3.1 0.0 copy-done.1
  3.1 0.0 copy-done.2
  3.1 0.6 shard_map.51
  3.7 4.6 %collective-permute-start.1 = (f32[96,256]{1,0:T(8,128)S(1)}, f32[96,256]{1,0:T(8,128)S(1)}, u32[]{:S(2)}, u32[]{:S(2)}) collective-permute-start(f32[96,256]{1,0:T(8,128)S(1)} %get-tuple-element.55), channel_id=1, source_target_pairs={{0,2},{4,6},{8,10},{12,14},{16,18},{20,22},{24,26},{28,30},{32,34}... | collective-permute-start | bytes 294920 | tf_op jit(solution)/shard_map/ppermute | solution.py:668
  8.3 3.1 %all-gather.1 = f32[640,256]{1,0:T(8,128)S(1)} all-gather(f32[320,256]{1,0:T(8,128)S(1)} %get-tuple-element.56), channel_id=3, replica_groups=mesh['box'=128,'slab'=2] {'slab'}, dimensions={0}, use_global_device_ids=true | all-gather | bytes 983040 | tf_op jit(solution)/shard_map/all_gather | solution.py:677
  11.4 2.3 %all-gather.2 = f32[640,256]{1,0:T(8,128)S(1)} all-gather(f32[320,256]{1,0:T(8,128)S(1)} %get-tuple-element.57), channel_id=4, replica_groups=mesh['box'=128,'slab'=2] {'slab'}, dimensions={0}, use_global_device_ids=true | all-gather | bytes 983040 | tf_op jit(solution)/shard_map/all_gather | solution.py:677
  13.7 0.8 %shard_map.52 = (f32[42,8,256]{2,1,0:T(8,128)S(1)}, f32[42,8,256]{2,1,0:T(8,128)S(1)}, f32[42,8,256]{2,1,0:T(8,128)S(1)}, f32[42,8,256]{2,1,0:T(8,128)S(1)}, f32...) custom-call(f32[2,320,256]{2,1,0:T(8,128)S(1)} %bitcast.39, ...), custom_call_target="tpu_custom_call" | custom-call | tf_op jit(solution)/shard_map/pallas_call | solution.py:634
  14.5 0.0 collective-permute-done
  14.5 0.0 collective-permute-done.1
  14.6 2.1 %all-gather = f32[4,96,256]{2,1,0:T(8,128)S(1)} all-gather(f32[2,96,256]{2,1,0:T(8,128)S(1)} %pad_maximum_fusion), channel_id=2, replica_groups=mesh['box'=128,'slab'=2] {'slab'}, dimensions={0}, use_global_device_ids=true | all-gather | bytes 589824 | tf_op jit(solution)/shard_map/all_gather | solution.py:678
  16.6 1.8 %shard_map.53 = (f32[42,8,256]{2,1,0:T(8,128)S(1)}, f32[42,8,256]{2,1,0:T(8,128)S(1)}, f32[42,8,256]{2,1,0:T(8,128)S(1)}, f32[42,8,256]{2,1,0:T(8,128)S(1)}, f32...) custom-call(f32[2,2,96,256]{3,2,1,0:T(8,128)S(1)} %bitcast.41, ...), custom_call_target="tpu_custom_call", output_to_operand_aliasing={{0}: (2, {}), {1}: (3, {}), {2}: (4, {}), {3}: (5, {}), {4}... | custom-call | tf_op jit(solution)/shard_map/pallas_call | solution.py:634
  18.5 0.7 collective-permute-start.2
  19.2 3.5 %collective-permute-start.3 = (f32[29,8,128]{2,1,0:T(8,128)S(1)}, f32[29,8,128]{2,1,0:T(8,128)S(1)}, u32[]{:S(2)}, u32[]{:S(2)}) collective-permute-start(f32[29,8,128]{2,1,0:T(8,128)S(1)} %get-tuple-element.76), channel_id=1, source_target_pairs={{0,2},{4,6},{8,10},{12,14},{16,18},{20,22},{24,26},{28,30},{32,34}... | collective-permute-start | bytes 356360 | tf_op jit(solution)/shard_map/ppermute | solution.py:668
  22.6 0.0 collective-permute-done.2.first
  22.6 3.0 %collective-permute-done.3.second = f32[29,8,128]{2,1,0:T(8,128)S(1)} collective-permute-done((f32[29,8,128]{2,1,0:T(8,128)S(1)}, f32[29,8,128]{2,1,0:T(8,128)S(1)}, u32[]{:S(2)}, u32[]{:S(2)}) %collective-permute-start.3) | collective-permute-done | bytes 118816 | tf_op jit(solution)/shard_map/ppermute | solution.py:668
  25.6 1.8 %shard_map.54 = (f32[42,8,128]{2,1,0:T(8,128)S(1)}, f32[42,8,128]{2,1,0:T(8,128)S(1)}, f32[42,8,128]{2,1,0:T(8,128)S(1)}, f32[42,8,128]{2,1,0:T(8,128)S(1)}, f32...) custom-call(f32[16,8,128]{2,1,0:T(8,128)S(1)} %get-tuple-element.74., ...), custom_call_target="tpu_custom_call" | custom-call | tf_op jit(solution)/shard_map/pallas_call | solution.py:634
  27.5 29.5 %all_to_all.5 = f32[128,2,128]{2,1,0:T(2,128)S(1)} all-to-all(f32[128,2,128]{2,1,0:T(2,128)S(1)} %bitcast.50), channel_id=1, replica_groups=mesh['box'=128,'slab'=2] {'box'}, dimensions={0} | all-to-all | bytes 262144 | tf_op jit(solution)/shard_map/all_to_all | solution.py:712
  56.9 0.7 collective-permute-start.4
  57.6 1.6 %collective-permute-start.5 = (f32[14,8,128]{2,1,0:T(8,128)S(1)}, f32[14,8,128]{2,1,0:T(8,128)S(1)}, u32[]{:S(2)}, u32[]{:S(2)}) collective-permute-start(f32[14,8,128]{2,1,0:T(8,128)S(1)} %get-tuple-element.82), channel_id=1, source_target_pairs={{0,2},{4,6},{8,10},{12,14},{16,18},{20,22},{24,26},{28,30},{32,34}... | collective-permute-start | bytes 172040 | tf_op jit(solution)/shard_map/ppermute | solution.py:668
  59.2 4.7 %all_gather.27.gathered = f32[2,256,128]{2,1,0:T(8,128)S(1)} all-gather(f32[1,256,128]{2,1,0:T(8,128)S(1)} %bitcast.43), channel_id=1, replica_groups=mesh['box'=128,'slab'=2] {'slab'}, dimensions={0}, use_global_device_ids=true | all-gather | bytes 393216 | tf_op jit(solution)/shard_map/all_gather | solution.py:714
  64.0 2.9 %shard_map.55.refs_0_ = f32[24,8,128]{2,1,0:T(8,128)S(1)} custom-call(f32[2,256,128]{2,1,0:T(8,128)S(1)} %all_gather.27.gathered), custom_call_target="tpu_custom_call" | custom-call | tf_op jit(solution)/shard_map/pallas_call | solution.py:634
  66.9 0.0 collective-permute-done.4.refs_1_
  66.9 0.0 collective-permute-done.5.refs_2_
  66.9 4.1 %shard_map.57 = (f32[512,128]{1,0:T(8,128)}, f32[512,128]{1,0:T(8,128)}) custom-call(f32[24,8,128]{2,1,0:T(8,128)S(1)} %shard_map.55.refs_0_, f32[14,8,128]{2,1,0:T(8,128)S(1)} %collective-permute-done.4.refs_1_, f32[14,8,128]{2,1,0:T(8,128)S(1)} %collective-permute-done.5.refs_2_, f32[16,8,128]{2,1,0:T(8,128)S(1)} %get-tuple-element.83.refs_3_, ...), custom_call_target="tpu_custom_call" | custom-call | tf_op jit(solution)/shard_map/pallas_call | solution.py:634
  (2 shorter events, 0.0 us)
Async XLA Ops:
  0.6 2.4 %copy-start = (f32[8,32,256]{2,1,0:T(8,128)S(1)}, f32[8,32,256]{2,1,0:T(8,128)}, u32[]{:S(2)}) copy-start(f32[8,32,256]{2,1,0:T(8,128)} %param.3) | copy-start | bytes 786436
  0.6 2.4 %copy-start.1 = (f32[8,32,256]{2,1,0:T(8,128)S(1)}, f32[8,32,256]{2,1,0:T(8,128)}, u32[]{:S(2)}) copy-start(f32[8,32,256]{2,1,0:T(8,128)} %param.4) | copy-start | bytes 786436
  0.6 2.4 %copy-start.2 = (f32[8,32,256]{2,1,0:T(8,128)S(1)}, f32[8,32,256]{2,1,0:T(8,128)}, u32[]{:S(2)}) copy-start(f32[8,32,256]{2,1,0:T(8,128)} %param.5) | copy-start | bytes 786436
  2.4 12.1 %collective-permute-start = (f32[96,256]{1,0:T(8,128)}, f32[96,256]{1,0:T(8,128)S(1)}, u32[]{:S(2)}, u32[]{:S(2)}) collective-permute-start(f32[96,256]{1,0:T(8,128)} %shard_map.50), channel_id=1, source_target_pairs={{2,4},{6,8},{10,12},{14,16},{18,20},{22,24},{26,28},{30,32},{34,36... | collective-permute-start | bytes 294920 | tf_op jit(solution)/shard_map/ppermute | solution.py:668
  3.7 10.8 %collective-permute-start.1 = (f32[96,256]{1,0:T(8,128)S(1)}, f32[96,256]{1,0:T(8,128)S(1)}, u32[]{:S(2)}, u32[]{:S(2)}) collective-permute-start(f32[96,256]{1,0:T(8,128)S(1)} %get-tuple-element.55), channel_id=1, source_target_pairs={{0,2},{4,6},{8,10},{12,14},{16,18},{20,22},{24,26},{28,30},{32,34}... | collective-permute-start | bytes 294920 | tf_op jit(solution)/shard_map/ppermute | solution.py:668
  18.5 4.1 %collective-permute-start.2 = (f32[29,8,128]{2,1,0:T(8,128)S(1)}, f32[29,8,128]{2,1,0:T(8,128)S(1)}, u32[]{:S(2)}, u32[]{:S(2)}) collective-permute-start(f32[29,8,128]{2,1,0:T(8,128)S(1)} %get-tuple-element.75), channel_id=1, source_target_pairs={{2,4},{6,8},{10,12},{14,16},{18,20},{22,24},{26,28},{30,32},{34,36... | collective-permute-start | bytes 356360 | tf_op jit(solution)/shard_map/ppermute | solution.py:668
  19.2 6.4 %collective-permute-start.3 = (f32[29,8,128]{2,1,0:T(8,128)S(1)}, f32[29,8,128]{2,1,0:T(8,128)S(1)}, u32[]{:S(2)}, u32[]{:S(2)}) collective-permute-start(f32[29,8,128]{2,1,0:T(8,128)S(1)} %get-tuple-element.76), channel_id=1, source_target_pairs={{0,2},{4,6},{8,10},{12,14},{16,18},{20,22},{24,26},{28,30},{32,34}... | collective-permute-start | bytes 356360 | tf_op jit(solution)/shard_map/ppermute | solution.py:668
  56.9 10.0 %collective-permute-start.4 = (f32[14,8,128]{2,1,0:T(8,128)S(1)}, f32[14,8,128]{2,1,0:T(8,128)S(1)}, u32[]{:S(2)}, u32[]{:S(2)}) collective-permute-start(f32[14,8,128]{2,1,0:T(8,128)S(1)} %get-tuple-element.81), channel_id=1, source_target_pairs={{2,4},{6,8},{10,12},{14,16},{18,20},{22,24},{26,28},{30,32},{34,36... | collective-permute-start | bytes 172040 | tf_op jit(solution)/shard_map/ppermute | solution.py:668
  57.6 9.3 %collective-permute-start.5 = (f32[14,8,128]{2,1,0:T(8,128)S(1)}, f32[14,8,128]{2,1,0:T(8,128)S(1)}, u32[]{:S(2)}, u32[]{:S(2)}) collective-permute-start(f32[14,8,128]{2,1,0:T(8,128)S(1)} %get-tuple-element.82), channel_id=1, source_target_pairs={{0,2},{4,6},{8,10},{12,14},{16,18},{20,22},{24,26},{28,30},{32,34}... | collective-permute-start | bytes 172040 | tf_op jit(solution)/shard_map/ppermute | solution.py:668

commit v11 on v10

--- a/solution.py
+++ b/solution.py
@@ -335,24 +335,27 @@
     planes(1, n - 1, 99, step, ax[0])
 
 
-def nsum_plain(v, ax, ay, az, i):
-    here = v[i]
-    t = ax[i] * v[i + 1] + ax[i - 1] * v[i - 1]
+def nsum_values(before, here, after, ax, ay, az, i):
+    t = ax[i] * after + ax[i - 1] * before
     t = t + (ay[i] * up(here, 1) + down(ay[i] * here, 1))
     return t + (az[i] * up(here, 0) + down(az[i] * here, 0))
 
 
+def nsum_plain(v, ax, ay, az, i):
+    return nsum_values(v[i - 1], v[i], v[i + 1], ax, ay, az, i)
+
+
 def colour(odd):
     return ((iota((8, 128), 0) + iota((8, 128), 1) + odd) & 1) == 0
 
 
 def sweep_plain(v, f, ax, ay, az, inv, odd, shift, first, last):
-    def step(i, plane_odd, carry):
-        cells = colour((plane_odd + shift + odd) % 2)
-        v[i] = jnp.where(cells, (f[i] + nsum_plain(v, ax, ay, az, i)) * inv[i], v[i])
-        return carry
-
-    planes(first, last, 99, step)
+    before, here = v[first - 1], v[first]
+    for i in range(first, last):
+        after = v[i + 1]
+        n = nsum_values(before, here, after, ax, ay, az, i)
+        v[i] = jnp.where(colour((i + shift + odd) % 2), (f[i] + n) * inv[i], here)
+        before, here = here, after
 
 
 def first_plain(v, f, inv, shift, first, last):

time: 71.6 us -> 70.8 us (0.989)
  Pallas kernels: 13.9 us -> 13.1 us
    pallas_call x7, Pallas kernels: 12.2 us -> 11.4 us  [call(): pl.pallas_call(kernel, out_shape=[jax.ShapeDtypeStruct(s, F32) for s in o...]
where the time goes in v11:
time: 70.8 us; the launch traced here: 70.2 us
  blocking collectives  41.6 us (59%)
  Pallas kernels  13.1 us (19%)
  starting transfers between devices  11.7 us (17%)
  waiting for transfers between devices  3 us (4%)
  between operations  0.78 us (1%)
    all_to_all x1, blocking collectives, body(): lax.all_to_all(message.reshape(boxes, 2, 128), 'box', 0, 0)  29.5 us
    ppermute x6, starting transfers between devices, exchange(): lax.ppermute(x, 'box', p + [(j, i) for i, j in p])  11.7 us
    pallas_call x7, Pallas kernels, call(): pl.pallas_call(kernel, out_shape=[jax.ShapeDtypeStruct(s, F32) for s in o...  11.4 us
    all_gather x2, blocking collectives, body(): low, high = (lax.all_gather(low, 'slab'), lax.all_gather(high, 'slab'))  5.39 us
    all_gather x1, blocking collectives, body(): gathered = lax.all_gather(spread, 'slab')  4.71 us
    ppermute x6, waiting for transfers between devices, exchange(): lax.ppermute(x, 'box', p + [(j, i) for i, j in p])  3 us
    all_gather x1, blocking collectives, body(): halo = lax.all_gather(jnp.stack([first, second]), 'slab')  2.09 us
    pallas_call x1, Pallas kernels, edges(): pl.pallas_call(edge_kernel, out_shape=jax.ShapeDtypeStruct((EDGE, 256), F...  1.73 us
  transfers between devices with their start and end apart: 6, of which 1 were waited for; matrix products, arithmetic and copies ran while one was open for 0% of the time, Pallas kernels for 6%

profile of v11, /device:TPU:1, one launch (start us, length us, event | category | flops | bytes accessed | tf_op | source)
XLA Modules:
  0.0 70.2 jit_solution(6416189414158306433)
XLA Ops:
  0.6 0.0 copy-start
  0.6 0.0 copy-start.1
  0.6 0.0 copy-start.2
  0.7 1.7 %shard_map.50 = f32[96,256]{1,0:T(8,128)} custom-call(f32[8,64,128]{2,1,0:T(8,128)} %bitcast.44, f32[8,64,128]{2,1,0:T(8,128)} %bitcast.46, f32[8,64,128]{2,1,0:T(8,128)} %bitcast.48), custom_call_target="tpu_custom_call" | custom-call | tf_op jit(solution)/shard_map/pallas_call | solution.py:649
  2.4 0.7 collective-permute-start
  3.1 0.0 copy-done
  3.1 0.0 copy-done.1
  3.1 0.0 copy-done.2
  3.1 0.6 shard_map.51
  3.7 4.6 %collective-permute-start.1 = (f32[96,256]{1,0:T(8,128)S(1)}, f32[96,256]{1,0:T(8,128)S(1)}, u32[]{:S(2)}, u32[]{:S(2)}) collective-permute-start(f32[96,256]{1,0:T(8,128)S(1)} %get-tuple-element.55), channel_id=1, source_target_pairs={{0,2},{4,6},{8,10},{12,14},{16,18},{20,22},{24,26},{28,30},{32,34}... | collective-permute-start | bytes 294920 | tf_op jit(solution)/shard_map/ppermute | solution.py:671
  8.3 3.1 %all-gather.1 = f32[640,256]{1,0:T(8,128)S(1)} all-gather(f32[320,256]{1,0:T(8,128)S(1)} %get-tuple-element.56), channel_id=3, replica_groups=mesh['box'=128,'slab'=2] {'slab'}, dimensions={0}, use_global_device_ids=true | all-gather | bytes 983040 | tf_op jit(solution)/shard_map/all_gather | solution.py:680
  11.4 2.3 %all-gather.2 = f32[640,256]{1,0:T(8,128)S(1)} all-gather(f32[320,256]{1,0:T(8,128)S(1)} %get-tuple-element.57), channel_id=4, replica_groups=mesh['box'=128,'slab'=2] {'slab'}, dimensions={0}, use_global_device_ids=true | all-gather | bytes 983040 | tf_op jit(solution)/shard_map/all_gather | solution.py:680
  13.7 0.8 %shard_map.52 = (f32[42,8,256]{2,1,0:T(8,128)S(1)}, f32[42,8,256]{2,1,0:T(8,128)S(1)}, f32[42,8,256]{2,1,0:T(8,128)S(1)}, f32[42,8,256]{2,1,0:T(8,128)S(1)}, f32...) custom-call(f32[2,320,256]{2,1,0:T(8,128)S(1)} %bitcast.39, ...), custom_call_target="tpu_custom_call" | custom-call | tf_op jit(solution)/shard_map/pallas_call | solution.py:637
  14.5 0.0 collective-permute-done
  14.5 0.0 collective-permute-done.1
  14.6 2.1 %all-gather = f32[4,96,256]{2,1,0:T(8,128)S(1)} all-gather(f32[2,96,256]{2,1,0:T(8,128)S(1)} %pad_maximum_fusion), channel_id=2, replica_groups=mesh['box'=128,'slab'=2] {'slab'}, dimensions={0}, use_global_device_ids=true | all-gather | bytes 589824 | tf_op jit(solution)/shard_map/all_gather | solution.py:681
  16.6 1.8 %shard_map.53 = (f32[42,8,256]{2,1,0:T(8,128)S(1)}, f32[42,8,256]{2,1,0:T(8,128)S(1)}, f32[42,8,256]{2,1,0:T(8,128)S(1)}, f32[42,8,256]{2,1,0:T(8,128)S(1)}, f32...) custom-call(f32[2,2,96,256]{3,2,1,0:T(8,128)S(1)} %bitcast.41, ...), custom_call_target="tpu_custom_call", output_to_operand_aliasing={{0}: (2, {}), {1}: (3, {}), {2}: (4, {}), {3}: (5, {}), {4}... | custom-call | tf_op jit(solution)/shard_map/pallas_call | solution.py:637
  18.5 0.7 collective-permute-start.2
  19.2 3.5 %collective-permute-start.3 = (f32[29,8,128]{2,1,0:T(8,128)S(1)}, f32[29,8,128]{2,1,0:T(8,128)S(1)}, u32[]{:S(2)}, u32[]{:S(2)}) collective-permute-start(f32[29,8,128]{2,1,0:T(8,128)S(1)} %get-tuple-element.76), channel_id=1, source_target_pairs={{0,2},{4,6},{8,10},{12,14},{16,18},{20,22},{24,26},{28,30},{32,34}... | collective-permute-start | bytes 356360 | tf_op jit(solution)/shard_map/ppermute | solution.py:671
  22.6 0.0 collective-permute-done.2.first
  22.6 3.0 %collective-permute-done.3.second = f32[29,8,128]{2,1,0:T(8,128)S(1)} collective-permute-done((f32[29,8,128]{2,1,0:T(8,128)S(1)}, f32[29,8,128]{2,1,0:T(8,128)S(1)}, u32[]{:S(2)}, u32[]{:S(2)}) %collective-permute-start.3) | collective-permute-done | bytes 118816 | tf_op jit(solution)/shard_map/ppermute | solution.py:671
  25.6 1.4 %shard_map.54 = (f32[42,8,128]{2,1,0:T(8,128)S(1)}, f32[42,8,128]{2,1,0:T(8,128)S(1)}, f32[42,8,128]{2,1,0:T(8,128)S(1)}, f32[42,8,128]{2,1,0:T(8,128)S(1)}, f32...) custom-call(f32[16,8,128]{2,1,0:T(8,128)S(1)} %get-tuple-element.74., ...), custom_call_target="tpu_custom_call" | custom-call | tf_op jit(solution)/shard_map/pallas_call | solution.py:637
  27.0 29.5 %all_to_all.5 = f32[128,2,128]{2,1,0:T(2,128)S(1)} all-to-all(f32[128,2,128]{2,1,0:T(2,128)S(1)} %bitcast.50), channel_id=1, replica_groups=mesh['box'=128,'slab'=2] {'box'}, dimensions={0} | all-to-all | bytes 262144 | tf_op jit(solution)/shard_map/all_to_all | solution.py:715
  56.5 0.7 collective-permute-start.4
  57.2 1.7 %collective-permute-start.5 = (f32[14,8,128]{2,1,0:T(8,128)S(1)}, f32[14,8,128]{2,1,0:T(8,128)S(1)}, u32[]{:S(2)}, u32[]{:S(2)}) collective-permute-start(f32[14,8,128]{2,1,0:T(8,128)S(1)} %get-tuple-element.82), channel_id=1, source_target_pairs={{0,2},{4,6},{8,10},{12,14},{16,18},{20,22},{24,26},{28,30},{32,34}... | collective-permute-start | bytes 172040 | tf_op jit(solution)/shard_map/ppermute | solution.py:671
  58.8 4.7 %all_gather.27.gathered = f32[2,256,128]{2,1,0:T(8,128)S(1)} all-gather(f32[1,256,128]{2,1,0:T(8,128)S(1)} %bitcast.43), channel_id=1, replica_groups=mesh['box'=128,'slab'=2] {'slab'}, dimensions={0}, use_global_device_ids=true | all-gather | bytes 393216 | tf_op jit(solution)/shard_map/all_gather | solution.py:717
  63.5 2.9 %shard_map.55.refs_0_ = f32[24,8,128]{2,1,0:T(8,128)S(1)} custom-call(f32[2,256,128]{2,1,0:T(8,128)S(1)} %all_gather.27.gathered), custom_call_target="tpu_custom_call" | custom-call | tf_op jit(solution)/shard_map/pallas_call | solution.py:637
  66.5 0.0 collective-permute-done.4.refs_1_
  66.5 0.0 collective-permute-done.5.refs_2_
  66.5 3.7 %shard_map.57 = (f32[512,128]{1,0:T(8,128)}, f32[512,128]{1,0:T(8,128)}) custom-call(f32[24,8,128]{2,1,0:T(8,128)S(1)} %shard_map.55.refs_0_, f32[14,8,128]{2,1,0:T(8,128)S(1)} %collective-permute-done.4.refs_1_, f32[14,8,128]{2,1,0:T(8,128)S(1)} %collective-permute-done.5.refs_2_, f32[16,8,128]{2,1,0:T(8,128)S(1)} %get-tuple-element.83.refs_3_, ...), custom_call_target="tpu_custom_call" | custom-call | tf_op jit(solution)/shard_map/pallas_call | solution.py:637
  (2 shorter events, 0.0 us)
Async XLA Ops:
  0.6 2.4 %copy-start = (f32[8,32,256]{2,1,0:T(8,128)S(1)}, f32[8,32,256]{2,1,0:T(8,128)}, u32[]{:S(2)}) copy-start(f32[8,32,256]{2,1,0:T(8,128)} %param.3) | copy-start | bytes 786436
  0.6 2.4 %copy-start.1 = (f32[8,32,256]{2,1,0:T(8,128)S(1)}, f32[8,32,256]{2,1,0:T(8,128)}, u32[]{:S(2)}) copy-start(f32[8,32,256]{2,1,0:T(8,128)} %param.4) | copy-start | bytes 786436
  0.6 2.4 %copy-start.2 = (f32[8,32,256]{2,1,0:T(8,128)S(1)}, f32[8,32,256]{2,1,0:T(8,128)}, u32[]{:S(2)}) copy-start(f32[8,32,256]{2,1,0:T(8,128)} %param.5) | copy-start | bytes 786436
  2.4 12.1 %collective-permute-start = (f32[96,256]{1,0:T(8,128)}, f32[96,256]{1,0:T(8,128)S(1)}, u32[]{:S(2)}, u32[]{:S(2)}) collective-permute-start(f32[96,256]{1,0:T(8,128)} %shard_map.50), channel_id=1, source_target_pairs={{2,4},{6,8},{10,12},{14,16},{18,20},{22,24},{26,28},{30,32},{34,36... | collective-permute-start | bytes 294920 | tf_op jit(solution)/shard_map/ppermute | solution.py:671
  3.7 10.8 %collective-permute-start.1 = (f32[96,256]{1,0:T(8,128)S(1)}, f32[96,256]{1,0:T(8,128)S(1)}, u32[]{:S(2)}, u32[]{:S(2)}) collective-permute-start(f32[96,256]{1,0:T(8,128)S(1)} %get-tuple-element.55), channel_id=1, source_target_pairs={{0,2},{4,6},{8,10},{12,14},{16,18},{20,22},{24,26},{28,30},{32,34}... | collective-permute-start | bytes 294920 | tf_op jit(solution)/shard_map/ppermute | solution.py:671
  18.5 4.1 %collective-permute-start.2 = (f32[29,8,128]{2,1,0:T(8,128)S(1)}, f32[29,8,128]{2,1,0:T(8,128)S(1)}, u32[]{:S(2)}, u32[]{:S(2)}) collective-permute-start(f32[29,8,128]{2,1,0:T(8,128)S(1)} %get-tuple-element.75), channel_id=1, source_target_pairs={{2,4},{6,8},{10,12},{14,16},{18,20},{22,24},{26,28},{30,32},{34,36... | collective-permute-start | bytes 356360 | tf_op jit(solution)/shard_map/ppermute | solution.py:671
  19.2 6.4 %collective-permute-start.3 = (f32[29,8,128]{2,1,0:T(8,128)S(1)}, f32[29,8,128]{2,1,0:T(8,128)S(1)}, u32[]{:S(2)}, u32[]{:S(2)}) collective-permute-start(f32[29,8,128]{2,1,0:T(8,128)S(1)} %get-tuple-element.76), channel_id=1, source_target_pairs={{0,2},{4,6},{8,10},{12,14},{16,18},{20,22},{24,26},{28,30},{32,34}... | collective-permute-start | bytes 356360 | tf_op jit(solution)/shard_map/ppermute | solution.py:671
  56.5 10.0 %collective-permute-start.4 = (f32[14,8,128]{2,1,0:T(8,128)S(1)}, f32[14,8,128]{2,1,0:T(8,128)S(1)}, u32[]{:S(2)}, u32[]{:S(2)}) collective-permute-start(f32[14,8,128]{2,1,0:T(8,128)S(1)} %get-tuple-element.81), channel_id=1, source_target_pairs={{2,4},{6,8},{10,12},{14,16},{18,20},{22,24},{26,28},{30,32},{34,36... | collective-permute-start | bytes 172040 | tf_op jit(solution)/shard_map/ppermute | solution.py:671
  57.2 9.3 %collective-permute-start.5 = (f32[14,8,128]{2,1,0:T(8,128)S(1)}, f32[14,8,128]{2,1,0:T(8,128)S(1)}, u32[]{:S(2)}, u32[]{:S(2)}) collective-permute-start(f32[14,8,128]{2,1,0:T(8,128)S(1)} %get-tuple-element.82), channel_id=1, source_target_pairs={{0,2},{4,6},{8,10},{12,14},{16,18},{20,22},{24,26},{28,30},{32,34}... | collective-permute-start | bytes 172040 | tf_op jit(solution)/shard_map/ppermute | solution.py:671

commit v12 on v11

--- a/solution.py
+++ b/solution.py
@@ -311,7 +311,7 @@
     return jnp.broadcast_to(row, (8, 128))
 
 
-def level_faces(b, ax, ay, az, inv, n, factor, depth, width, inside):
+def level_faces(b, ax, ay, az, inv, centers, n, factor, depth, width, inside):
     row, lane = iota((8, 128), 0), iota((8, 128), 1)
     top, bot = row == depth - 1, row == 0
     end, begin = lane == width - 1, lane == 0
@@ -329,6 +329,7 @@
         ay[i] = jnp.where(end, 0.0, fy)
         az[i] = jnp.where(top, 0.0, fz)
         center = (fz + gz) + (fx + before) + (fy + gy)
+        centers[i] = center
         inv[i] = jnp.where(jnp.logical_and(cell, inside(i)), 1.0 / center, 0.0)
         return fx
 
@@ -370,15 +371,7 @@
     return f[i] - (center * v[i] - nsum_plain(v, ax, ay, az, i))
 
 
-def center_plain(b, ax, i, factor, depth, width):
-    row, lane = iota((8, 128), 0), iota((8, 128), 1)
-    v = b[i]
-    fy = jnp.where(lane == width - 1, 0.0, up(v, 1)) + jnp.where(lane == 0, 0.0, down(v, 1))
-    fz = jnp.where(row == depth - 1, 0.0, up(v, 0)) + jnp.where(row == 0, 0.0, down(v, 0))
-    return factor * (4.0 * v + fy + fz) + (ax[i] + ax[i - 1])
-
-
-def middle_kernel(boxes, source, coarse, first, second, bottom, v1, f1, ax1, ay1, az1, inv1, ax2, ay2, az2, inv2, send, compact, message, v2, f2, b2, b1, tmp):
+def middle_kernel(boxes, source, coarse, first, second, bottom, v1, f1, ax1, ay1, az1, inv1, ax2, ay2, az2, inv2, send, compact, message, v2, f2, b2, c2, b1, c1, tmp):
     box = my_place()[1]
     w = H1 + 1
     swapped = (box & 1) == 1
@@ -414,8 +407,8 @@
         return inside
 
     k1, k2 = 0.5 * 0.25, 0.5 * 0.25**2
-    level_faces(b1, ax1, ay1, az1, inv1, N1, k1, 8, 128, within(16, w))
-    level_faces(b2, ax2, ay2, az2, inv2, N2, k2, 4, 64, within(8, 8))
+    level_faces(b1, ax1, ay1, az1, inv1, c1, N1, k1, 8, 128, within(16, w))
+    level_faces(b2, ax2, ay2, az2, inv2, c2, N2, k2, 4, 64, within(8, 8))
 
     one = (f1, ax1, ay1, az1, inv1)
     first_plain(v1, f1, inv1, 1, 1, N1 - 1)
@@ -425,7 +418,7 @@
 
     def restrict(j, carry):
         i = 5 + 2 * j
-        parts = [residual_plain(v1, *one[:4], center_plain(b1, ax1, k, k1, 8, 128), k) for k in (i, i + 1)]
+        parts = [residual_plain(v1, *one[:4], c1[k], k) for k in (i, i + 1)]
         tmp[8 * j : 8 * j + 8, :] = parts[0] + parts[1]
         return carry
 
@@ -450,7 +443,7 @@
     pairs = []
     for k in range(4):
         parts = [
-            residual_plain(v2, *two[:4], center_plain(b2, ax2, i, k2, 4, 64), i)
+            residual_plain(v2, *two[:4], c2[i], i)
             for i in (8 + 2 * k, 9 + 2 * k)
         ]
         pairs.append(parts[0] + parts[1])
@@ -705,7 +698,7 @@
     *levels, send, compact, message = call(
         functools.partial(middle_kernel, boxes),
         [one] * 6 + [two] * 4 + [(16, 8, 128), (4, 8, 128), (2 * boxes, 128)],
-        [two] * 3 + [one, (128, 128)],
+        [two] * 4 + [one, one, (128, 128)],
         source,
         coarse,
         first,

time: 70.8 us -> 70.7 us (level)
  no operation moved by 1% of the time
where the time goes in v12:
time: 70.7 us; the launch traced here: 70.2 us
  blocking collectives  41.7 us (59%)
  Pallas kernels  13 us (18%)
  starting transfers between devices  11.7 us (17%)
  waiting for transfers between devices  3 us (4%)
  between operations  0.78 us (1%)
    all_to_all x1, blocking collectives, body(): lax.all_to_all(message.reshape(boxes, 2, 128), 'box', 0, 0)  29.5 us
    ppermute x6, starting transfers between devices, exchange(): lax.ppermute(x, 'box', p + [(j, i) for i, j in p])  11.7 us
    pallas_call x7, Pallas kernels, call(): pl.pallas_call(kernel, out_shape=[jax.ShapeDtypeStruct(s, F32) for s in o...  11.3 us
    all_gather x2, blocking collectives, body(): low, high = (lax.all_gather(low, 'slab'), lax.all_gather(high, 'slab'))  5.39 us
    all_gather x1, blocking collectives, body(): gathered = lax.all_gather(spread, 'slab')  4.72 us
    ppermute x6, waiting for transfers between devices, exchange(): lax.ppermute(x, 'box', p + [(j, i) for i, j in p])  3 us
    all_gather x1, blocking collectives, body(): halo = lax.all_gather(jnp.stack([first, second]), 'slab')  2.09 us
    pallas_call x1, Pallas kernels, edges(): pl.pallas_call(edge_kernel, out_shape=jax.ShapeDtypeStruct((EDGE, 256), F...  1.73 us
  transfers between devices with their start and end apart: 6, of which 1 were waited for; matrix products, arithmetic and copies ran while one was open for 0% of the time, Pallas kernels for 6%

profile of v12, /device:TPU:1, one launch (start us, length us, event | category | flops | bytes accessed | tf_op | source)
XLA Modules:
  0.0 70.2 jit_solution(6939807141410599043)
XLA Ops:
  0.6 0.0 copy-start
  0.6 0.0 copy-start.1
  0.6 0.0 copy-start.2
  0.7 1.7 %shard_map.50 = f32[96,256]{1,0:T(8,128)} custom-call(f32[8,64,128]{2,1,0:T(8,128)} %bitcast.44, f32[8,64,128]{2,1,0:T(8,128)} %bitcast.46, f32[8,64,128]{2,1,0:T(8,128)} %bitcast.48), custom_call_target="tpu_custom_call" | custom-call | tf_op jit(solution)/shard_map/pallas_call | solution.py:642
  2.4 0.7 collective-permute-start
  3.1 0.0 copy-done
  3.1 0.0 copy-done.1
  3.1 0.0 copy-done.2
  3.1 0.6 shard_map.51
  3.7 4.6 %collective-permute-start.1 = (f32[96,256]{1,0:T(8,128)S(1)}, f32[96,256]{1,0:T(8,128)S(1)}, u32[]{:S(2)}, u32[]{:S(2)}) collective-permute-start(f32[96,256]{1,0:T(8,128)S(1)} %get-tuple-element.55), channel_id=1, source_target_pairs={{0,2},{4,6},{8,10},{12,14},{16,18},{20,22},{24,26},{28,30},{32,34}... | collective-permute-start | bytes 294920 | tf_op jit(solution)/shard_map/ppermute | solution.py:664
  8.3 3.1 %all-gather.1 = f32[640,256]{1,0:T(8,128)S(1)} all-gather(f32[320,256]{1,0:T(8,128)S(1)} %get-tuple-element.56), channel_id=3, replica_groups=mesh['box'=128,'slab'=2] {'slab'}, dimensions={0}, use_global_device_ids=true | all-gather | bytes 983040 | tf_op jit(solution)/shard_map/all_gather | solution.py:673
  11.4 2.3 %all-gather.2 = f32[640,256]{1,0:T(8,128)S(1)} all-gather(f32[320,256]{1,0:T(8,128)S(1)} %get-tuple-element.57), channel_id=4, replica_groups=mesh['box'=128,'slab'=2] {'slab'}, dimensions={0}, use_global_device_ids=true | all-gather | bytes 983040 | tf_op jit(solution)/shard_map/all_gather | solution.py:673
  13.7 0.8 %shard_map.52 = (f32[42,8,256]{2,1,0:T(8,128)S(1)}, f32[42,8,256]{2,1,0:T(8,128)S(1)}, f32[42,8,256]{2,1,0:T(8,128)S(1)}, f32[42,8,256]{2,1,0:T(8,128)S(1)}, f32...) custom-call(f32[2,320,256]{2,1,0:T(8,128)S(1)} %bitcast.39, ...), custom_call_target="tpu_custom_call" | custom-call | tf_op jit(solution)/shard_map/pallas_call | solution.py:630
  14.5 0.0 collective-permute-done
  14.5 0.0 collective-permute-done.1
  14.6 2.1 %all-gather = f32[4,96,256]{2,1,0:T(8,128)S(1)} all-gather(f32[2,96,256]{2,1,0:T(8,128)S(1)} %pad_maximum_fusion), channel_id=2, replica_groups=mesh['box'=128,'slab'=2] {'slab'}, dimensions={0}, use_global_device_ids=true | all-gather | bytes 589824 | tf_op jit(solution)/shard_map/all_gather | solution.py:674
  16.6 1.8 %shard_map.53 = (f32[42,8,256]{2,1,0:T(8,128)S(1)}, f32[42,8,256]{2,1,0:T(8,128)S(1)}, f32[42,8,256]{2,1,0:T(8,128)S(1)}, f32[42,8,256]{2,1,0:T(8,128)S(1)}, f32...) custom-call(f32[2,2,96,256]{3,2,1,0:T(8,128)S(1)} %bitcast.41, ...), custom_call_target="tpu_custom_call", output_to_operand_aliasing={{0}: (2, {}), {1}: (3, {}), {2}: (4, {}), {3}: (5, {}), {4}... | custom-call | tf_op jit(solution)/shard_map/pallas_call | solution.py:630
  18.5 0.7 collective-permute-start.2
  19.2 3.5 %collective-permute-start.3 = (f32[29,8,128]{2,1,0:T(8,128)S(1)}, f32[29,8,128]{2,1,0:T(8,128)S(1)}, u32[]{:S(2)}, u32[]{:S(2)}) collective-permute-start(f32[29,8,128]{2,1,0:T(8,128)S(1)} %get-tuple-element.76), channel_id=1, source_target_pairs={{0,2},{4,6},{8,10},{12,14},{16,18},{20,22},{24,26},{28,30},{32,34}... | collective-permute-start | bytes 356360 | tf_op jit(solution)/shard_map/ppermute | solution.py:664
  22.6 0.0 collective-permute-done.2.first
  22.6 3.0 %collective-permute-done.3.second = f32[29,8,128]{2,1,0:T(8,128)S(1)} collective-permute-done((f32[29,8,128]{2,1,0:T(8,128)S(1)}, f32[29,8,128]{2,1,0:T(8,128)S(1)}, u32[]{:S(2)}, u32[]{:S(2)}) %collective-permute-start.3) | collective-permute-done | bytes 118816 | tf_op jit(solution)/shard_map/ppermute | solution.py:664
  25.6 1.3 %shard_map.54 = (f32[42,8,128]{2,1,0:T(8,128)S(1)}, f32[42,8,128]{2,1,0:T(8,128)S(1)}, f32[42,8,128]{2,1,0:T(8,128)S(1)}, f32[42,8,128]{2,1,0:T(8,128)S(1)}, f32...) custom-call(f32[16,8,128]{2,1,0:T(8,128)S(1)} %get-tuple-element.74., ...), custom_call_target="tpu_custom_call" | custom-call | tf_op jit(solution)/shard_map/pallas_call | solution.py:630
  27.0 29.5 %all_to_all.5 = f32[128,2,128]{2,1,0:T(2,128)S(1)} all-to-all(f32[128,2,128]{2,1,0:T(2,128)S(1)} %bitcast.50), channel_id=1, replica_groups=mesh['box'=128,'slab'=2] {'box'}, dimensions={0} | all-to-all | bytes 262144 | tf_op jit(solution)/shard_map/all_to_all | solution.py:708
  56.4 0.7 collective-permute-start.4
  57.1 1.7 %collective-permute-start.5 = (f32[14,8,128]{2,1,0:T(8,128)S(1)}, f32[14,8,128]{2,1,0:T(8,128)S(1)}, u32[]{:S(2)}, u32[]{:S(2)}) collective-permute-start(f32[14,8,128]{2,1,0:T(8,128)S(1)} %get-tuple-element.82), channel_id=1, source_target_pairs={{0,2},{4,6},{8,10},{12,14},{16,18},{20,22},{24,26},{28,30},{32,34}... | collective-permute-start | bytes 172040 | tf_op jit(solution)/shard_map/ppermute | solution.py:664
  58.8 4.7 %all_gather.27.gathered = f32[2,256,128]{2,1,0:T(8,128)S(1)} all-gather(f32[1,256,128]{2,1,0:T(8,128)S(1)} %bitcast.43), channel_id=1, replica_groups=mesh['box'=128,'slab'=2] {'slab'}, dimensions={0}, use_global_device_ids=true | all-gather | bytes 393216 | tf_op jit(solution)/shard_map/all_gather | solution.py:710
  63.5 2.9 %shard_map.55.refs_0_ = f32[24,8,128]{2,1,0:T(8,128)S(1)} custom-call(f32[2,256,128]{2,1,0:T(8,128)S(1)} %all_gather.27.gathered), custom_call_target="tpu_custom_call" | custom-call | tf_op jit(solution)/shard_map/pallas_call | solution.py:630
  66.4 0.0 collective-permute-done.4.refs_1_
  66.4 0.0 collective-permute-done.5.refs_2_
  66.4 3.7 %shard_map.57 = (f32[512,128]{1,0:T(8,128)}, f32[512,128]{1,0:T(8,128)}) custom-call(f32[24,8,128]{2,1,0:T(8,128)S(1)} %shard_map.55.refs_0_, f32[14,8,128]{2,1,0:T(8,128)S(1)} %collective-permute-done.4.refs_1_, f32[14,8,128]{2,1,0:T(8,128)S(1)} %collective-permute-done.5.refs_2_, f32[16,8,128]{2,1,0:T(8,128)S(1)} %get-tuple-element.83.refs_3_, ...), custom_call_target="tpu_custom_call" | custom-call | tf_op jit(solution)/shard_map/pallas_call | solution.py:630
  (2 shorter events, 0.0 us)
Async XLA Ops:
  0.6 2.4 %copy-start = (f32[8,32,256]{2,1,0:T(8,128)S(1)}, f32[8,32,256]{2,1,0:T(8,128)}, u32[]{:S(2)}) copy-start(f32[8,32,256]{2,1,0:T(8,128)} %param.3) | copy-start | bytes 786436
  0.6 2.4 %copy-start.1 = (f32[8,32,256]{2,1,0:T(8,128)S(1)}, f32[8,32,256]{2,1,0:T(8,128)}, u32[]{:S(2)}) copy-start(f32[8,32,256]{2,1,0:T(8,128)} %param.4) | copy-start | bytes 786436
  0.6 2.4 %copy-start.2 = (f32[8,32,256]{2,1,0:T(8,128)S(1)}, f32[8,32,256]{2,1,0:T(8,128)}, u32[]{:S(2)}) copy-start(f32[8,32,256]{2,1,0:T(8,128)} %param.5) | copy-start | bytes 786436
  2.4 12.1 %collective-permute-start = (f32[96,256]{1,0:T(8,128)}, f32[96,256]{1,0:T(8,128)S(1)}, u32[]{:S(2)}, u32[]{:S(2)}) collective-permute-start(f32[96,256]{1,0:T(8,128)} %shard_map.50), channel_id=1, source_target_pairs={{2,4},{6,8},{10,12},{14,16},{18,20},{22,24},{26,28},{30,32},{34,36... | collective-permute-start | bytes 294920 | tf_op jit(solution)/shard_map/ppermute | solution.py:664
  3.7 10.8 %collective-permute-start.1 = (f32[96,256]{1,0:T(8,128)S(1)}, f32[96,256]{1,0:T(8,128)S(1)}, u32[]{:S(2)}, u32[]{:S(2)}) collective-permute-start(f32[96,256]{1,0:T(8,128)S(1)} %get-tuple-element.55), channel_id=1, source_target_pairs={{0,2},{4,6},{8,10},{12,14},{16,18},{20,22},{24,26},{28,30},{32,34}... | collective-permute-start | bytes 294920 | tf_op jit(solution)/shard_map/ppermute | solution.py:664
  18.5 4.1 %collective-permute-start.2 = (f32[29,8,128]{2,1,0:T(8,128)S(1)}, f32[29,8,128]{2,1,0:T(8,128)S(1)}, u32[]{:S(2)}, u32[]{:S(2)}) collective-permute-start(f32[29,8,128]{2,1,0:T(8,128)S(1)} %get-tuple-element.75), channel_id=1, source_target_pairs={{2,4},{6,8},{10,12},{14,16},{18,20},{22,24},{26,28},{30,32},{34,36... | collective-permute-start | bytes 356360 | tf_op jit(solution)/shard_map/ppermute | solution.py:664
  19.2 6.4 %collective-permute-start.3 = (f32[29,8,128]{2,1,0:T(8,128)S(1)}, f32[29,8,128]{2,1,0:T(8,128)S(1)}, u32[]{:S(2)}, u32[]{:S(2)}) collective-permute-start(f32[29,8,128]{2,1,0:T(8,128)S(1)} %get-tuple-element.76), channel_id=1, source_target_pairs={{0,2},{4,6},{8,10},{12,14},{16,18},{20,22},{24,26},{28,30},{32,34}... | collective-permute-start | bytes 356360 | tf_op jit(solution)/shard_map/ppermute | solution.py:664
  56.4 10.0 %collective-permute-start.4 = (f32[14,8,128]{2,1,0:T(8,128)S(1)}, f32[14,8,128]{2,1,0:T(8,128)S(1)}, u32[]{:S(2)}, u32[]{:S(2)}) collective-permute-start(f32[14,8,128]{2,1,0:T(8,128)S(1)} %get-tuple-element.81), channel_id=1, source_target_pairs={{2,4},{6,8},{10,12},{14,16},{18,20},{22,24},{26,28},{30,32},{34,36... | collective-permute-start | bytes 172040 | tf_op jit(solution)/shard_map/ppermute | solution.py:664
  57.1 9.3 %collective-permute-start.5 = (f32[14,8,128]{2,1,0:T(8,128)S(1)}, f32[14,8,128]{2,1,0:T(8,128)S(1)}, u32[]{:S(2)}, u32[]{:S(2)}) collective-permute-start(f32[14,8,128]{2,1,0:T(8,128)S(1)} %get-tuple-element.82), channel_id=1, source_target_pairs={{0,2},{4,6},{8,10},{12,14},{16,18},{20,22},{24,26},{28,30},{32,34}... | collective-permute-start | bytes 172040 | tf_op jit(solution)/shard_map/ppermute | solution.py:664
